TPU v7x, 32 devices: a whole 2x2x4 slice. The times are simulated.
32 devices in a mesh: gx: 16 (over z, y, x), gy: 2 (over core).
Axes of the slice: x: 2, y: 2, z: 4, core: 2. Of those that a mesh axis runs over, the one named last changes fastest.
Arguments:
- loads: bfloat16 [16, 2, 512, 128], P('gx', 'gy'), may hold values from -16 to 16
- schur: bfloat16 [16, 2, 512, 512], P('gx', 'gy'), may hold values from -0.5 to 3.5, as said below
- local_inverse: bfloat16 [16, 2, 512, 512], P('gx', 'gy'), may hold values from -0.5 to 3.5, as said below
- coarse_basis: float32 [16, 2, 4, 512], P('gx', 'gy'), may hold values from -0.75 to 0.75
- coarse_inverse: float32 [16, 2, 4, 128], P('gx', 'gy'), may hold values from -0.5 to 2, as said below
- face_map: int32 [16, 2, 512], P('gx', 'gy'), may hold values from 0 to 511, each once within a row
Outputs:
- solution: float32 [16, 2, 512, 128], P('gx', 'gy')
Inputs may be any that keep to these rules, and one draw needn't show every extreme that they name: `face_map`: each subdomain's row is a permutation of its 512 interface slots. `schur`: each subdomain's matrix is symmetric and positive definite. `local_inverse`: each subdomain's matrix is symmetric and positive definite. `coarse_inverse`: the whole 128 x 128 matrix is symmetric and positive definite.
All inputs are finite; a program needn't handle non-finite values.
Results may differ from a plain program's by a relative error of at most 0.0006.
The roundings to bfloat16 on the way count: a program that leaves them out, or rounds other values in their place, can miss the bound.
Values sent between devices are 32-bit elements; how exact they have to be, the bound alone decides.
No kernel may reach another device: no remote copies, remote signals or barrier semaphores. Data moves between devices by JAX's collectives and lax.ppermute only.
A program may use at most 64 MiB of HBM per device.

v0:
```python
import jax
import jax.numpy as jnp
from jax import lax
from jax.sharding import PartitionSpec as P

ITERS = 2


def extended(array, sides, width):
    for axis, dim in sides:
        peers, length = (lax.axis_size(axis), array.shape[dim])
        up = [(i, (i + 1) % peers) for i in range(peers - 1)]
        down = [(j, i) for i, j in up]
        last = lax.slice_in_dim(array, length - width, length, axis=dim)
        leading = lax.slice_in_dim(array, 0, width, axis=dim)
        before = lax.ppermute(last, axis, up)
        after = lax.ppermute(leading, axis, down)
        array = jnp.concatenate([before, array, after], axis=dim)
    return array


def face_weights(face_rows):
    index_x = lax.axis_index("gx")
    index_y = lax.axis_index("gy")
    neighbours = [
        index_x > 0,
        index_x < lax.axis_size("gx") - 1,
        index_y > 0,
        index_y < lax.axis_size("gy") - 1,
    ]
    pieces = [
        jnp.broadcast_to(jnp.where(shared, 0.5, 1.0).astype(jnp.float32), (face_rows, 1))
        for shared in neighbours
    ]
    return jnp.concatenate(pieces, axis=0)


def assemble(values):
    face_rows = values.shape[0] // 4
    width_cols = values.shape[1]
    along_x = values[0 : 2 * face_rows].reshape(2, face_rows, width_cols)
    along_y = values[2 * face_rows :].reshape(2, face_rows, width_cols)
    padded_x = extended(along_x, (("gx", 0),), 1)
    padded_y = extended(along_y, (("gy", 0),), 1)
    return jnp.concatenate(
        [
            along_x[0] + padded_x[0],
            along_x[1] + padded_x[3],
            along_y[0] + padded_y[0],
            along_y[1] + padded_y[3],
        ],
        axis=0,
    )


def permuted_product(matrix, halves, face_map, inverse_map):
    local_order = jnp.take(halves, face_map, axis=0)
    product = jnp.dot(matrix, local_order, preferred_element_type=jnp.float32)
    return jnp.take(product, inverse_map, axis=0)


def contract_rows(left_mat, right_mat):
    return lax.dot_general(
        left_mat,
        right_mat,
        (((0,), (0,)), ((), ())),
        precision=lax.Precision.HIGHEST,
        preferred_element_type=jnp.float32,
    )


def times_small(values, small_matrix):
    return jnp.dot(
        values, small_matrix, precision=lax.Precision.HIGHEST, preferred_element_type=jnp.float32
    )


def global_gram(left_mat, right_mat):
    return lax.psum(contract_rows(left_mat, right_mat), ("gx", "gy"))


def solve_gram(matrix, right_side):
    factor = jnp.linalg.cholesky(matrix)
    return jax.scipy.linalg.cho_solve((factor, True), right_side)


def coarse_solve(coarse_input, coarse_rows):
    return jnp.dot(
        coarse_rows,
        lax.all_gather(coarse_input, ("gx", "gy"), axis=0, tiled=True),
        precision=lax.Precision.HIGHEST,
        preferred_element_type=jnp.float32,
    )


def precondition(residual, weights, local_block, basis_block, coarse_rows, face_map, inverse_map):
    scaled = weights * residual
    local_part = permuted_product(local_block, scaled.astype(jnp.bfloat16), face_map, inverse_map)
    coarse_input = jnp.dot(
        basis_block, scaled, precision=lax.Precision.HIGHEST, preferred_element_type=jnp.float32
    )
    coarse_values = coarse_solve(coarse_input, coarse_rows)
    correction = local_part + contract_rows(basis_block, coarse_values)
    precond_gram = global_gram(scaled, correction)
    update = assemble(weights * correction)
    return (update, precond_gram)


def local(loads, schur, local_inverse, coarse_basis, coarse_inverse, face_map):
    schur_block = schur[0, 0]
    local_block = local_inverse[0, 0]
    basis_block = coarse_basis[0, 0]
    coarse_rows = coarse_inverse[0, 0]
    slot_map = face_map[0, 0]
    unknowns = slot_map.shape[0]
    inverse_map = (
        jnp.zeros((unknowns,), jnp.int32).at[slot_map].set(jnp.arange(unknowns, dtype=jnp.int32))
    )
    weights = face_weights(unknowns // 4)
    residual = assemble(loads[0, 0].astype(jnp.float32))
    solution = jnp.zeros_like(residual)
    update, precond_gram = precondition(
        residual, weights, local_block, basis_block, coarse_rows, slot_map, inverse_map
    )
    direction = update
    for iteration in range(ITERS):
        unassembled = permuted_product(
            schur_block, direction.astype(jnp.bfloat16), slot_map, inverse_map
        )
        curvature = global_gram(direction, unassembled)
        image_vec = assemble(unassembled)
        step_size = solve_gram(curvature, precond_gram)
        solution = solution + times_small(direction, step_size)
        if iteration + 1 < ITERS:
            residual = residual - times_small(image_vec, step_size)
            update, next_gram = precondition(
                residual, weights, local_block, basis_block, coarse_rows, slot_map, inverse_map
            )
            ratio_coef = solve_gram(precond_gram, next_gram)
            direction = update + times_small(direction, ratio_coef)
            precond_gram = next_gram
    return solution[None, None]


def solution(mesh):
    return jax.shard_map(
        local,
        mesh=mesh,
        in_specs=(
            P("gx", "gy", None, None),
            P("gx", "gy", None, None),
            P("gx", "gy", None, None),
            P("gx", "gy", None, None),
            P("gx", "gy", None, None),
            P("gx", "gy", None),
        ),
        out_specs=P("gx", "gy", None, None),
        check_vma=False,
    )
```

profile of v0, /device:TPU:0, one launch (start us, length us, event | category | flops | bytes accessed | tf_op | source)
XLA Modules:
  0.0 589.1 jit_solution(1564005855754439794)
XLA Ops:
  6.5 1.1 copy.43
  7.7 4.8 collective-permute-start
  12.5 1.3 collective-permute-start.1
  13.8 1.3 collective-permute-start.3
  15.1 3.0 collective-permute-start.2
  18.2 0.7 copy-done.7
  18.9 2.4 scatter_custom_fusion
  21.6 0.7 copy-done.6
  22.6 43.1 %all-gather = f32[32,4,128]{2,1,0:T(4,128)S(1)} all-gather(f32[1,4,128]{2,1,0:T(4,128)S(1)} %convolution_bitcast_fusion.7), channel_id=1, replica_groups=mesh['gx'=16,'gy'=2] {'gx','gy'}, dimensions={0}, use_global_device_ids=true | all-gather | bytes 67584 | tf_op jit(solution)/shard_map/all_gather | solution.py:90
  65.8 1.3 gather_fusion
  67.2 0.4 convolution_bitcast_fusion.5
  67.8 1.0 gather_fusion.1
  69.0 0.5 copy-done.8
  69.7 0.5 broadcast_multiply_fusion.1
  70.1 1.3 collective-permute-start.4
  71.4 2.1 collective-permute-done.4
  73.6 1.3 collective-permute-start.5
  74.9 1.3 collective-permute-start.7
  76.2 3.0 collective-permute-start.6
  79.2 1.0 fusion.17
  80.4 1.3 gather_fusion.2
  81.8 0.5 convolution_bitcast_fusion.3
  82.4 1.0 gather_fusion.3
  83.6 1.2 fusion.71
  84.9 5.2 collective-permute-start.8
  90.1 118.0 %all-reduce.9.cloned.1.call-done = (f32[128,128]{0,1:T(8,128)}, f32[128,128]{0,1:T(8,128)}) async-done(((f32[128,128]{0,1:T(8,128)}, f32[128,128]{0,1:T(8,128)}), (f32[128,128]{0,1:T(8,128)}, f32[128,128]{0,1:T(8,128)})) %all-reduce.9.cloned.1.call-update) | async-done | bytes 131088 | tf_op jit(solution)/shard_map/psum | solution.py:79
  208.1 1.0 copy.50
  209.2 0.7 copy-done.5
  209.9 11.7 %cholesky.70 = f32[128,128]{1,0:T(8,128)S(1)} custom-call(f32[128,128]{1,0:T(8,128)S(1)} %get-tuple-element.48), custom_call_target="Cholesky" | custom-call | tf_op jit(solution)/shard_map/jit(cholesky)/cholesky | solution.py:83
  221.7 11.7 %cholesky.59 = f32[128,128]{1,0:T(8,128)S(1)} custom-call(f32[128,128]{1,0:T(8,128)S(1)} %get-tuple-element.49), custom_call_target="Cholesky" | custom-call | tf_op jit(solution)/shard_map/jit(cholesky)/cholesky | solution.py:83
  233.4 0.6 compare_reduce_fusion.2
  234.1 0.7 fusion.32
  234.8 9.8 %custom-call.9 = f32[1,128,128]{1,2,0:T(8,128)S(1)} custom-call(f32[1,128,128]{2,1,0:T(8,128)S(1)} %fusion.32), custom_call_target="InvertDiagBlocksLowerTriangular" | custom-call | tf_op jit(solution)/shard_map/jit(_cho_solve)/triangular_solve | solution.py:84
  245.1 0.6 compare_reduce_fusion.1
  245.7 1.3 collective-permute-start.9
  247.0 1.3 collective-permute-start.11
  248.3 3.3 collective-permute-start.10
  251.6 0.7 fusion.33
  252.3 9.8 %custom-call.10 = f32[1,128,128]{1,2,0:T(8,128)S(1)} custom-call(f32[1,128,128]{2,1,0:T(8,128)S(1)} %fusion.33), custom_call_target="InvertDiagBlocksLowerTriangular" | custom-call | tf_op jit(solution)/shard_map/jit(_cho_solve)/triangular_solve | solution.py:84
  262.7 1.3 gather_fusion.4
  264.3 41.7 %all-gather.1 = f32[32,4,128]{2,1,0:T(4,128)S(1)} all-gather(f32[1,4,128]{2,1,0:T(4,128)S(1)} %convolution_bitcast_fusion.6), channel_id=1, replica_groups=mesh['gx'=16,'gy'=2] {'gx','gy'}, dimensions={0}, use_global_device_ids=true | all-gather | bytes 67584 | tf_op jit(solution)/shard_map/all_gather | solution.py:90
  306.2 0.5 convolution_bitcast_fusion.2
  306.8 1.0 gather_fusion.5
  308.0 0.4 broadcast_multiply_fusion
  308.4 1.0 fusion.75
  309.5 1.3 collective-permute-start.12
  310.8 112.4 %all-reduce.5.cloned.1.call-done = f32[128,128]{1,0:T(8,128)} async-done(((f32[128,128]{1,0:T(8,128)}), f32[128,128]{1,0:T(8,128)}) %all-reduce.5.cloned.1.call-update) | async-done | bytes 65552 | tf_op jit(solution)/shard_map/psum | solution.py:79
  423.2 1.1 fusion.42
  424.4 1.3 collective-permute-start.13
  425.7 1.3 collective-permute-start.15
  427.0 3.5 collective-permute-start.14
  430.7 0.6 collective-permute-done.14
  432.0 1.3 gather_fusion.6
  433.3 0.4 convolution_bitcast_fusion
  433.9 1.0 gather_fusion.7
  434.9 1.3 fusion.15
  436.3 119.9 %all-reduce.7.cloned.1.call-done = f32[128,128]{0,1:T(8,128)} async-done(((f32[128,128]{0,1:T(8,128)}), f32[128,128]{0,1:T(8,128)}) %all-reduce.7.cloned.1.call-update) | async-done | bytes 65552 | tf_op jit(solution)/shard_map/psum | solution.py:79
  556.2 1.0 copy.61
  557.3 11.7 %cholesky.81 = f32[128,128]{1,0:T(8,128)S(1)} custom-call(f32[128,128]{1,0:T(8,128)S(1)} %fusion.39), custom_call_target="Cholesky" | custom-call | tf_op jit(solution)/shard_map/jit(cholesky)/cholesky | solution.py:83
  569.0 0.6 compare_reduce_fusion
  569.6 0.7 fusion.34
  570.3 9.8 %custom-call.11 = f32[1,128,128]{1,2,0:T(8,128)S(1)} custom-call(f32[1,128,128]{2,1,0:T(8,128)S(1)} %fusion.34), custom_call_target="InvertDiagBlocksLowerTriangular" | custom-call | tf_op jit(solution)/shard_map/jit(_cho_solve)/triangular_solve | solution.py:84
  580.7 0.6 fusion.76
  581.3 1.3 fusion.1
  (93 shorter events, 5.0 us)
Async XLA Ops:
  6.5 60.6 %copy-start = (bf16[1,1,512,512]{3,2,1,0:T(8,128)(2,1)S(1)}, bf16[1,1,512,512]{3,2,1,0:T(8,128)(2,1)}, u32[]{:S(2)}) copy-start(bf16[1,1,512,512]{3,2,1,0:T(8,128)(2,1)} %param.15) | copy-start | bytes 1572868
  6.5 201.6 %all-reduce.9.cloned.1.call-start = ((), (), s32[]{:S(2)}) async-start(), calls=%async_computation.2 | async-start | bytes 262144 | tf_op jit(solution)/shard_map/psum | solution.py:79
  7.7 13.9 %collective-permute-start = (f32[1,128,128]{1,2,0:T(8,128)S(1)}, f32[1,128,128]{1,2,0:T(8,128)S(1)}, u32[]{:S(2)}, u32[]{:S(2)}) collective-permute-start(f32[1,128,128]{1,2,0:T(8,128)S(1)} %get-tuple-element.36), channel_id=1, source_target_pairs={{0,2},{2,4},{4,6},{6,8},{8,10},{10,12},{12,14},{14,16},{16,18},{18... | collective-permute-start | bytes 196616 | tf_op jit(solution)/shard_map/ppermute | solution.py:16
  12.5 9.0 %collective-permute-start.1 = (f32[1,128,128]{1,2,0:T(8,128)S(1)}, f32[1,128,128]{1,2,0:T(8,128)S(1)}, u32[]{:S(2)}, u32[]{:S(2)}) collective-permute-start(f32[1,128,128]{1,2,0:T(8,128)S(1)} %get-tuple-element.37), channel_id=1, source_target_pairs={{2,0},{4,2},{6,4},{8,6},{10,8},{12,10},{14,12},{16,14},{18,16},{20... | collective-permute-start | bytes 196616 | tf_op jit(solution)/shard_map/ppermute | solution.py:17
  13.8 7.7 %collective-permute-start.3 = (f32[1,128,128]{1,2,0:T(8,128)S(1)}, f32[1,128,128]{1,2,0:T(8,128)S(1)}, u32[]{:S(2)}, u32[]{:S(2)}) collective-permute-start(f32[1,128,128]{1,2,0:T(8,128)S(1)} %get-tuple-element.38), channel_id=1, source_target_pairs={{1,0},{3,2},{5,4},{7,6},{9,8},{11,10},{13,12},{15,14},{17,16},{19,... | collective-permute-start | bytes 196616 | tf_op jit(solution)/shard_map/ppermute | solution.py:17
  15.1 6.4 %collective-permute-start.2 = (f32[1,128,128]{1,2,0:T(8,128)S(1)}, f32[1,128,128]{1,2,0:T(8,128)S(1)}, u32[]{:S(2)}, u32[]{:S(2)}) collective-permute-start(f32[1,128,128]{1,2,0:T(8,128)S(1)} %get-tuple-element.39), channel_id=1, source_target_pairs={{0,1},{2,3},{4,5},{6,7},{8,9},{10,11},{12,13},{14,15},{16,17},{18,... | collective-permute-start | bytes 196616 | tf_op jit(solution)/shard_map/ppermute | solution.py:16
  18.2 0.7 copy-start.7
  21.6 0.7 copy-start.6
  68.8 0.7 copy-start.8
  70.1 3.4 collective-permute-start.4
  73.6 6.7 %collective-permute-start.5 = (f32[1,128,128]{1,2,0:T(8,128)S(1)}, f32[1,128,128]{1,2,0:T(8,128)S(1)}, u32[]{:S(2)}, u32[]{:S(2)}) collective-permute-start(f32[1,128,128]{1,2,0:T(8,128)S(1)} %get-tuple-element.26), channel_id=1, source_target_pairs={{2,0},{4,2},{6,4},{8,6},{10,8},{12,10},{14,12},{16,14},{18,16},{20... | collective-permute-start | bytes 196616 | tf_op jit(solution)/shard_map/ppermute | solution.py:17
  74.9 5.4 collective-permute-start.7
  76.2 4.1 collective-permute-start.6
  80.4 1.4 copy-start.1
  84.8 338.4 %all-reduce.5.cloned.1.call-start = ((), (), s32[]{:S(2)}) async-start(), calls=%async_computation | async-start | bytes 131072 | tf_op jit(solution)/shard_map/psum | solution.py:79
  84.9 160.9 %collective-permute-start.8 = (f32[1,128,128]{2,1,0:T(8,128)S(1)}, f32[1,128,128]{2,1,0:T(8,128)S(1)}, u32[]{:S(2)}, u32[]{:S(2)}) collective-permute-start(f32[1,128,128]{2,1,0:T(8,128)S(1)} %slice_bitcast_fusion.6), channel_id=1, source_target_pairs={{0,2},{2,4},{4,6},{6,8},{8,10},{10,12},{12,14},{14,16},{16,18},{18... | collective-permute-start | bytes 196616 | tf_op jit(solution)/shard_map/ppermute | solution.py:16
  208.1 1.0 copy-start.2
  209.1 0.8 copy-start.5
  245.7 16.3 %collective-permute-start.9 = (f32[1,128,128]{2,1,0:T(8,128)S(1)}, f32[1,128,128]{2,1,0:T(8,128)S(1)}, u32[]{:S(2)}, u32[]{:S(2)}) collective-permute-start(f32[1,128,128]{2,1,0:T(8,128)S(1)} %get-tuple-element.19), channel_id=1, source_target_pairs={{2,0},{4,2},{6,4},{8,6},{10,8},{12,10},{14,12},{16,14},{18,16},{20... | collective-permute-start | bytes 196616 | tf_op jit(solution)/shard_map/ppermute | solution.py:17
  247.0 15.1 %collective-permute-start.11 = (f32[1,128,128]{2,1,0:T(8,128)S(1)}, f32[1,128,128]{2,1,0:T(8,128)S(1)}, u32[]{:S(2)}, u32[]{:S(2)}) collective-permute-start(f32[1,128,128]{2,1,0:T(8,128)S(1)} %get-tuple-element.20), channel_id=1, source_target_pairs={{1,0},{3,2},{5,4},{7,6},{9,8},{11,10},{13,12},{15,14},{17,16},{19,... | collective-permute-start | bytes 196616 | tf_op jit(solution)/shard_map/ppermute | solution.py:17
  248.3 13.8 %collective-permute-start.10 = (f32[1,128,128]{2,1,0:T(8,128)S(1)}, f32[1,128,128]{2,1,0:T(8,128)S(1)}, u32[]{:S(2)}, u32[]{:S(2)}) collective-permute-start(f32[1,128,128]{2,1,0:T(8,128)S(1)} %get-tuple-element.21), channel_id=1, source_target_pairs={{0,1},{2,3},{4,5},{6,7},{8,9},{10,11},{12,13},{14,15},{16,17},{18,... | collective-permute-start | bytes 196616 | tf_op jit(solution)/shard_map/ppermute | solution.py:16
  309.5 246.8 %all-reduce.7.cloned.1.call-start = ((), (), s32[]{:S(2)}) async-start(), calls=%async_computation.1 | async-start | bytes 131072 | tf_op jit(solution)/shard_map/psum | solution.py:79
  309.5 114.8 %collective-permute-start.12 = (f32[1,128,128]{1,2,0:T(8,128)S(1)}, f32[1,128,128]{1,2,0:T(8,128)S(1)}, u32[]{:S(2)}, u32[]{:S(2)}) collective-permute-start(f32[1,128,128]{1,2,0:T(8,128)S(1)} %slice_bitcast_fusion.2), channel_id=1, source_target_pairs={{0,2},{2,4},{4,6},{6,8},{8,10},{10,12},{12,14},{14,16},{16,18},{18... | collective-permute-start | bytes 196616 | tf_op jit(solution)/shard_map/ppermute | solution.py:16
  424.4 6.3 %collective-permute-start.13 = (f32[1,128,128]{1,2,0:T(8,128)S(1)}, f32[1,128,128]{1,2,0:T(8,128)S(1)}, u32[]{:S(2)}, u32[]{:S(2)}) collective-permute-start(f32[1,128,128]{1,2,0:T(8,128)S(1)} %get-tuple-element.12), channel_id=1, source_target_pairs={{2,0},{4,2},{6,4},{8,6},{10,8},{12,10},{14,12},{16,14},{18,16},{20... | collective-permute-start | bytes 196616 | tf_op jit(solution)/shard_map/ppermute | solution.py:17
  425.7 5.0 collective-permute-start.15
  427.0 4.4 collective-permute-start.14
  556.2 1.0 copy-start.4
  569.6 10.5 %copy-start.3 = (f32[128,128]{1,0:T(8,128)S(1)}, f32[128,128]{1,0:T(8,128)}, u32[]{:S(2)}) copy-start(f32[128,128]{1,0:T(8,128)} %all-reduce.5.cloned.1.call-done) | copy-start | bytes 196612
Sparse Core Ops, SparseCore 0:
  84.9 123.1 all-reduce.8
  309.6 113.6 all-reduce.4
  436.4 119.7 all-reduce.6
where the time goes:
time: 591 us; the launch traced here: 589 us
  waiting for transfers between devices  353 us (60%)
  blocking collectives  84.9 us (14%)
  other arithmetic  69 us (12%)
  starting transfers between devices  35.9 us (6%)
  local copies, waits for them, and re-layouts  19 us (3%)
  between operations  14 us (2%)
  matrix products  13.1 us (2%)
    psum x3, waiting for transfers between devices, global_gram(): return lax.psum(contract_rows(left_mat, right_mat), ('gx', 'gy'))  350 us
    all_gather x2, blocking collectives, coarse_solve(): lax.all_gather(coarse_input, ('gx', 'gy'), axis=0, tiled=True)  84.9 us
    another operation x9, other arithmetic, solve_gram(): factor = jnp.linalg.cholesky(matrix)  37.2 us
    another operation x6, other arithmetic, solve_gram(): return jax.scipy.linalg.cho_solve((factor, True), right_side)  31.4 us
    ppermute x8, starting transfers between devices, extended(): before = lax.ppermute(last, axis, up)  25.5 us
  transfers between devices with their start and end apart: 19, of which 5 were waited for; matrix products, arithmetic and copies ran while one was open for 9% of the time, Pallas kernels for 0%

commit v1 on v0

v1 whole, which is shorter than its diff:
```python
import functools

import jax
import jax.numpy as jnp
from jax import lax
from jax.experimental import pallas as pl
from jax.experimental.pallas import tpu as pltpu
from jax.sharding import PartitionSpec as P

AXES = ("gx", "gy")
F32 = jnp.float32
BF16 = jnp.bfloat16
EXACT = lax.Precision.HIGHEST


def dot(left, right, left_dim=1, right_dim=0, precision=EXACT):
    return lax.dot_general(
        left,
        right,
        (((left_dim,), (right_dim,)), ((), ())),
        precision=precision,
        preferred_element_type=F32,
    )


def half_dot(left, right):
    return lax.dot_general(
        left, right, (((1,), (0,)), ((), ())), preferred_element_type=F32
    )


def call(body, outs, scratch=(), flops=0, moved=0):
    return pl.pallas_call(
        body,
        scratch_shapes=[pltpu.VMEM(shape, kind) for shape, kind in scratch],
        out_shape=[jax.ShapeDtypeStruct(shape, kind) for shape, kind in outs],
        compiler_params=pltpu.CompilerParams(vmem_limit_bytes=48 * 1024 * 1024),
        cost_estimate=pl.CostEstimate(flops=flops, bytes_accessed=moved, transcendentals=0),
    )


def pair_rounds(size):
    first = [(i, i + 1) for i in range(0, size - 1, 2)]
    second = [(i, i + 1) for i in range(1, size - 1, 2)]
    return [pairs + [(j, i) for i, j in pairs] for pairs in (first, second)]


def exchange(sends):
    got = []
    for axis, pieces in zip(AXES, (sends[0:2], sends[2:4])):
        for pairs, piece in zip(pair_rounds(lax.axis_size(axis)), pieces):
            got.append(lax.ppermute(piece, axis, pairs) if pairs else None)
    return got


def rounds_used():
    return [bool(p) for axis in AXES for p in pair_rounds(lax.axis_size(axis))]


def even(axis):
    return lax.rem(lax.axis_index(axis), 2) == 0


def to_rounds(faces):
    ex, ey = even("gx"), even("gy")
    return [
        jnp.where(ex, faces[1], faces[0]),
        jnp.where(ex, faces[0], faces[1]),
        jnp.where(ey, faces[3], faces[2]),
        jnp.where(ey, faces[2], faces[3]),
    ]


def to_faces(parts):
    ex, ey = even("gx"), even("gy")
    a, b, c, d = parts

    def choose(flag, yes, no):
        if yes is None and no is None:
            return None
        if yes is None:
            return jnp.where(flag, jnp.zeros_like(no), no)
        if no is None:
            return jnp.where(flag, yes, jnp.zeros_like(yes))
        return jnp.where(flag, yes, no)

    return [choose(ex, b, a), choose(ex, a, b), choose(ey, d, c), choose(ey, c, d)]


def face_weights():
    ix, iy = lax.axis_index("gx"), lax.axis_index("gy")
    shared = [
        ix > 0,
        ix < lax.axis_size("gx") - 1,
        iy > 0,
        iy < lax.axis_size("gy") - 1,
    ]
    return [jnp.where(flag, 0.5, 1.0).astype(F32) for flag in shared]


def split_faces(field):
    rows = field.shape[0] // 4
    return [field[rows * f : rows * (f + 1)] for f in range(4)]


def add_faces(field, got):
    faces = [
        mine if other is None else mine + other for mine, other in zip(split_faces(field), got)
    ]
    return jnp.concatenate(faces, axis=0)


def weighted(field, weights):
    return jnp.concatenate([w * v for w, v in zip(weights, split_faces(field))], axis=0)


def write_blocks(out_ref, rows):
    out_ref[...] = jnp.zeros(out_ref.shape, F32)
    per = out_ref.shape[1]
    used = rows.shape[0] // per
    out_ref[0:used] = rows.reshape(used, per, rows.shape[1])


def unit_inverse(matrix, work_ref):
    size = matrix.shape[0]
    row_id = lax.broadcasted_iota(jnp.int32, (size, size), 0)
    col_id = lax.broadcasted_iota(jnp.int32, (size, size), 1)
    eye = (row_id == col_id).astype(F32)
    only = matrix * eye
    by_row = lax.rsqrt(jnp.sum(only, axis=1, keepdims=True))
    by_col = lax.rsqrt(jnp.sum(only, axis=0, keepdims=True))
    unit = matrix * by_row * by_col
    bound = jnp.max(jnp.sum(jnp.abs(unit), axis=0, keepdims=True), axis=1, keepdims=True)
    scale = 2.0 / (1.0 + bound)
    power = eye - scale * unit
    total = eye + power
    power = dot(power, power)

    def step(total, power):
        both = dot(jnp.concatenate([total, power], axis=0), power)
        return total + both[:size], both[size:]

    for _ in range(3):
        total, power = step(total, power)
    work_ref[0:size] = total
    work_ref[size:] = power

    def again(carry):
        total, power = step(work_ref[0:size], work_ref[size:])
        work_ref[0:size] = total
        work_ref[size:] = power
        return carry[0] + 1, jnp.max(jnp.abs(power))

    lax.while_loop(
        lambda carry: jnp.logical_and(carry[0] < 40, carry[1] > 1e-7),
        again,
        (jnp.int32(0), jnp.max(jnp.abs(power))),
    )
    return work_ref[0:size] * (by_row * scale) * by_col


def local(loads, schur, local_inverse, coarse_basis, coarse_inverse, face_map):
    loads, schur, local_inverse = loads[0, 0], schur[0, 0], local_inverse[0, 0]
    basis, coarse_rows, slot_map = coarse_basis[0, 0], coarse_inverse[0, 0], face_map[0, 0]
    unknowns, cols = loads.shape
    face = unknowns // 4
    nco, coarse_all = coarse_rows.shape
    devices = lax.axis_size("gx") * lax.axis_size("gy")
    chunks = coarse_all // cols
    used = rounds_used()
    field = (unknowns, cols)
    gram_shape = (cols, cols)
    work = [((2 * cols, cols), F32)]
    face_out = ((face, cols), F32)

    def give(refs, faces):
        for ref, value, flag in zip(refs, to_rounds(faces), used):
            if flag:
                ref[...] = value

    def take(refs):
        return to_faces([ref[...] if flag else None for ref, flag in zip(refs, used)])

    def trade(sends):
        return [got for got in exchange(sends) if got is not None]

    def spread(refs):
        left = list(refs)
        return [left.pop(0) if flag else None for flag in used]

    nrounds = sum(used)

    def fill(values):
        left = list(values)
        return [left.pop(0) if flag else None for flag in used]

    head = face + nco + nco * chunks

    def send_loads(loads_ref, basis_ref, rows_ref, *outs):
        outs = spread(outs)
        basis_now = basis_ref[...]
        rows_now = rows_ref[...]
        packs = []
        for f, part in enumerate(split_faces(loads_ref[...].astype(F32))):
            packs.append(
                jnp.concatenate(
                    [part, basis_now[:, face * f : face * (f + 1)]]
                    + [rows_now[:, cols * c : cols * (c + 1)] for c in range(chunks)],
                    axis=0,
                )
            )
        give(outs, packs)

    sends = call(send_loads, [((head, cols), F32)] * nrounds)(loads, basis, coarse_rows)
    got_a = trade(fill(sends))

    def reorder(map_ref, first_ref, second_ref, first_out, second_out):
        slots = lax.broadcasted_iota(jnp.int32, (unknowns, unknowns), 0)
        pick = (slots == map_ref[...]).astype(F32).astype(BF16)
        for ref, out in ((first_ref, first_out), (second_ref, second_out)):
            rows = half_dot(pick, ref[...]).astype(BF16)
            out[...] = lax.dot_general(
                rows, pick, (((1,), (1,)), ((), ())), preferred_element_type=F32
            ).astype(BF16)

    inverse_here, schur_here = call(
        reorder, [((unknowns, unknowns), BF16)] * 2, flops=8 * unknowns**3, moved=8 * unknowns**2
    )(slot_map.reshape(1, unknowns), local_inverse, schur)

    def first_local(*refs):
        got = take(spread(refs[:nrounds]))
        loads_ref, inverse_ref, basis_ref, rows_ref = refs[nrounds : nrounds + 4]
        res_ref, part_ref, gram_ref, ci_ref, bases_ref, table_ref = refs[nrounds + 4 : nrounds + 10]
        sends = spread(refs[nrounds + 10 :])
        weights = face_weights()
        residual = add_faces(loads_ref[...].astype(F32), [g if g is None else g[:face] for g in got])
        scaled = weighted(residual, weights)
        product = half_dot(inverse_ref[...], scaled.astype(BF16))
        part = weighted(product, weights)
        give(sends, split_faces(part))
        res_ref[...] = residual
        part_ref[...] = part
        gram_ref[...] = dot(scaled, product, 0, 0)
        coarse_input = dot(basis_ref[...], scaled)
        ci_ref[...] = jnp.broadcast_to(coarse_input[None], ci_ref.shape)
        basis_now = basis_ref[...]
        bases, tables = [], []
        for f in range(4):
            mine = weights[f] * basis_now[:, face * f : face * (f + 1)]
            other = got[f]
            if other is None:
                bases += [mine, jnp.zeros_like(mine)]
                tables += [rows_ref[...], jnp.zeros((nco, coarse_all), F32)]
            else:
                bases += [mine, 0.5 * other[face : face + nco]]
                tables += [
                    rows_ref[...],
                    jnp.concatenate(
                        [
                            other[face + nco * (c + 1) : face + nco * (c + 2)]
                            for c in range(chunks)
                        ],
                        axis=1,
                    ),
                ]
        bases_ref[...] = jnp.concatenate(bases, axis=0)
        table_ref[...] = jnp.concatenate(tables, axis=0)

    outs = call(
        first_local,
        [
            (field, F32),
            (field, F32),
            (gram_shape, F32),
            ((devices, nco, cols), F32),
            ((8 * nco, face), F32),
            ((8 * nco, coarse_all), F32),
        ]
        + [face_out] * nrounds,
    )(*got_a, loads, inverse_here, basis, coarse_rows)
    residual, part, gram_part, coarse_input, bases, table = outs[:6]
    got_b = trade(fill(outs[6:]))
    coarse_all_in = lax.all_to_all(coarse_input, AXES, 0, 0).reshape(coarse_all, cols)

    def coarse_part(bases_now, values):
        return [
            dot(bases_now[2 * nco * f : 2 * nco * (f + 1)], values[2 * nco * f : 2 * nco * (f + 1)], 0, 0)
            for f in range(4)
        ]

    per = 8 * -(-2 * cols // (8 * devices))

    def first_direction(*refs):
        got = take(spread(refs[:nrounds]))
        part_ref, gram_ref, all_ref, bases_ref, table_ref, schur_ref, mine_ref = refs[
            nrounds : nrounds + 7
        ]
        dir_ref, image_ref, values_ref, blocks_ref = refs[nrounds + 7 : nrounds + 11]
        sends = spread(refs[nrounds + 11 :])
        values = dot(table_ref[...], all_ref[...])
        values_ref[...] = values
        coarse = coarse_part(bases_ref[...], values)
        update = add_faces(part_ref[...], got) + jnp.concatenate(coarse, axis=0)
        dir_ref[...] = update
        image = half_dot(schur_ref[...], update.astype(BF16))
        image_ref[...] = image
        give(sends, split_faces(image))
        first = gram_ref[...] + dot(mine_ref[0], values[:nco], 0, 0)
        curvature = dot(update, image, 0, 0)
        write_blocks(blocks_ref, jnp.concatenate([curvature, first], axis=0))

    outs = call(
        first_direction,
        [
            (field, F32),
            (field, F32),
            ((8 * nco, cols), F32),
            ((devices, per, cols), F32),
        ]
        + [face_out] * nrounds,
    )(*got_b, part, gram_part, coarse_all_in, bases, table, schur_here, coarse_input)
    direction, image, values, blocks = outs[:4]
    got_d = trade(fill(outs[4:]))
    blocks = lax.all_to_all(blocks, AXES, 0, 0)

    def first_sums(*refs):
        got = take(spread(refs[:nrounds]))
        image_ref, blocks_ref, basis_ref = refs[nrounds : nrounds + 3]
        full_ref, sum_ref, mine_ref = refs[nrounds + 3 :]
        image_vec = add_faces(image_ref[...], got)
        full_ref[...] = image_vec
        coarse_image = dot(basis_ref[...], weighted(image_vec, face_weights()))
        mine_ref[...] = coarse_image
        block = jnp.concatenate(
            [jnp.sum(blocks_ref[...], axis=0), coarse_image, jnp.zeros((8 - nco, cols), F32)], axis=0
        )
        sum_ref[...] = jnp.broadcast_to(block[None], sum_ref.shape)

    image_vec, sums, coarse_image = call(
        first_sums,
        [(field, F32), ((devices, per + 8, cols), F32), ((nco, cols), F32)],
    )(*got_d, image, blocks, basis)
    sums = lax.all_to_all(sums, AXES, 0, 0)

    def second_local(
        sums_ref, res_ref, full_ref, inverse_ref, table_ref, values_ref, mine_ref, image_ref, *outs
    ):
        outs, work_ref = outs[:-1], outs[-1]
        curv_ref, first_ref, step_ref, next_ref, values_out, part_ref = outs[:6]
        sends = spread(outs[6:])
        both = sums_ref[:, 0:per, :].reshape(devices * per, cols)
        curvature, first = both[:cols], both[cols : 2 * cols]
        step = dot(unit_inverse(curvature, work_ref), first)
        weights = face_weights()
        residual = res_ref[...] - dot(full_ref[...], step)
        scaled = weighted(residual, weights)
        product = half_dot(inverse_ref[...], scaled.astype(BF16))
        part = weighted(product, weights)
        part_ref[...] = part
        give(sends, split_faces(part))
        curv_ref[...] = curvature
        first_ref[...] = first
        step_ref[...] = step
        wide = cols // nco * 8
        src = lax.broadcasted_iota(jnp.int32, (cols, wide), 0)
        dst = lax.broadcasted_iota(jnp.int32, (cols, wide), 1)
        widen = (dst == src // nco * 8 + lax.rem(src, nco)).astype(F32)
        rows = sums_ref[:, per : per + 8, :].reshape(devices * 8, cols)
        got = values_ref[...] * 0.0
        for c in range(chunks):
            table_c = dot(table_ref[:, cols * c : cols * (c + 1)], widen)
            got = got + dot(table_c, rows[wide * c : wide * (c + 1)])
        values_now = values_ref[...] - dot(got, step)
        values_out[...] = values_now
        own = mine_ref[0] - dot(image_ref[...], step)
        next_ref[...] = dot(scaled, product, 0, 0) + dot(own, values_now[:nco], 0, 0)

    outs = call(
        second_local,
        [
            (gram_shape, F32),
            (gram_shape, F32),
            (gram_shape, F32),
            (gram_shape, F32),
            ((8 * nco, cols), F32),
            (field, F32),
        ]
        + [face_out] * nrounds,
        work,
    )(sums, residual, image_vec, inverse_here, table, values, coarse_input, coarse_image)
    curvature, first, step, next_part, values, part = outs[:6]
    got_e = trade(fill(outs[6:]))

    def invert(first_ref, out_ref, work_ref):
        out_ref[...] = unit_inverse(first_ref[...], work_ref)

    (first_inverse,) = call(invert, [(gram_shape, F32)], work, flops=2 * 60 * cols**3)(first)

    per2 = 8 * -(-3 * cols // (8 * devices))
    per2 = per2 if (3 * cols) % per2 == 0 else 8 * -(-4 * cols // (8 * devices))

    def second_direction(*refs):
        got = take(spread(refs[:nrounds]))
        part_ref, next_ref, values_ref, bases_ref, schur_ref, image_ref = refs[nrounds : nrounds + 6]
        update_ref, blocks_ref = refs[nrounds + 6 :]
        coarse = coarse_part(bases_ref[...], values_ref[...])
        update = add_faces(part_ref[...], got) + jnp.concatenate(coarse, axis=0)
        update_ref[...] = update
        product = half_dot(schur_ref[...], update.astype(BF16))
        square = dot(update, product, 0, 0)
        cross = dot(image_ref[...], update, 0, 0)
        rows = [next_ref[...], square, cross]
        if (3 * cols) % per2:
            rows.append(jnp.zeros(gram_shape, F32))
        write_blocks(blocks_ref, jnp.concatenate(rows, axis=0))

    update, blocks = call(
        second_direction, [(field, F32), ((devices, per2, cols), F32)]
    )(*got_e, part, next_part, values, bases, schur_here, image)
    blocks = lax.all_to_all(blocks, AXES, 0, 0)

    def second_sums(blocks_ref, out_ref):
        out_ref[...] = jnp.broadcast_to(jnp.sum(blocks_ref[...], axis=0)[None], out_ref.shape)

    (sums,) = call(second_sums, [((devices, per2, cols), F32)])(blocks)
    sums = lax.all_to_all(sums, AXES, 0, 0).reshape(devices * per2, cols)

    def finish(sums_ref, first_ref, curv_ref, step_ref, dir_ref, update_ref, out_ref, work_ref):
        rows = sums_ref[...]
        next_gram, square, cross = (rows[cols * k : cols * (k + 1)] for k in range(3))
        ratio = dot(first_ref[...], next_gram)
        mixed = dot(cross, ratio, 0, 0)
        curvature = square + mixed + mixed.T + dot(ratio, dot(curv_ref[...], ratio), 0, 0)
        step = dot(unit_inverse(curvature, work_ref), next_gram)
        total = step_ref[...] + dot(ratio, step)
        out_ref[...] = dot(dir_ref[...], total) + dot(update_ref[...], step)

    (solved,) = call(finish, [(field, F32)], work)(
        sums, first_inverse, curvature, step, direction, update
    )
    return solved[None, None]


def solution(mesh):
    return jax.shard_map(
        local,
        mesh=mesh,
        in_specs=(
            P("gx", "gy", None, None),
            P("gx", "gy", None, None),
            P("gx", "gy", None, None),
            P("gx", "gy", None, None),
            P("gx", "gy", None, None),
            P("gx", "gy", None),
        ),
        out_specs=P("gx", "gy", None, None),
        check_vma=False,
    )
```

time: 591 us -> 109 us (0.18)
  waiting for transfers between devices: 353 us -> 22.2 us
  other arithmetic: 69 us -> 0 us
  blocking collectives: 84.9 us -> 32.6 us
  Pallas kernels: 0 us -> 21.4 us
  local copies, waits for them, and re-layouts: 19 us -> 5.05 us
  between operations: 14 us -> 0.18 us
  matrix products: 13.1 us -> 0 us
  starting transfers between devices: 35.9 us -> 26.6 us
    psum x3 -> x0, waiting for transfers between devices: 350 us -> none  [global_gram(): return lax.psum(contract_rows(left_mat, right_mat), ('gx', 'gy'))]
    all_gather x2 -> x0, blocking collectives: 84.9 us -> none  [coarse_solve(): lax.all_gather(coarse_input, ('gx', 'gy'), axis=0, tiled=True)]
    another operation x15 -> x0, other arithmetic: 68.6 us -> none  [the longest x9 37.2 us: solve_gram(): factor = jnp.linalg.cholesky(matrix)]
    all_to_all x0 -> x2, blocking collectives: none -> 32.6 us  [the longest x1 16.9 us: local(): blocks = lax.all_to_all(blocks, AXES, 0, 0)]
    ppermute x16 -> x12, starting transfers between devices: 35.8 us -> 10.2 us  [exchange(): got.append(lax.ppermute(piece, axis, pairs) if pairs else None)]
    pallas_call x0 -> x10, Pallas kernels: none -> 21.4 us  [the longest x1 6.53 us: local(): call(finish, [(field, F32)], work)]
    all_to_all x0 -> x3, starting transfers between devices: none -> 16.4 us  [the longest x1 7.72 us: local(): lax.all_to_all(coarse_input, AXES, 0, 0).reshape(coarse_all, cols)]
    all_to_all x0 -> x3, waiting for transfers between devices: none -> 14.7 us  [the longest x1 8.72 us: local(): sums = lax.all_to_all(sums, AXES, 0, 0).reshape(devices * per2, cols)]
  transfers between devices with their start and end apart: 19 -> 15, of which waited for: 5 -> 6; matrix products, arithmetic and copies ran while one was open for 9% -> 0% of each run, Pallas kernels for 0% -> 3%
where the time goes in v1:
time: 109 us; the launch traced here: 108 us
  blocking collectives  32.6 us (30%)
  starting transfers between devices  26.6 us (24%)
  waiting for transfers between devices  22.2 us (20%)
  Pallas kernels  21.4 us (20%)
  local copies, waits for them, and re-layouts  5.05 us (5%)
    all_to_all x1, blocking collectives, local(): blocks = lax.all_to_all(blocks, AXES, 0, 0)  16.9 us
    all_to_all x1, blocking collectives, local(): sums = lax.all_to_all(sums, AXES, 0, 0)  15.7 us
    ppermute x12, starting transfers between devices, exchange(): got.append(lax.ppermute(piece, axis, pairs) if pairs else None)  10.2 us
    all_to_all x1, waiting for transfers between devices, local(): sums = lax.all_to_all(sums, AXES, 0, 0).reshape(devices * per2, cols)  8.72 us
    all_to_all x1, starting transfers between devices, local(): lax.all_to_all(coarse_input, AXES, 0, 0).reshape(coarse_all, cols)  7.72 us
    ppermute x12, waiting for transfers between devices, exchange(): got.append(lax.ppermute(piece, axis, pairs) if pairs else None)  7.54 us
    pallas_call x1, Pallas kernels, local(): call(finish, [(field, F32)], work)  6.53 us
    all_to_all x1, starting transfers between devices, local(): blocks = lax.all_to_all(blocks, AXES, 0, 0)  6.1 us
  transfers between devices with their start and end apart: 15, of which 6 were waited for; matrix products, arithmetic and copies ran while one was open for 0% of the time, Pallas kernels for 3%

profile of v1, /device:TPU:0, one launch (start us, length us, event | category | flops | bytes accessed | tf_op | source)
XLA Modules:
  0.0 108.0 jit_solution(2790780906169345873)
XLA Ops:
  0.0 0.0 copy-start.4
  0.0 0.7 copy-done.4
  0.7 0.0 copy-start
  0.7 0.9 copy-done
  1.6 0.0 copy-start.2
  1.6 0.7 copy-done.2
  2.3 3.0 %collective-permute-start = (f32[136,128]{1,0:T(8,128)S(1)}, f32[136,128]{1,0:T(8,128)S(1)}, u32[]{:S(2)}, u32[]{:S(2)}) collective-permute-start(f32[136,128]{1,0:T(8,128)S(1)} %get-tuple-element.40), channel_id=1, source_target_pairs={{0,2},{4,6},{8,10},{12,14},{16,18},{20,22},{24,26},{28,30},{2,0},{... | collective-permute-start | bytes 208904 | tf_op jit(solution)/shard_map/ppermute | solution.py:52
  5.3 0.7 collective-permute-start.1
  6.0 0.1 collective-permute-start.2
  6.1 0.0 copy-start.7
  6.1 0.7 copy-done.7
  6.7 0.0 copy-start.5
  6.7 1.0 copy-done.5
  7.8 0.0 copy-start.6
  7.8 1.0 copy-done.6
  8.8 0.0 copy-start.1
  8.8 0.0 copy-start.3
  8.8 1.3 %shard_map.65 = (bf16[512,512]{1,0:T(8,128)(2,1)S(1)}, bf16[512,512]{1,0:T(8,128)(2,1)S(1)}) custom-call(s32[1,512]{1,0:T(1,128)S(1)} %bitcast.20, bf16[512,512]{1,0:T(8,128)(2,1)S(1)} %bitcast.18, bf16[512,512]{1,0:T(8,128)(2,1)S(1)} %bitcast.19), custom_call_target="tpu_custom_call" | custom-call | flops 1073741824 | bytes 2097152 | tf_op jit(solution)/shard_map/pallas_call | solution.py:226
  10.1 0.0 collective-permute-done.refs_0_
  10.1 0.0 collective-permute-done.1.refs_1_
  10.1 0.0 collective-permute-done.2.refs_2_
  10.1 0.0 copy-done.1
  10.1 0.0 copy-done.3
  10.1 1.6 %shard_map.66 = (f32[512,128]{1,0:T(8,128)S(1)}, f32[512,128]{1,0:T(8,128)S(1)}, f32[128,128]{1,0:T(8,128)S(1)}, f32[32,4,128]{2,1,0:T(4,128)}, f32[32,128]{1,0:...) custom-call(f32[136,128]{1,0:T(8,128)S(1)} %collective-permute-done., ...), custom_call_target="tpu_custom_call" | custom-call | tf_op jit(solution)/shard_map/pallas_call | solution.py:269
  11.7 7.7 %all-to-all-start = ((f32[32,4,128]{2,1,0:T(4,128)}), f32[32,4,128]{2,1,0:T(4,128)S(1)}, u32[]{:S(2)}, u32[]{:S(2)}) async-start(f32[32,4,128]{2,1,0:T(4,128)} %get-tuple-element.49.refs_9_.mine_ref), calls=%async_computation | async-start | bytes 131072 | tf_op jit(solution)/shard_map/all_to_all | solution.py:283
  19.5 1.8 %collective-permute-start.3 = (f32[128,128]{1,0:T(8,128)S(1)}, f32[128,128]{1,0:T(8,128)S(1)}, u32[]{:S(2)}, u32[]{:S(2)}) collective-permute-start(f32[128,128]{1,0:T(8,128)S(1)} %get-tuple-element.44), channel_id=1, source_target_pairs={{0,2},{4,6},{8,10},{12,14},{16,18},{20,22},{24,26},{28,30},{2,0},{... | collective-permute-start | bytes 196616 | tf_op jit(solution)/shard_map/ppermute | solution.py:52
  21.3 0.7 collective-permute-start.4
  21.9 0.1 collective-permute-start.5
  22.0 2.0 %collective-permute-done.3.refs_0_ = f32[128,128]{1,0:T(8,128)S(1)} collective-permute-done((f32[128,128]{1,0:T(8,128)S(1)}, f32[128,128]{1,0:T(8,128)S(1)}, u32[]{:S(2)}, u32[]{:S(2)}) %collective-permute-start.3) | collective-permute-done | bytes 65568 | tf_op jit(solution)/shard_map/ppermute | solution.py:52
  24.1 0.0 collective-permute-done.4.refs_1_
  24.1 0.0 collective-permute-done.5.refs_2_
  24.1 2.8 %all-to-all-done = f32[32,4,128]{2,1,0:T(4,128)S(1)} async-done(((f32[32,4,128]{2,1,0:T(4,128)}), f32[32,4,128]{2,1,0:T(4,128)S(1)}, u32[]{:S(2)}, u32[]{:S(2)}) %all-to-all-start) | async-done | bytes 65568 | tf_op jit(solution)/shard_map/all_to_all | solution.py:283
  26.9 2.8 %shard_map.67 = (f32[512,128]{1,0:T(8,128)S(1)}, f32[512,128]{1,0:T(8,128)S(1)}, f32[32,128]{1,0:T(8,128)S(1)}, f32[32,8,128]{2,1,0:T(8,128)}, f32[128,128]{1,0:...) custom-call(f32[128,128]{1,0:T(8,128)S(1)} %collective-permute-done.3.refs_0_, ...), custom_call_target="tpu_custom_call" | custom-call | tf_op jit(solution)/shard_map/pallas_call | solution.py:312
  29.6 6.1 %all-to-all-start.1 = ((f32[32,8,128]{2,1,0:T(8,128)}), f32[32,8,128]{2,1,0:T(8,128)S(1)}, u32[]{:S(2)}, u32[]{:S(2)}) async-start(f32[32,8,128]{2,1,0:T(8,128)} %get-tuple-element.57), calls=%async_computation.1 | async-start | bytes 262144 | tf_op jit(solution)/shard_map/all_to_all | solution.py:324
  35.7 1.8 %collective-permute-start.6 = (f32[128,128]{1,0:T(8,128)S(1)}, f32[128,128]{1,0:T(8,128)S(1)}, u32[]{:S(2)}, u32[]{:S(2)}) collective-permute-start(f32[128,128]{1,0:T(8,128)S(1)} %get-tuple-element.53), channel_id=1, source_target_pairs={{0,2},{4,6},{8,10},{12,14},{16,18},{20,22},{24,26},{28,30},{2,0},{... | collective-permute-start | bytes 196616 | tf_op jit(solution)/shard_map/ppermute | solution.py:52
  37.6 0.7 collective-permute-start.7
  38.2 0.1 collective-permute-start.8
  38.3 2.5 %collective-permute-done.6.refs_0_ = f32[128,128]{1,0:T(8,128)S(1)} collective-permute-done((f32[128,128]{1,0:T(8,128)S(1)}, f32[128,128]{1,0:T(8,128)S(1)}, u32[]{:S(2)}, u32[]{:S(2)}) %collective-permute-start.6) | collective-permute-done | bytes 65568 | tf_op jit(solution)/shard_map/ppermute | solution.py:52
  40.8 0.0 collective-permute-done.7.refs_1_
  40.8 0.0 collective-permute-done.8.refs_2_
  40.8 3.2 %all-to-all-done.1.refs_4_ = f32[32,8,128]{2,1,0:T(8,128)S(1)} async-done(((f32[32,8,128]{2,1,0:T(8,128)}), f32[32,8,128]{2,1,0:T(8,128)S(1)}, u32[]{:S(2)}, u32[]{:S(2)}) %all-to-all-start.1) | async-done | bytes 131104 | tf_op jit(solution)/shard_map/all_to_all | solution.py:324
  44.0 0.3 shard_map.68
  44.2 15.7 %all_to_all.25.sums_ref = f32[32,16,128]{2,1,0:T(8,128)S(1)} all-to-all(f32[32,16,128]{2,1,0:T(8,128)S(1)} %get-tuple-element.58), channel_id=1, replica_groups=mesh['gx'=16,'gy'=2] {'gx','gy'}, dimensions={0} | all-to-all | bytes 524288 | tf_op jit(solution)/shard_map/all_to_all | solution.py:343
  59.9 5.1 %shard_map.69 = (f32[128,128]{1,0:T(8,128)S(1)}, f32[128,128]{1,0:T(8,128)S(1)}, f32[128,128]{1,0:T(8,128)S(1)}, f32[128,128]{1,0:T(8,128)S(1)}, f32[32,128]{1,0...) custom-call(f32[32,16,128]{2,1,0:T(8,128)S(1)} %all_to_all.25.sums_r, ...), custom_call_target="tpu_custom_call" | custom-call | tf_op jit(solution)/shard_map/pallas_call | solution.py:378
  65.0 0.3 collective-permute-start.9
  65.3 0.7 collective-permute-start.10
  66.0 0.4 collective-permute-start.11
  66.4 3.0 %collective-permute-done.9.refs_0_ = f32[128,128]{1,0:T(8,128)S(1)} collective-permute-done((f32[128,128]{1,0:T(8,128)S(1)}, f32[128,128]{1,0:T(8,128)S(1)}, u32[]{:S(2)}, u32[]{:S(2)}) %collective-permute-start.9) | collective-permute-done | bytes 65568 | tf_op jit(solution)/shard_map/ppermute | solution.py:52
  69.4 0.0 collective-permute-done.10.refs_1_
  69.4 0.0 collective-permute-done.11.refs_2_
  69.4 1.3 %shard_map.70 = (f32[512,128]{1,0:T(8,128)S(1)}, f32[32,16,128]{2,1,0:T(8,128)S(1)}) custom-call(f32[128,128]{1,0:T(8,128)S(1)} %collective-permute-done.9.refs_0_, f32[128,128]{1,0:T(8,128)S(1)} %collective-permute-done.10.refs_1_, f32[128,128]{1,0:T(8,128)S(1)} %collective-permute-done.11.refs_2_, f32[512,128]{1,0:T(8,128)S(1)} %get-tuple-element.66.refs_3_, ...), custom_call_target="tpu_custom_call" | custom-call | tf_op jit(solution)/shard_map/pallas_call | solution.py:417
  70.7 16.9 %all_to_all.26.blocks_ref = f32[32,16,128]{2,1,0:T(8,128)S(1)} all-to-all(f32[32,16,128]{2,1,0:T(8,128)S(1)} %get-tuple-element.69), channel_id=1, replica_groups=mesh['gx'=16,'gy'=2] {'gx','gy'}, dimensions={0} | all-to-all | bytes 524288 | tf_op jit(solution)/shard_map/all_to_all | solution.py:420
  87.6 0.8 shard_map.71
  88.3 2.6 %all-to-all-start.4 = ((f32[32,16,128]{2,1,0:T(8,128)}), f32[32,16,128]{2,1,0:T(8,128)S(1)}, u32[]{:S(2)}, u32[]{:S(2)}) async-start(f32[32,16,128]{2,1,0:T(8,128)} %shard_map.71), calls=%async_computation.4 | async-start | bytes 524288 | tf_op jit(solution)/shard_map/all_to_all | solution.py:426
  90.9 1.9 %shard_map.72.first_ref = f32[128,128]{1,0:T(8,128)S(1)} custom-call(f32[128,128]{1,0:T(8,128)S(1)} %get-tuple-element.70.first_ref), custom_call_target="tpu_custom_call" | custom-call | flops 251658240 | tf_op jit(solution)/shard_map/pallas_call | solution.py:397
  92.8 8.7 %all-to-all-done.4 = f32[32,16,128]{2,1,0:T(8,128)S(1)} async-done(((f32[32,16,128]{2,1,0:T(8,128)}), f32[32,16,128]{2,1,0:T(8,128)S(1)}, u32[]{:S(2)}, u32[]{:S(2)}) %all-to-all-start.4) | async-done | bytes 262176 | tf_op jit(solution)/shard_map/all_to_all | solution.py:426
  101.5 6.5 %shard_map.73 = f32[512,128]{1,0:T(8,128)} custom-call(f32[512,128]{1,0:T(8,128)S(1)} %bitcast.9, f32[128,128]{1,0:T(8,128)S(1)} %shard_map.72.first_ref, f32[128,128]{1,0:T(8,128)S(1)} %get-tuple-element.71.curv_ref, f32[128,128]{1,0:T(8,128)S(1)} %get-tuple-element.72.step_ref, f32[512,128]{1,0:T(8,128)S(1)} %get-tuple-element.73.dir_ref, ...), custom_call_target="tpu_custom_call" | custom-call | tf_op jit(solution)/shard_map/pallas_call | solution.py:438
  (1 shorter events, 0.0 us)
Async XLA Ops:
  0.0 0.7 copy-start.4
  0.7 0.9 copy-start
  1.6 0.7 copy-start.2
  2.3 7.8 %collective-permute-start = (f32[136,128]{1,0:T(8,128)S(1)}, f32[136,128]{1,0:T(8,128)S(1)}, u32[]{:S(2)}, u32[]{:S(2)}) collective-permute-start(f32[136,128]{1,0:T(8,128)S(1)} %get-tuple-element.40), channel_id=1, source_target_pairs={{0,2},{4,6},{8,10},{12,14},{16,18},{20,22},{24,26},{28,30},{2,0},{... | collective-permute-start | bytes 208904 | tf_op jit(solution)/shard_map/ppermute | solution.py:52
  5.3 4.8 %collective-permute-start.1 = (f32[136,128]{1,0:T(8,128)S(1)}, f32[136,128]{1,0:T(8,128)S(1)}, u32[]{:S(2)}, u32[]{:S(2)}) collective-permute-start(f32[136,128]{1,0:T(8,128)S(1)} %get-tuple-element.41), channel_id=1, source_target_pairs={{2,4},{6,8},{10,12},{14,16},{18,20},{22,24},{26,28},{4,2},{8,6},{1... | collective-permute-start | bytes 208904 | tf_op jit(solution)/shard_map/ppermute | solution.py:52
  6.0 4.1 %collective-permute-start.2 = (f32[136,128]{1,0:T(8,128)S(1)}, f32[136,128]{1,0:T(8,128)S(1)}, u32[]{:S(2)}, u32[]{:S(2)}) collective-permute-start(f32[136,128]{1,0:T(8,128)S(1)} %get-tuple-element.42), channel_id=1, source_target_pairs={{0,1},{1,0},{2,3},{3,2},{4,5},{5,4},{6,7},{7,6},{8,9},{9,8},{10,11... | collective-permute-start | bytes 208904 | tf_op jit(solution)/shard_map/ppermute | solution.py:52
  6.1 0.7 copy-start.7
  6.7 1.0 copy-start.5
  7.8 1.0 copy-start.6
  8.8 1.3 %copy-start.1 = (bf16[1,1,512,128]{3,2,1,0:T(8,128)(2,1)S(1)}, bf16[1,1,512,128]{3,2,1,0:T(8,128)(2,1)}, u32[]{:S(2)}) copy-start(bf16[1,1,512,128]{3,2,1,0:T(8,128)(2,1)} %param.6) | copy-start | bytes 393220
  8.8 1.3 %copy-start.3 = (f32[1,1,4,512]{3,2,1,0:T(4,128)S(1)}, f32[1,1,4,512]{3,2,1,0:T(4,128)}, u32[]{:S(2)}) copy-start(f32[1,1,4,512]{3,2,1,0:T(4,128)} %param.9) | copy-start | bytes 24580
  11.7 15.1 %all-to-all-start = ((f32[32,4,128]{2,1,0:T(4,128)}), f32[32,4,128]{2,1,0:T(4,128)S(1)}, u32[]{:S(2)}, u32[]{:S(2)}) async-start(f32[32,4,128]{2,1,0:T(4,128)} %get-tuple-element.49.refs_9_.mine_ref), calls=%async_computation | async-start | bytes 131072 | tf_op jit(solution)/shard_map/all_to_all | solution.py:283
  19.5 4.6 %collective-permute-start.3 = (f32[128,128]{1,0:T(8,128)S(1)}, f32[128,128]{1,0:T(8,128)S(1)}, u32[]{:S(2)}, u32[]{:S(2)}) collective-permute-start(f32[128,128]{1,0:T(8,128)S(1)} %get-tuple-element.44), channel_id=1, source_target_pairs={{0,2},{4,6},{8,10},{12,14},{16,18},{20,22},{24,26},{28,30},{2,0},{... | collective-permute-start | bytes 196616 | tf_op jit(solution)/shard_map/ppermute | solution.py:52
  21.3 2.8 %collective-permute-start.4 = (f32[128,128]{1,0:T(8,128)S(1)}, f32[128,128]{1,0:T(8,128)S(1)}, u32[]{:S(2)}, u32[]{:S(2)}) collective-permute-start(f32[128,128]{1,0:T(8,128)S(1)} %get-tuple-element.45), channel_id=1, source_target_pairs={{2,4},{6,8},{10,12},{14,16},{18,20},{22,24},{26,28},{4,2},{8,6},{1... | collective-permute-start | bytes 196616 | tf_op jit(solution)/shard_map/ppermute | solution.py:52
  21.9 2.1 %collective-permute-start.5 = (f32[128,128]{1,0:T(8,128)S(1)}, f32[128,128]{1,0:T(8,128)S(1)}, u32[]{:S(2)}, u32[]{:S(2)}) collective-permute-start(f32[128,128]{1,0:T(8,128)S(1)} %get-tuple-element.46), channel_id=1, source_target_pairs={{0,1},{1,0},{2,3},{3,2},{4,5},{5,4},{6,7},{7,6},{8,9},{9,8},{10,11... | collective-permute-start | bytes 196616 | tf_op jit(solution)/shard_map/ppermute | solution.py:52
  29.6 14.3 %all-to-all-start.1 = ((f32[32,8,128]{2,1,0:T(8,128)}), f32[32,8,128]{2,1,0:T(8,128)S(1)}, u32[]{:S(2)}, u32[]{:S(2)}) async-start(f32[32,8,128]{2,1,0:T(8,128)} %get-tuple-element.57), calls=%async_computation.1 | async-start | bytes 262144 | tf_op jit(solution)/shard_map/all_to_all | solution.py:324
  35.7 5.1 %collective-permute-start.6 = (f32[128,128]{1,0:T(8,128)S(1)}, f32[128,128]{1,0:T(8,128)S(1)}, u32[]{:S(2)}, u32[]{:S(2)}) collective-permute-start(f32[128,128]{1,0:T(8,128)S(1)} %get-tuple-element.53), channel_id=1, source_target_pairs={{0,2},{4,6},{8,10},{12,14},{16,18},{20,22},{24,26},{28,30},{2,0},{... | collective-permute-start | bytes 196616 | tf_op jit(solution)/shard_map/ppermute | solution.py:52
  37.6 3.2 %collective-permute-start.7 = (f32[128,128]{1,0:T(8,128)S(1)}, f32[128,128]{1,0:T(8,128)S(1)}, u32[]{:S(2)}, u32[]{:S(2)}) collective-permute-start(f32[128,128]{1,0:T(8,128)S(1)} %get-tuple-element.54), channel_id=1, source_target_pairs={{2,4},{6,8},{10,12},{14,16},{18,20},{22,24},{26,28},{4,2},{8,6},{1... | collective-permute-start | bytes 196616 | tf_op jit(solution)/shard_map/ppermute | solution.py:52
  38.2 2.6 %collective-permute-start.8 = (f32[128,128]{1,0:T(8,128)S(1)}, f32[128,128]{1,0:T(8,128)S(1)}, u32[]{:S(2)}, u32[]{:S(2)}) collective-permute-start(f32[128,128]{1,0:T(8,128)S(1)} %get-tuple-element.55), channel_id=1, source_target_pairs={{0,1},{1,0},{2,3},{3,2},{4,5},{5,4},{6,7},{7,6},{8,9},{9,8},{10,11... | collective-permute-start | bytes 196616 | tf_op jit(solution)/shard_map/ppermute | solution.py:52
  65.0 4.3 %collective-permute-start.9 = (f32[128,128]{1,0:T(8,128)S(1)}, f32[128,128]{1,0:T(8,128)S(1)}, u32[]{:S(2)}, u32[]{:S(2)}) collective-permute-start(f32[128,128]{1,0:T(8,128)S(1)} %get-tuple-element.63), channel_id=1, source_target_pairs={{0,2},{4,6},{8,10},{12,14},{16,18},{20,22},{24,26},{28,30},{2,0},{... | collective-permute-start | bytes 196616 | tf_op jit(solution)/shard_map/ppermute | solution.py:52
  65.3 4.0 %collective-permute-start.10 = (f32[128,128]{1,0:T(8,128)S(1)}, f32[128,128]{1,0:T(8,128)S(1)}, u32[]{:S(2)}, u32[]{:S(2)}) collective-permute-start(f32[128,128]{1,0:T(8,128)S(1)} %get-tuple-element.64), channel_id=1, source_target_pairs={{2,4},{6,8},{10,12},{14,16},{18,20},{22,24},{26,28},{4,2},{8,6},{1... | collective-permute-start | bytes 196616 | tf_op jit(solution)/shard_map/ppermute | solution.py:52
  66.0 3.4 %collective-permute-start.11 = (f32[128,128]{1,0:T(8,128)S(1)}, f32[128,128]{1,0:T(8,128)S(1)}, u32[]{:S(2)}, u32[]{:S(2)}) collective-permute-start(f32[128,128]{1,0:T(8,128)S(1)} %get-tuple-element.65), channel_id=1, source_target_pairs={{0,1},{1,0},{2,3},{3,2},{4,5},{5,4},{6,7},{7,6},{8,9},{9,8},{10,11... | collective-permute-start | bytes 196616 | tf_op jit(solution)/shard_map/ppermute | solution.py:52
  88.3 13.2 %all-to-all-start.4 = ((f32[32,16,128]{2,1,0:T(8,128)}), f32[32,16,128]{2,1,0:T(8,128)S(1)}, u32[]{:S(2)}, u32[]{:S(2)}) async-start(f32[32,16,128]{2,1,0:T(8,128)} %shard_map.71), calls=%async_computation.4 | async-start | bytes 524288 | tf_op jit(solution)/shard_map/all_to_all | solution.py:426

commit v2 on v1

v2 whole, which is shorter than its diff:
```python
import jax
import jax.numpy as jnp
from jax import lax
from jax.experimental import pallas as pl
from jax.experimental.pallas import tpu as pltpu
from jax.sharding import PartitionSpec as P

AXES = ("gx", "gy")
F32 = jnp.float32
BF16 = jnp.bfloat16
EXACT = lax.Precision.HIGHEST


def dot(left, right, left_dim=1, right_dim=0, precision=EXACT):
    return lax.dot_general(
        left,
        right,
        (((left_dim,), (right_dim,)), ((), ())),
        precision=precision,
        preferred_element_type=F32,
    )


def half_dot(left, right):
    return lax.dot_general(
        left, right, (((1,), (0,)), ((), ())), preferred_element_type=F32
    )


def call(body, outs, scratch=(), flops=0, moved=0, far=0, copies=0):
    sems = [pltpu.SemaphoreType.DMA((copies,))] if copies else []

    def run(*args):
        specs = [pl.BlockSpec(memory_space=pltpu.HBM if i < far else pltpu.VMEM) for i in range(len(args))]
        args = [pltpu.with_memory_space_constraint(a, pltpu.HBM) if i < far else a for i, a in enumerate(args)]
        return kernel_call(body, outs, scratch, flops, moved, sems, specs)(*args)

    return run


def kernel_call(body, outs, scratch, flops, moved, sems, specs):
    return pl.pallas_call(
        body,
        in_specs=specs,
        scratch_shapes=[pltpu.VMEM(shape, kind) for shape, kind in scratch] + sems,
        out_shape=[jax.ShapeDtypeStruct(shape, kind) for shape, kind in outs],
        compiler_params=pltpu.CompilerParams(vmem_limit_bytes=48 * 1024 * 1024),
        cost_estimate=pl.CostEstimate(flops=flops, bytes_accessed=moved, transcendentals=0),
    )


def pair_rounds(size):
    first = [(i, i + 1) for i in range(0, size - 1, 2)]
    second = [(i, i + 1) for i in range(1, size - 1, 2)]
    return [pairs + [(j, i) for i, j in pairs] for pairs in (first, second)]


def exchange(sends):
    got = []
    for axis, pieces in zip(AXES, (sends[0:2], sends[2:4])):
        for pairs, piece in zip(pair_rounds(lax.axis_size(axis)), pieces):
            got.append(lax.ppermute(piece, axis, pairs) if pairs else None)
    return got


def rounds_used():
    return [bool(p) for axis in AXES for p in pair_rounds(lax.axis_size(axis))]


def even(axis):
    return lax.rem(lax.axis_index(axis), 2) == 0


def to_rounds(faces):
    ex, ey = even("gx"), even("gy")
    return [
        jnp.where(ex, faces[1], faces[0]),
        jnp.where(ex, faces[0], faces[1]),
        jnp.where(ey, faces[3], faces[2]),
        jnp.where(ey, faces[2], faces[3]),
    ]


def to_faces(parts):
    ex, ey = even("gx"), even("gy")
    a, b, c, d = parts

    def choose(flag, yes, no):
        if yes is None and no is None:
            return None
        if yes is None:
            return jnp.where(flag, jnp.zeros_like(no), no)
        if no is None:
            return jnp.where(flag, yes, jnp.zeros_like(yes))
        return jnp.where(flag, yes, no)

    return [choose(ex, b, a), choose(ex, a, b), choose(ey, d, c), choose(ey, c, d)]


def face_weights():
    ix, iy = lax.axis_index("gx"), lax.axis_index("gy")
    shared = [
        ix > 0,
        ix < lax.axis_size("gx") - 1,
        iy > 0,
        iy < lax.axis_size("gy") - 1,
    ]
    return [jnp.where(flag, 0.5, 1.0).astype(F32) for flag in shared]


def split_faces(field):
    rows = field.shape[0] // 4
    return [field[rows * f : rows * (f + 1)] for f in range(4)]


def add_faces(field, got):
    faces = [
        mine if other is None else mine + other for mine, other in zip(split_faces(field), got)
    ]
    return jnp.concatenate(faces, axis=0)


def weighted(field, weights):
    return jnp.concatenate([w * v for w, v in zip(weights, split_faces(field))], axis=0)


def write_blocks(out_ref, rows):
    per = out_ref.shape[1]
    used = rows.shape[0] // per
    if used < out_ref.shape[0]:
        out_ref[...] = jnp.zeros(out_ref.shape, F32)
    out_ref[0:used] = rows.reshape(used, per, rows.shape[1])


def solve(matrix, right, work_ref, boosts, squarings):
    size = matrix.shape[0]
    row_id = lax.broadcasted_iota(jnp.int32, (size, size), 0)
    col_id = lax.broadcasted_iota(jnp.int32, (size, size), 1)
    eye = (row_id == col_id).astype(F32)
    matrix = 0.5 * (matrix + matrix.T)
    only = matrix * eye
    by_row = lax.rsqrt(jnp.sum(only, axis=1, keepdims=True))
    by_col = lax.rsqrt(jnp.sum(only, axis=0, keepdims=True))
    unit = matrix * by_row * by_col
    bound = jnp.max(jnp.sum(jnp.abs(unit), axis=0, keepdims=True), axis=1, keepdims=True)
    scale = 1.9 / bound
    answer = right * (by_row * scale)
    power = eye - scale * unit

    def step(answer, power):
        both = dot(power, jnp.concatenate([answer, power], axis=1))
        return answer + both[:, :size], both[:, size:]

    for k in range(squarings):
        answer, power = step(answer, power)
        if k < len(boosts):
            power = boosts[k] * power + (1.0 - boosts[k]) * eye
            answer = boosts[k] * answer
    work_ref[:, 0:size] = answer + dot(power, answer)
    largest = jnp.max(jnp.abs(power))

    @pl.when(jnp.logical_not(largest < 3e-4))
    def _():
        work_ref[:, 0:size] = answer
        work_ref[:, size:] = power

        def again(carry):
            answer, power = step(work_ref[:, 0:size], work_ref[:, size:])
            work_ref[:, 0:size] = answer
            work_ref[:, size:] = power
            return carry[0] + 1, jnp.max(jnp.abs(power))

        lax.while_loop(
            lambda carry: jnp.logical_and(carry[0] < 40, carry[1] > 1e-7),
            again,
            (jnp.int32(0), largest),
        )

    return work_ref[:, 0:size] * by_row


def local(loads, schur, local_inverse, coarse_basis, coarse_inverse, face_map):
    loads, schur, local_inverse = loads[0, 0], schur[0, 0], local_inverse[0, 0]
    basis, coarse_rows, slot_map = coarse_basis[0, 0], coarse_inverse[0, 0], face_map[0, 0]
    unknowns, cols = loads.shape
    face = unknowns // 4
    nco, coarse_all = coarse_rows.shape
    devices = lax.axis_size("gx") * lax.axis_size("gy")
    chunks = coarse_all // cols
    used = rounds_used()
    field = (unknowns, cols)
    gram_shape = (cols, cols)
    work = [((cols, 2 * cols), F32)]
    face_out = ((face, cols), F32)

    def give(refs, faces):
        for ref, value, flag in zip(refs, to_rounds(faces), used):
            if flag:
                ref[...] = value

    def take(refs):
        return to_faces([ref[...] if flag else None for ref, flag in zip(refs, used)])

    def trade(sends):
        return [got for got in exchange(sends) if got is not None]

    def spread(refs):
        left = list(refs)
        return [left.pop(0) if flag else None for flag in used]

    nrounds = sum(used)

    def fill(values):
        left = list(values)
        return [left.pop(0) if flag else None for flag in used]

    head = face + nco + nco * chunks

    def send_loads(loads_hbm, basis_hbm, rows_hbm, loads_ref, basis_ref, rows_ref, *outs):
        outs, raw_ref, sems = spread(outs[:-2]), outs[-2], outs[-1]
        fetches = [
            pltpu.make_async_copy(src, dst, sems.at[k])
            for k, (src, dst) in enumerate(
                ((loads_hbm, raw_ref), (basis_hbm, basis_ref), (rows_hbm, rows_ref))
            )
        ]
        for fetch in fetches:
            fetch.start()
        for fetch in fetches:
            fetch.wait()
        wide_loads = raw_ref[...].astype(F32)
        loads_ref[...] = wide_loads
        basis_now = basis_ref[...]
        rows_now = rows_ref[...]
        packs = []
        for f, part in enumerate(split_faces(wide_loads)):
            packs.append(
                jnp.concatenate(
                    [part, basis_now[:, face * f : face * (f + 1)]]
                    + [rows_now[:, cols * c : cols * (c + 1)] for c in range(chunks)],
                    axis=0,
                )
            )
        give(outs, packs)

    outs = call(
        send_loads,
        [(field, F32), (basis.shape, F32), (coarse_rows.shape, F32)] + [((head, cols), F32)] * nrounds,
        [(field, BF16)],
        far=3,
        copies=3,
    )(loads, basis, coarse_rows)
    loads, basis, coarse_rows = outs[:3]
    got_a = trade(fill(outs[3:]))

    def reorder(first_hbm, second_hbm, map_ref, first_out, second_out, first_raw, second_raw, sems):
        fetches = [
            pltpu.make_async_copy(src, dst, sems.at[k])
            for k, (src, dst) in enumerate(((first_hbm, first_raw), (second_hbm, second_raw)))
        ]
        for fetch in fetches:
            fetch.start()
        slots = lax.broadcasted_iota(jnp.int32, (unknowns, unknowns), 0)
        pick = (slots == map_ref[...]).astype(F32).astype(BF16)
        for fetch, ref, out in zip(fetches, (first_raw, second_raw), (first_out, second_out)):
            fetch.wait()
            rows = half_dot(pick, ref[...]).astype(BF16)
            out[...] = lax.dot_general(
                rows, pick, (((1,), (1,)), ((), ())), preferred_element_type=F32
            ).astype(BF16)

    square = (unknowns, unknowns)
    inverse_here, schur_here = call(
        reorder,
        [(square, BF16)] * 2,
        [(square, BF16)] * 2,
        flops=8 * unknowns**3,
        moved=8 * unknowns**2,
        far=2,
        copies=2,
    )(local_inverse, schur, slot_map.reshape(1, unknowns))

    def first_local(*refs):
        got = take(spread(refs[:nrounds]))
        loads_ref, inverse_ref = refs[nrounds : nrounds + 2]
        res_ref, scaled_ref, product_ref, part_ref = refs[nrounds + 2 : nrounds + 6]
        sends = spread(refs[nrounds + 6 :])
        weights = face_weights()
        residual = add_faces(loads_ref[...], [g if g is None else g[:face] for g in got])
        scaled = weighted(residual, weights)
        product = half_dot(inverse_ref[...], scaled.astype(BF16))
        part = weighted(product, weights)
        give(sends, split_faces(part))
        res_ref[...] = residual
        scaled_ref[...] = scaled
        product_ref[...] = product
        part_ref[...] = part

    outs = call(first_local, [(field, F32)] * 4 + [face_out] * nrounds)(*got_a, loads, inverse_here)
    residual, scaled, product, part = outs[:4]
    got_b = trade(fill(outs[4:]))

    def first_coarse(basis_ref, scaled_ref, ci_ref):
        coarse_input = dot(basis_ref[...], scaled_ref[...])
        ci_ref[...] = jnp.broadcast_to(coarse_input[None], ci_ref.shape)

    (coarse_input,) = call(first_coarse, [((devices, nco, cols), F32)])(basis, scaled)
    coarse_all_in = lax.all_to_all(coarse_input, AXES, 0, 0).reshape(coarse_all, cols)

    def first_tables(*refs):
        got = take(spread(refs[:nrounds]))
        scaled_ref, product_ref, basis_ref, rows_ref = refs[nrounds : nrounds + 4]
        gram_ref, bases_ref, table_ref, wide_ref = refs[nrounds + 4 :]
        weights = face_weights()
        gram_ref[...] = dot(scaled_ref[...], product_ref[...], 0, 0)
        basis_now = basis_ref[...]
        bases, tables = [], []
        for f in range(4):
            mine = weights[f] * basis_now[:, face * f : face * (f + 1)]
            other = got[f]
            if other is None:
                bases += [mine, jnp.zeros_like(mine)]
                tables += [rows_ref[...], jnp.zeros((nco, coarse_all), F32)]
            else:
                bases += [mine, 0.5 * other[face : face + nco]]
                tables += [
                    rows_ref[...],
                    jnp.concatenate(
                        [
                            other[face + nco * (c + 1) : face + nco * (c + 2)]
                            for c in range(chunks)
                        ],
                        axis=1,
                    ),
                ]
        bases_ref[...] = jnp.concatenate(bases, axis=0)
        table_ref[...] = jnp.concatenate(tables, axis=0)
        src = lax.broadcasted_iota(jnp.int32, (cols, wide), 0)
        dst = lax.broadcasted_iota(jnp.int32, (cols, wide), 1)
        widen = (dst == src // nco * 8 + lax.rem(src, nco)).astype(F32)
        for c in range(chunks):
            wide_ref[:, wide * c : wide * (c + 1)] = dot(table_ref[:, cols * c : cols * (c + 1)], widen)

    wide = cols // nco * 8
    gram_part, bases, table, table_wide = call(
        first_tables,
        [
            (gram_shape, F32),
            ((8 * nco, face), F32),
            ((8 * nco, coarse_all), F32),
            ((8 * nco, wide * chunks), F32),
        ],
    )(*got_a, scaled, product, basis, coarse_rows)

    def coarse_part(bases_now, values):
        return [
            dot(bases_now[2 * nco * f : 2 * nco * (f + 1)], values[2 * nco * f : 2 * nco * (f + 1)], 0, 0)
            for f in range(4)
        ]

    per = 8 * -(-2 * cols // (8 * devices))
    blocks_out = ((devices, per, cols), F32)

    def first_direction(*refs):
        got = take(spread(refs[:nrounds]))
        part_ref, all_ref, bases_ref, table_ref, schur_ref = refs[nrounds : nrounds + 5]
        dir_ref, image_ref, values_ref = refs[nrounds + 5 : nrounds + 8]
        sends = spread(refs[nrounds + 8 :])
        values = dot(table_ref[...], all_ref[...])
        values_ref[...] = values
        coarse = coarse_part(bases_ref[...], values)
        update = add_faces(part_ref[...], got) + jnp.concatenate(coarse, axis=0)
        dir_ref[...] = update
        image = half_dot(schur_ref[...], update.astype(BF16))
        image_ref[...] = image
        give(sends, split_faces(image))

    outs = call(
        first_direction,
        [(field, F32), (field, F32), ((8 * nco, cols), F32)] + [face_out] * nrounds,
    )(*got_b, part, coarse_all_in, bases, table, schur_here)
    direction, image, values = outs[:3]
    got_d = trade(fill(outs[3:]))

    def first_grams(dir_ref, image_ref, values_ref, mine_ref, gram_ref, blocks_ref):
        first = gram_ref[...] + dot(mine_ref[0], values_ref[0:nco], 0, 0)
        curvature = dot(dir_ref[...], image_ref[...], 0, 0)
        write_blocks(blocks_ref, jnp.concatenate([curvature, first], axis=0))

    (blocks,) = call(first_grams, [blocks_out])(direction, image, values, coarse_input, gram_part)
    blocks = lax.all_to_all(blocks, AXES, 0, 0)

    def first_sums(*refs):
        got = take(spread(refs[:nrounds]))
        image_ref, blocks_ref, basis_ref = refs[nrounds : nrounds + 3]
        full_ref, sum_ref, mine_ref = refs[nrounds + 3 :]
        image_vec = add_faces(image_ref[...], got)
        full_ref[...] = image_vec
        coarse_image = dot(basis_ref[...], weighted(image_vec, face_weights()))
        mine_ref[...] = coarse_image
        block = jnp.concatenate(
            [jnp.sum(blocks_ref[...], axis=0), coarse_image, jnp.zeros((8 - nco, cols), F32)], axis=0
        )
        sum_ref[...] = jnp.broadcast_to(block[None], sum_ref.shape)

    image_vec, sums, coarse_image = call(
        first_sums,
        [(field, F32), ((devices, per + 8, cols), F32), ((nco, cols), F32)],
    )(*got_d, image, blocks, basis)
    sums = lax.all_to_all(sums, AXES, 0, 0)

    def second_local(sums_ref, res_ref, full_ref, inverse_ref, *outs):
        outs, work_ref = outs[:-1], outs[-1]
        curv_ref, first_ref, step_ref, scaled_ref, product_ref, part_ref = outs[:6]
        sends = spread(outs[6:])
        both = sums_ref[:, 0:per, :].reshape(devices * per, cols)
        curvature, first = both[:cols], both[cols : 2 * cols]
        step = solve(curvature, first, work_ref, (), 5)
        weights = face_weights()
        residual = res_ref[...] - dot(full_ref[...], step)
        scaled = weighted(residual, weights)
        product = half_dot(inverse_ref[...], scaled.astype(BF16))
        part = weighted(product, weights)
        part_ref[...] = part
        give(sends, split_faces(part))
        scaled_ref[...] = scaled
        product_ref[...] = product
        curv_ref[...] = curvature
        first_ref[...] = first
        step_ref[...] = step

    outs = call(
        second_local,
        [(gram_shape, F32)] * 3 + [(field, F32)] * 3 + [face_out] * nrounds,
        work,
    )(sums, residual, image_vec, inverse_here)
    curvature, first, step, scaled, product, part = outs[:6]
    got_e = trade(fill(outs[6:]))

    def second_coarse(
        sums_ref, table_ref, values_ref, mine_ref, image_ref, step_ref, scaled_ref, product_ref,
        next_ref, values_out
    ):
        rows = sums_ref[:, per : per + 8, :].reshape(devices * 8, cols)
        step = step_ref[...]
        values_now = values_ref[...] - dot(dot(table_ref[...], rows), step)
        values_out[...] = values_now
        own = mine_ref[0] - dot(image_ref[...], step)
        next_ref[...] = dot(scaled_ref[...], product_ref[...], 0, 0) + dot(own, values_now[:nco], 0, 0)

    next_part, values = call(
        second_coarse, [(gram_shape, F32), ((8 * nco, cols), F32)], flops=2 * 12 * unknowns * cols**2
    )(sums, table_wide, values, coarse_input, coarse_image, step, scaled, product)

    def second_direction(*refs):
        got = take(spread(refs[:nrounds]))
        part_ref, next_ref, values_ref, bases_ref, schur_ref = refs[nrounds : nrounds + 5]
        update_ref, blocks_ref = refs[nrounds + 5 :]
        coarse = coarse_part(bases_ref[...], values_ref[...])
        update = add_faces(part_ref[...], got) + jnp.concatenate(coarse, axis=0)
        update_ref[...] = update
        high = update.astype(BF16)
        low = (update - high.astype(F32)).astype(BF16)
        both = half_dot(schur_ref[...], jnp.concatenate([high, low], axis=1))
        product = both[:, :cols] + both[:, cols:]
        square = dot(update, product, 0, 0)
        write_blocks(blocks_ref, jnp.concatenate([next_ref[...], square], axis=0))

    update, blocks = call(second_direction, [(field, F32), blocks_out])(
        *got_e, part, next_part, values, bases, schur_here
    )
    blocks = lax.all_to_all(blocks, AXES, 0, 0)

    def invert(first_ref, out_ref, work_ref):
        size = first_ref.shape[0]
        row_id = lax.broadcasted_iota(jnp.int32, (size, size), 0)
        col_id = lax.broadcasted_iota(jnp.int32, (size, size), 1)
        out_ref[...] = solve(first_ref[...], (row_id == col_id).astype(F32), work_ref, (), 5)

    (first_inverse,) = call(invert, [(gram_shape, F32)], work, flops=2 * 60 * cols**3)(first)

    def second_sums(blocks_ref, out_ref):
        out_ref[...] = jnp.broadcast_to(jnp.sum(blocks_ref[...], axis=0)[None], out_ref.shape)

    (sums,) = call(second_sums, [blocks_out])(blocks)
    sums = lax.all_to_all(sums, AXES, 0, 0).reshape(devices * per, cols)

    def finish(sums_ref, first_ref, curv_ref, step_ref, dir_ref, update_ref, out_ref, work_ref):
        next_gram, square = sums_ref[0:cols], sums_ref[cols : 2 * cols]
        ratio = dot(first_ref[...], next_gram)
        curvature = square - dot(ratio, dot(curv_ref[...], ratio), 0, 0)
        step = solve(curvature, next_gram, work_ref, (1.8, 1.8, 1.5), 7)
        total = step_ref[...] + dot(ratio, step)
        out_ref[...] = dot(dir_ref[...], total) + dot(update_ref[...], step)

    (solved,) = call(finish, [(field, F32)], work)(
        sums, first_inverse, curvature, step, direction, update
    )
    return solved[None, None]


def solution(mesh):
    return jax.shard_map(
        local,
        mesh=mesh,
        in_specs=(
            P("gx", "gy", None, None),
            P("gx", "gy", None, None),
            P("gx", "gy", None, None),
            P("gx", "gy", None, None),
            P("gx", "gy", None, None),
            P("gx", "gy", None),
        ),
        out_specs=P("gx", "gy", None, None),
        check_vma=False,
    )
```

time: 109 us -> 98 us (0.90)
  waiting for transfers between devices: 22.2 us -> 17.5 us
  local copies, waits for them, and re-layouts: 5.05 us -> 0.68 us
  blocking collectives: 32.6 us -> 30.2 us
    unnamed x16 -> x2, local copies, waits for them, and re-layouts: 5.05 us -> 0.68 us
    all_to_all x1, waiting for transfers between devices: 8.72 us -> 6.13 us  [local(): sums = lax.all_to_all(sums, AXES, 0, 0).reshape(devices * per, cols)]
    all_to_all x1, blocking collectives: 16.9 us -> 14.5 us  [local(): blocks = lax.all_to_all(blocks, AXES, 0, 0)]
    ppermute x12, waiting for transfers between devices: 7.54 us -> 5.43 us  [exchange(): got.append(lax.ppermute(piece, axis, pairs) if pairs else None)]
    pallas_call x10 -> x14, Pallas kernels: 21.4 us -> 21.6 us  [run(): return kernel_call(body, outs, scratch, flops, moved, sems, specs)(*args)]
  transfers between devices with their start and end apart: 15 -> 15, of which waited for: 6 -> 6; matrix products, arithmetic and copies ran while one was open for 0% -> 0% of each run, Pallas kernels for 3% -> 7%
where the time goes in v2:
time: 98 us; the launch traced here: 97.1 us
  blocking collectives  30.2 us (31%)
  starting transfers between devices  26.9 us (27%)
  Pallas kernels  21.6 us (22%)
  waiting for transfers between devices  17.5 us (18%)
    pallas_call x14, Pallas kernels, run(): return kernel_call(body, outs, scratch, flops, moved, sems, specs)(*args)  21.6 us
    all_to_all x1, blocking collectives, local(): sums = lax.all_to_all(sums, AXES, 0, 0)  15.7 us
    all_to_all x1, blocking collectives, local(): blocks = lax.all_to_all(blocks, AXES, 0, 0)  14.5 us
    ppermute x12, starting transfers between devices, exchange(): got.append(lax.ppermute(piece, axis, pairs) if pairs else None)  10.2 us
    all_to_all x1, starting transfers between devices, local(): lax.all_to_all(coarse_input, AXES, 0, 0).reshape(coarse_all, cols)  8.06 us
    all_to_all x1, waiting for transfers between devices, local(): sums = lax.all_to_all(sums, AXES, 0, 0).reshape(devices * per, cols)  6.13 us
    all_to_all x1, starting transfers between devices, local(): blocks = lax.all_to_all(blocks, AXES, 0, 0)  6.1 us
    ppermute x12, waiting for transfers between devices, exchange(): got.append(lax.ppermute(piece, axis, pairs) if pairs else None)  5.43 us
  transfers between devices with their start and end apart: 15, of which 6 were waited for; matrix products, arithmetic and copies ran while one was open for 0% of the time, Pallas kernels for 7%

profile of v2, /device:TPU:0, one launch (start us, length us, event | category | flops | bytes accessed | tf_op | source)
XLA Modules:
  0.0 97.1 jit_solution(9912965417174109841)
XLA Ops:
  0.0 1.0 shard_map.64
  1.0 3.0 %collective-permute-start = (f32[136,128]{1,0:T(8,128)S(1)}, f32[136,128]{1,0:T(8,128)S(1)}, u32[]{:S(2)}, u32[]{:S(2)}) collective-permute-start(f32[136,128]{1,0:T(8,128)S(1)} %get-tuple-element.46), channel_id=1, source_target_pairs={{0,2},{4,6},{8,10},{12,14},{16,18},{20,22},{24,26},{28,30},{2,0},{... | collective-permute-start | bytes 208904 | tf_op jit(solution)/shard_map/ppermute | solution.py:62
  4.0 0.7 collective-permute-start.1
  4.6 0.1 collective-permute-start.2
  4.7 0.0 copy-start
  4.7 0.7 copy-done
  5.4 2.5 %shard_map.65 = (bf16[512,512]{1,0:T(8,128)(2,1)S(1)}, bf16[512,512]{1,0:T(8,128)(2,1)S(1)}) custom-call(bf16[512,512]{1,0:T(8,128)(2,1)} %bitcast.15, bf16[512,512]{1,0:T(8,128)(2,1)} %bitcast.16, s32[1,512]{1,0:T(1,128)S(1)} %bitcast.11), custom_call_target="tpu_custom_call" | custom-call | flops 1073741824 | bytes 2097152 | tf_op jit(solution)/shard_map/pallas_call | solution.py:36
  7.9 0.0 collective-permute-done.refs_0_
  7.9 0.0 collective-permute-done.1.refs_1_
  7.9 0.0 collective-permute-done.2.refs_2_
  7.9 0.3 shard_map.66
  8.3 0.9 shard_map.67.mine_ref
  9.1 8.1 %all-to-all-start = ((f32[32,4,128]{2,1,0:T(4,128)}), f32[32,4,128]{2,1,0:T(4,128)S(1)}, u32[]{:S(2)}, u32[]{:S(2)}) async-start(f32[32,4,128]{2,1,0:T(4,128)} %shard_map.67.mine_ref), calls=%async_computation | async-start | bytes 131072 | tf_op jit(solution)/shard_map/all_to_all | solution.py:308
  17.2 1.8 %collective-permute-start.3 = (f32[128,128]{1,0:T(8,128)S(1)}, f32[128,128]{1,0:T(8,128)S(1)}, u32[]{:S(2)}, u32[]{:S(2)}) collective-permute-start(f32[128,128]{1,0:T(8,128)S(1)} %get-tuple-element.51), channel_id=1, source_target_pairs={{0,2},{4,6},{8,10},{12,14},{16,18},{20,22},{24,26},{28,30},{2,0},{... | collective-permute-start | bytes 196616 | tf_op jit(solution)/shard_map/ppermute | solution.py:62
  19.0 0.7 collective-permute-start.4
  19.7 0.1 collective-permute-start.5
  19.8 0.5 shard_map.68
  20.2 1.6 %collective-permute-done.3.refs_0_ = f32[128,128]{1,0:T(8,128)S(1)} collective-permute-done((f32[128,128]{1,0:T(8,128)S(1)}, f32[128,128]{1,0:T(8,128)S(1)}, u32[]{:S(2)}, u32[]{:S(2)}) %collective-permute-start.3) | collective-permute-done | bytes 65568 | tf_op jit(solution)/shard_map/ppermute | solution.py:62
  21.8 0.0 collective-permute-done.4.refs_1_
  21.8 0.0 collective-permute-done.5.refs_2_
  21.8 2.8 %all-to-all-done = f32[32,4,128]{2,1,0:T(4,128)S(1)} async-done(((f32[32,4,128]{2,1,0:T(4,128)}), f32[32,4,128]{2,1,0:T(4,128)S(1)}, u32[]{:S(2)}, u32[]{:S(2)}) %all-to-all-start) | async-done | bytes 65568 | tf_op jit(solution)/shard_map/all_to_all | solution.py:308
  24.6 0.9 shard_map.69
  25.5 2.0 %shard_map.70 = f32[32,8,128]{2,1,0:T(8,128)} custom-call(f32[512,128]{1,0:T(8,128)S(1)} %get-tuple-element.66.dir_ref, f32[512,128]{1,0:T(8,128)S(1)} %get-tuple-element.65.image_ref.refs_3_, f32[32,128]{1,0:T(8,128)S(1)} %get-tuple-element.67.values_ref, f32[32,4,128]{2,1,0:T(4,128)} %shard_map.67.mine_ref, f32[128,128]{1,0:T(8,128)S(1)} %get-tuple-element.68.gram_ref), custom_call_target="tpu_custom_call" | custom-call | tf_op jit(solution)/shard_map/pallas_call | solution.py:36
  27.5 6.1 %all-to-all-start.1 = ((f32[32,8,128]{2,1,0:T(8,128)}), f32[32,8,128]{2,1,0:T(8,128)S(1)}, u32[]{:S(2)}, u32[]{:S(2)}) async-start(f32[32,8,128]{2,1,0:T(8,128)} %shard_map.70), calls=%async_computation.1 | async-start | bytes 262144 | tf_op jit(solution)/shard_map/all_to_all | solution.py:391
  33.6 1.8 %collective-permute-start.6 = (f32[128,128]{1,0:T(8,128)S(1)}, f32[128,128]{1,0:T(8,128)S(1)}, u32[]{:S(2)}, u32[]{:S(2)}) collective-permute-start(f32[128,128]{1,0:T(8,128)S(1)} %get-tuple-element.62), channel_id=1, source_target_pairs={{0,2},{4,6},{8,10},{12,14},{16,18},{20,22},{24,26},{28,30},{2,0},{... | collective-permute-start | bytes 196616 | tf_op jit(solution)/shard_map/ppermute | solution.py:62
  35.4 0.7 collective-permute-start.7
  36.1 0.1 collective-permute-start.8
  36.2 2.5 %collective-permute-done.6.refs_0_ = f32[128,128]{1,0:T(8,128)S(1)} collective-permute-done((f32[128,128]{1,0:T(8,128)S(1)}, f32[128,128]{1,0:T(8,128)S(1)}, u32[]{:S(2)}, u32[]{:S(2)}) %collective-permute-start.6) | collective-permute-done | bytes 65568 | tf_op jit(solution)/shard_map/ppermute | solution.py:62
  38.6 0.0 collective-permute-done.7.refs_1_
  38.6 0.0 collective-permute-done.8.refs_2_
  38.7 3.2 %all-to-all-done.1.refs_4_ = f32[32,8,128]{2,1,0:T(8,128)S(1)} async-done(((f32[32,8,128]{2,1,0:T(8,128)}), f32[32,8,128]{2,1,0:T(8,128)S(1)}, u32[]{:S(2)}, u32[]{:S(2)}) %all-to-all-start.1) | async-done | bytes 131104 | tf_op jit(solution)/shard_map/all_to_all | solution.py:391
  41.8 0.3 shard_map.71
  42.1 15.7 %all_to_all.25.sums_ref = f32[32,16,128]{2,1,0:T(8,128)S(1)} all-to-all(f32[32,16,128]{2,1,0:T(8,128)S(1)} %get-tuple-element.69), channel_id=1, replica_groups=mesh['gx'=16,'gy'=2] {'gx','gy'}, dimensions={0} | all-to-all | bytes 524288 | tf_op jit(solution)/shard_map/all_to_all | solution.py:410
  57.8 2.9 %shard_map.72 = (f32[128,128]{1,0:T(8,128)S(1)}, f32[128,128]{1,0:T(8,128)S(1)}, f32[128,128]{1,0:T(8,128)S(1)}, f32[512,128]{1,0:T(8,128)S(1)}, f32[512,128]{1,...) custom-call(f32[32,16,128]{2,1,0:T(8,128)S(1)} %all_to_all.25.sums_r, ...), custom_call_target="tpu_custom_call" | custom-call | tf_op jit(solution)/shard_map/pallas_call | solution.py:36
  60.7 0.3 collective-permute-start.9
  61.0 0.7 collective-permute-start.10
  61.7 0.4 collective-permute-start.11
  62.1 1.6 %shard_map.73 = (f32[128,128]{1,0:T(8,128)S(1)}, f32[32,128]{1,0:T(8,128)S(1)}) custom-call(f32[32,16,128]{2,1,0:T(8,128)S(1)} %all_to_all.25.sums_ref, f32[32,256]{1,0:T(8,128)S(1)} %get-tuple-element.76.table_ref, f32[32,128]{1,0:T(8,128)S(1)} %get-tuple-element.67.values_ref, f32[32,4,128]{2,1,0:T(4,128)} %shard_map.67.mine_ref, ...), custom_call_target="tpu_custom_call" | custom-call | flops 201326592 | tf_op jit(solution)/shard_map/pallas_call | solution.py:36
  63.7 1.4 %collective-permute-done.9.refs_0_ = f32[128,128]{1,0:T(8,128)S(1)} collective-permute-done((f32[128,128]{1,0:T(8,128)S(1)}, f32[128,128]{1,0:T(8,128)S(1)}, u32[]{:S(2)}, u32[]{:S(2)}) %collective-permute-start.9) | collective-permute-done | bytes 65568 | tf_op jit(solution)/shard_map/ppermute | solution.py:62
  65.1 0.0 collective-permute-done.10.refs_1_
  65.1 0.0 collective-permute-done.11.refs_2_
  65.1 1.1 %shard_map.74 = (f32[512,128]{1,0:T(8,128)S(1)}, f32[32,8,128]{2,1,0:T(8,128)S(1)}) custom-call(f32[128,128]{1,0:T(8,128)S(1)} %collective-permute-done.9.refs_0_, f32[128,128]{1,0:T(8,128)S(1)} %collective-permute-done.10.refs_1_, f32[128,128]{1,0:T(8,128)S(1)} %collective-permute-done.11.refs_2_, f32[512,128]{1,0:T(8,128)S(1)} %get-tuple-element.75.refs_3_, ...), custom_call_target="tpu_custom_call" | custom-call | tf_op jit(solution)/shard_map/pallas_call | solution.py:36
  66.2 14.5 %all_to_all.26.blocks_ref = f32[32,8,128]{2,1,0:T(8,128)S(1)} all-to-all(f32[32,8,128]{2,1,0:T(8,128)S(1)} %get-tuple-element.83), channel_id=1, replica_groups=mesh['gx'=16,'gy'=2] {'gx','gy'}, dimensions={0} | all-to-all | bytes 262144 | tf_op jit(solution)/shard_map/all_to_all | solution.py:472
  80.7 0.7 shard_map.75
  81.4 2.6 %all-to-all-start.4 = ((f32[32,8,128]{2,1,0:T(8,128)}), f32[32,8,128]{2,1,0:T(8,128)S(1)}, u32[]{:S(2)}, u32[]{:S(2)}) async-start(f32[32,8,128]{2,1,0:T(8,128)} %shard_map.75), calls=%async_computation.4 | async-start | bytes 262144 | tf_op jit(solution)/shard_map/all_to_all | solution.py:486
  84.0 2.1 %shard_map.76.first_ref = f32[128,128]{1,0:T(8,128)S(1)} custom-call(f32[128,128]{1,0:T(8,128)S(1)} %get-tuple-element.84.first_ref), custom_call_target="tpu_custom_call" | custom-call | flops 251658240 | tf_op jit(solution)/shard_map/pallas_call | solution.py:36
  86.1 6.1 %all-to-all-done.4 = f32[32,8,128]{2,1,0:T(8,128)S(1)} async-done(((f32[32,8,128]{2,1,0:T(8,128)}), f32[32,8,128]{2,1,0:T(8,128)S(1)}, u32[]{:S(2)}, u32[]{:S(2)}) %all-to-all-start.4) | async-done | bytes 131104 | tf_op jit(solution)/shard_map/all_to_all | solution.py:486
  92.2 4.9 %shard_map.77 = f32[512,128]{1,0:T(8,128)} custom-call(f32[256,128]{1,0:T(8,128)S(1)} %bitcast.9, f32[128,128]{1,0:T(8,128)S(1)} %shard_map.76.first_ref, f32[128,128]{1,0:T(8,128)S(1)} %get-tuple-element.85.curv_ref, f32[128,128]{1,0:T(8,128)S(1)} %get-tuple-element.78.step_ref, f32[512,128]{1,0:T(8,128)S(1)} %get-tuple-element.66.dir_ref, ...), custom_call_target="tpu_custom_call" | custom-call | tf_op jit(solution)/shard_map/pallas_call | solution.py:36
Async XLA Ops:
  1.0 6.9 %collective-permute-start = (f32[136,128]{1,0:T(8,128)S(1)}, f32[136,128]{1,0:T(8,128)S(1)}, u32[]{:S(2)}, u32[]{:S(2)}) collective-permute-start(f32[136,128]{1,0:T(8,128)S(1)} %get-tuple-element.46), channel_id=1, source_target_pairs={{0,2},{4,6},{8,10},{12,14},{16,18},{20,22},{24,26},{28,30},{2,0},{... | collective-permute-start | bytes 208904 | tf_op jit(solution)/shard_map/ppermute | solution.py:62
  4.0 3.9 %collective-permute-start.1 = (f32[136,128]{1,0:T(8,128)S(1)}, f32[136,128]{1,0:T(8,128)S(1)}, u32[]{:S(2)}, u32[]{:S(2)}) collective-permute-start(f32[136,128]{1,0:T(8,128)S(1)} %get-tuple-element.47), channel_id=1, source_target_pairs={{2,4},{6,8},{10,12},{14,16},{18,20},{22,24},{26,28},{4,2},{8,6},{1... | collective-permute-start | bytes 208904 | tf_op jit(solution)/shard_map/ppermute | solution.py:62
  4.6 3.3 %collective-permute-start.2 = (f32[136,128]{1,0:T(8,128)S(1)}, f32[136,128]{1,0:T(8,128)S(1)}, u32[]{:S(2)}, u32[]{:S(2)}) collective-permute-start(f32[136,128]{1,0:T(8,128)S(1)} %get-tuple-element.48), channel_id=1, source_target_pairs={{0,1},{1,0},{2,3},{3,2},{4,5},{5,4},{6,7},{7,6},{8,9},{9,8},{10,11... | collective-permute-start | bytes 208904 | tf_op jit(solution)/shard_map/ppermute | solution.py:62
  4.7 0.7 copy-start
  9.1 15.5 %all-to-all-start = ((f32[32,4,128]{2,1,0:T(4,128)}), f32[32,4,128]{2,1,0:T(4,128)S(1)}, u32[]{:S(2)}, u32[]{:S(2)}) async-start(f32[32,4,128]{2,1,0:T(4,128)} %shard_map.67.mine_ref), calls=%async_computation | async-start | bytes 131072 | tf_op jit(solution)/shard_map/all_to_all | solution.py:308
  17.2 4.6 %collective-permute-start.3 = (f32[128,128]{1,0:T(8,128)S(1)}, f32[128,128]{1,0:T(8,128)S(1)}, u32[]{:S(2)}, u32[]{:S(2)}) collective-permute-start(f32[128,128]{1,0:T(8,128)S(1)} %get-tuple-element.51), channel_id=1, source_target_pairs={{0,2},{4,6},{8,10},{12,14},{16,18},{20,22},{24,26},{28,30},{2,0},{... | collective-permute-start | bytes 196616 | tf_op jit(solution)/shard_map/ppermute | solution.py:62
  19.0 2.8 %collective-permute-start.4 = (f32[128,128]{1,0:T(8,128)S(1)}, f32[128,128]{1,0:T(8,128)S(1)}, u32[]{:S(2)}, u32[]{:S(2)}) collective-permute-start(f32[128,128]{1,0:T(8,128)S(1)} %get-tuple-element.52), channel_id=1, source_target_pairs={{2,4},{6,8},{10,12},{14,16},{18,20},{22,24},{26,28},{4,2},{8,6},{1... | collective-permute-start | bytes 196616 | tf_op jit(solution)/shard_map/ppermute | solution.py:62
  19.7 2.1 %collective-permute-start.5 = (f32[128,128]{1,0:T(8,128)S(1)}, f32[128,128]{1,0:T(8,128)S(1)}, u32[]{:S(2)}, u32[]{:S(2)}) collective-permute-start(f32[128,128]{1,0:T(8,128)S(1)} %get-tuple-element.53), channel_id=1, source_target_pairs={{0,1},{1,0},{2,3},{3,2},{4,5},{5,4},{6,7},{7,6},{8,9},{9,8},{10,11... | collective-permute-start | bytes 196616 | tf_op jit(solution)/shard_map/ppermute | solution.py:62
  27.5 14.3 %all-to-all-start.1 = ((f32[32,8,128]{2,1,0:T(8,128)}), f32[32,8,128]{2,1,0:T(8,128)S(1)}, u32[]{:S(2)}, u32[]{:S(2)}) async-start(f32[32,8,128]{2,1,0:T(8,128)} %shard_map.70), calls=%async_computation.1 | async-start | bytes 262144 | tf_op jit(solution)/shard_map/all_to_all | solution.py:391
  33.6 5.1 %collective-permute-start.6 = (f32[128,128]{1,0:T(8,128)S(1)}, f32[128,128]{1,0:T(8,128)S(1)}, u32[]{:S(2)}, u32[]{:S(2)}) collective-permute-start(f32[128,128]{1,0:T(8,128)S(1)} %get-tuple-element.62), channel_id=1, source_target_pairs={{0,2},{4,6},{8,10},{12,14},{16,18},{20,22},{24,26},{28,30},{2,0},{... | collective-permute-start | bytes 196616 | tf_op jit(solution)/shard_map/ppermute | solution.py:62
  35.4 3.2 %collective-permute-start.7 = (f32[128,128]{1,0:T(8,128)S(1)}, f32[128,128]{1,0:T(8,128)S(1)}, u32[]{:S(2)}, u32[]{:S(2)}) collective-permute-start(f32[128,128]{1,0:T(8,128)S(1)} %get-tuple-element.63), channel_id=1, source_target_pairs={{2,4},{6,8},{10,12},{14,16},{18,20},{22,24},{26,28},{4,2},{8,6},{1... | collective-permute-start | bytes 196616 | tf_op jit(solution)/shard_map/ppermute | solution.py:62
  36.1 2.6 %collective-permute-start.8 = (f32[128,128]{1,0:T(8,128)S(1)}, f32[128,128]{1,0:T(8,128)S(1)}, u32[]{:S(2)}, u32[]{:S(2)}) collective-permute-start(f32[128,128]{1,0:T(8,128)S(1)} %get-tuple-element.64), channel_id=1, source_target_pairs={{0,1},{1,0},{2,3},{3,2},{4,5},{5,4},{6,7},{7,6},{8,9},{9,8},{10,11... | collective-permute-start | bytes 196616 | tf_op jit(solution)/shard_map/ppermute | solution.py:62
  60.7 4.3 %collective-permute-start.9 = (f32[128,128]{1,0:T(8,128)S(1)}, f32[128,128]{1,0:T(8,128)S(1)}, u32[]{:S(2)}, u32[]{:S(2)}) collective-permute-start(f32[128,128]{1,0:T(8,128)S(1)} %get-tuple-element.72), channel_id=1, source_target_pairs={{0,2},{4,6},{8,10},{12,14},{16,18},{20,22},{24,26},{28,30},{2,0},{... | collective-permute-start | bytes 196616 | tf_op jit(solution)/shard_map/ppermute | solution.py:62
  61.0 4.0 %collective-permute-start.10 = (f32[128,128]{1,0:T(8,128)S(1)}, f32[128,128]{1,0:T(8,128)S(1)}, u32[]{:S(2)}, u32[]{:S(2)}) collective-permute-start(f32[128,128]{1,0:T(8,128)S(1)} %get-tuple-element.73), channel_id=1, source_target_pairs={{2,4},{6,8},{10,12},{14,16},{18,20},{22,24},{26,28},{4,2},{8,6},{1... | collective-permute-start | bytes 196616 | tf_op jit(solution)/shard_map/ppermute | solution.py:62
  61.7 3.4 %collective-permute-start.11 = (f32[128,128]{1,0:T(8,128)S(1)}, f32[128,128]{1,0:T(8,128)S(1)}, u32[]{:S(2)}, u32[]{:S(2)}) collective-permute-start(f32[128,128]{1,0:T(8,128)S(1)} %get-tuple-element.74), channel_id=1, source_target_pairs={{0,1},{1,0},{2,3},{3,2},{4,5},{5,4},{6,7},{7,6},{8,9},{9,8},{10,11... | collective-permute-start | bytes 196616 | tf_op jit(solution)/shard_map/ppermute | solution.py:62
  81.4 10.8 %all-to-all-start.4 = ((f32[32,8,128]{2,1,0:T(8,128)}), f32[32,8,128]{2,1,0:T(8,128)S(1)}, u32[]{:S(2)}, u32[]{:S(2)}) async-start(f32[32,8,128]{2,1,0:T(8,128)} %shard_map.75), calls=%async_computation.4 | async-start | bytes 262144 | tf_op jit(solution)/shard_map/all_to_all | solution.py:486

commit v3 on v2

--- a/solution.py
+++ b/solution.py
@@ -19,6 +19,37 @@
         precision=precision,
         preferred_element_type=F32,
     )
+
+
+def thirds(value):
+    high = value.astype(BF16)
+    rest = value - high.astype(F32)
+    middle = rest.astype(BF16)
+    return high, middle, (rest - middle.astype(F32)).astype(BF16)
+
+
+def plain(left, right, left_dim=1, right_dim=0):
+    return lax.dot_general(
+        left, right, (((left_dim,), (right_dim,)), ((), ())), preferred_element_type=F32
+    )
+
+
+def deep_dot(left, right):
+    a, b, c = thirds(left)
+    p, q, r = thirds(right)
+    return plain(
+        jnp.concatenate([a, a, b, a, c, b], axis=1), jnp.concatenate([p, q, p, r, p, q], axis=0)
+    )
+
+
+def gram_dot(left, right):
+    a, b, c = thirds(left)
+    p, q, r = thirds(right)
+    cols = right.shape[1]
+    pair = jnp.concatenate([p, q], axis=1)
+    first, second = plain(a, pair, 0, 0), plain(b, pair, 0, 0)
+    small = second[:, cols:] + plain(a, r, 0, 0) + plain(c, p, 0, 0)
+    return first[:, :cols] + (first[:, cols:] + second[:, :cols] + small)
 
 
 def half_dot(left, right):
@@ -52,7 +83,7 @@
 def pair_rounds(size):
     first = [(i, i + 1) for i in range(0, size - 1, 2)]
     second = [(i, i + 1) for i in range(1, size - 1, 2)]
-    return [pairs + [(j, i) for i, j in pairs] for pairs in (first, second)]
+    return [pairs + [(j, i) for i, j in pairs] for pairs in (second, first)]
 
 
 def exchange(sends):
@@ -74,16 +105,16 @@
 def to_rounds(faces):
     ex, ey = even("gx"), even("gy")
     return [
+        jnp.where(ex, faces[0], faces[1]),
         jnp.where(ex, faces[1], faces[0]),
-        jnp.where(ex, faces[0], faces[1]),
+        jnp.where(ey, faces[2], faces[3]),
         jnp.where(ey, faces[3], faces[2]),
-        jnp.where(ey, faces[2], faces[3]),
     ]
 
 
 def to_faces(parts):
     ex, ey = even("gx"), even("gy")
-    a, b, c, d = parts
+    b, a, d, c = parts
 
     def choose(flag, yes, no):
         if yes is None and no is None:
@@ -137,7 +168,6 @@
     row_id = lax.broadcasted_iota(jnp.int32, (size, size), 0)
     col_id = lax.broadcasted_iota(jnp.int32, (size, size), 1)
     eye = (row_id == col_id).astype(F32)
-    matrix = 0.5 * (matrix + matrix.T)
     only = matrix * eye
     by_row = lax.rsqrt(jnp.sum(only, axis=1, keepdims=True))
     by_col = lax.rsqrt(jnp.sum(only, axis=0, keepdims=True))
@@ -148,15 +178,14 @@
     power = eye - scale * unit
 
     def step(answer, power):
-        both = dot(power, jnp.concatenate([answer, power], axis=1))
-        return answer + both[:, :size], both[:, size:]
+        return answer + deep_dot(power, answer), deep_dot(power, power)
 
     for k in range(squarings):
         answer, power = step(answer, power)
         if k < len(boosts):
             power = boosts[k] * power + (1.0 - boosts[k]) * eye
             answer = boosts[k] * answer
-    work_ref[:, 0:size] = answer + dot(power, answer)
+    work_ref[:, 0:size] = answer + deep_dot(power, answer)
     largest = jnp.max(jnp.abs(power))
 
     @pl.when(jnp.logical_not(largest < 3e-4))
@@ -216,12 +245,12 @@
 
     head = face + nco + nco * chunks
 
-    def send_loads(loads_hbm, basis_hbm, rows_hbm, loads_ref, basis_ref, rows_ref, *outs):
+    def send_loads(loads_hbm, basis_hbm, rows_hbm, map_hbm, loads_ref, basis_ref, rows_ref, map_ref, *outs):
         outs, raw_ref, sems = spread(outs[:-2]), outs[-2], outs[-1]
         fetches = [
             pltpu.make_async_copy(src, dst, sems.at[k])
             for k, (src, dst) in enumerate(
-                ((loads_hbm, raw_ref), (basis_hbm, basis_ref), (rows_hbm, rows_ref))
+                ((loads_hbm, raw_ref), (basis_hbm, basis_ref), (rows_hbm, rows_ref), (map_hbm, map_ref))
             )
         ]
         for fetch in fetches:
@@ -245,13 +274,14 @@
 
     outs = call(
         send_loads,
-        [(field, F32), (basis.shape, F32), (coarse_rows.shape, F32)] + [((head, cols), F32)] * nrounds,
+        [(field, F32), (basis.shape, F32), (coarse_rows.shape, F32), ((1, unknowns), jnp.int32)]
+        + [((head, cols), F32)] * nrounds,
         [(field, BF16)],
-        far=3,
-        copies=3,
-    )(loads, basis, coarse_rows)
-    loads, basis, coarse_rows = outs[:3]
-    got_a = trade(fill(outs[3:]))
+        far=4,
+        copies=4,
+    )(loads, basis, coarse_rows, slot_map.reshape(1, unknowns))
+    loads, basis, coarse_rows, slot_map = outs[:4]
+    got_a = trade(fill(outs[4:]))
 
     def reorder(first_hbm, second_hbm, map_ref, first_out, second_out, first_raw, second_raw, sems):
         fetches = [
@@ -278,41 +308,39 @@
         moved=8 * unknowns**2,
         far=2,
         copies=2,
-    )(local_inverse, schur, slot_map.reshape(1, unknowns))
+    )(local_inverse, schur, slot_map)
 
     def first_local(*refs):
         got = take(spread(refs[:nrounds]))
-        loads_ref, inverse_ref = refs[nrounds : nrounds + 2]
-        res_ref, scaled_ref, product_ref, part_ref = refs[nrounds + 2 : nrounds + 6]
-        sends = spread(refs[nrounds + 6 :])
+        loads_ref, inverse_ref, basis_ref = refs[nrounds : nrounds + 3]
+        res_ref, scaled_ref, product_ref, part_ref, ci_ref = refs[nrounds + 3 : nrounds + 8]
+        sends = spread(refs[nrounds + 8 :])
         weights = face_weights()
         residual = add_faces(loads_ref[...], [g if g is None else g[:face] for g in got])
         scaled = weighted(residual, weights)
         product = half_dot(inverse_ref[...], scaled.astype(BF16))
         part = weighted(product, weights)
         give(sends, split_faces(part))
+        coarse_input = dot(basis_ref[...], scaled)
+        ci_ref[...] = jnp.broadcast_to(coarse_input[None], ci_ref.shape)
         res_ref[...] = residual
         scaled_ref[...] = scaled
         product_ref[...] = product
         part_ref[...] = part
 
-    outs = call(first_local, [(field, F32)] * 4 + [face_out] * nrounds)(*got_a, loads, inverse_here)
-    residual, scaled, product, part = outs[:4]
-    got_b = trade(fill(outs[4:]))
-
-    def first_coarse(basis_ref, scaled_ref, ci_ref):
-        coarse_input = dot(basis_ref[...], scaled_ref[...])
-        ci_ref[...] = jnp.broadcast_to(coarse_input[None], ci_ref.shape)
-
-    (coarse_input,) = call(first_coarse, [((devices, nco, cols), F32)])(basis, scaled)
+    outs = call(
+        first_local, [(field, F32)] * 4 + [((devices, nco, cols), F32)] + [face_out] * nrounds
+    )(*got_a, loads, inverse_here, basis)
+    residual, scaled, product, part, coarse_input = outs[:5]
+    got_b = trade(fill(outs[5:]))
     coarse_all_in = lax.all_to_all(coarse_input, AXES, 0, 0).reshape(coarse_all, cols)
 
     def first_tables(*refs):
         got = take(spread(refs[:nrounds]))
         scaled_ref, product_ref, basis_ref, rows_ref = refs[nrounds : nrounds + 4]
-        gram_ref, bases_ref, table_ref, wide_ref = refs[nrounds + 4 :]
+        gram_ref, bases_ref, table_ref = refs[nrounds + 4 :]
         weights = face_weights()
-        gram_ref[...] = dot(scaled_ref[...], product_ref[...], 0, 0)
+        gram_ref[...] = gram_dot(scaled_ref[...], product_ref[...])
         basis_now = basis_ref[...]
         bases, tables = [], []
         for f in range(4):
@@ -335,20 +363,13 @@
                 ]
         bases_ref[...] = jnp.concatenate(bases, axis=0)
         table_ref[...] = jnp.concatenate(tables, axis=0)
-        src = lax.broadcasted_iota(jnp.int32, (cols, wide), 0)
-        dst = lax.broadcasted_iota(jnp.int32, (cols, wide), 1)
-        widen = (dst == src // nco * 8 + lax.rem(src, nco)).astype(F32)
-        for c in range(chunks):
-            wide_ref[:, wide * c : wide * (c + 1)] = dot(table_ref[:, cols * c : cols * (c + 1)], widen)
-
-    wide = cols // nco * 8
-    gram_part, bases, table, table_wide = call(
+
+    gram_part, bases, table = call(
         first_tables,
         [
             (gram_shape, F32),
             ((8 * nco, face), F32),
             ((8 * nco, coarse_all), F32),
-            ((8 * nco, wide * chunks), F32),
         ],
     )(*got_a, scaled, product, basis, coarse_rows)
 
@@ -358,14 +379,20 @@
             for f in range(4)
         ]
 
-    per = 8 * -(-2 * cols // (8 * devices))
-    blocks_out = ((devices, per, cols), F32)
+    mine = -(-cols // devices)
+    packers = cols // mine
+    packed = 8 * -(-(mine + 1) // 8)
+
+    def triangles():
+        row_id = lax.broadcasted_iota(jnp.int32, gram_shape, 0)
+        col_id = lax.broadcasted_iota(jnp.int32, gram_shape, 1)
+        return row_id < col_id, row_id == col_id
 
     def first_direction(*refs):
         got = take(spread(refs[:nrounds]))
-        part_ref, all_ref, bases_ref, table_ref, schur_ref = refs[nrounds : nrounds + 5]
-        dir_ref, image_ref, values_ref = refs[nrounds + 5 : nrounds + 8]
-        sends = spread(refs[nrounds + 8 :])
+        part_ref, all_ref, bases_ref, table_ref, schur_ref, mine_ref, gram_ref = refs[nrounds : nrounds + 7]
+        dir_ref, image_ref, values_ref, blocks_ref = refs[nrounds + 7 : nrounds + 11]
+        sends = spread(refs[nrounds + 11 :])
         values = dot(table_ref[...], all_ref[...])
         values_ref[...] = values
         coarse = coarse_part(bases_ref[...], values)
@@ -374,47 +401,59 @@
         image = half_dot(schur_ref[...], update.astype(BF16))
         image_ref[...] = image
         give(sends, split_faces(image))
+        first = gram_ref[...] + dot(mine_ref[0], values[:nco], 0, 0)
+        curvature = gram_dot(update, image)
+        above, on = triangles()
+        both = jnp.where(above, curvature + curvature.T, first + first.T) * 0.5
+        diagonal = jnp.sum(jnp.where(on, curvature, 0.0), axis=0, keepdims=True)
+        blocks_ref[:, mine : mine + 1, :] = jnp.broadcast_to(diagonal[None], (devices, 1, cols))
+        if packers < devices:
+            blocks_ref[:, 0:mine, :] = jnp.zeros((devices, mine, cols), F32)
+        if mine + 1 < packed:
+            blocks_ref[:, mine + 1 :, :] = jnp.zeros((devices, packed - mine - 1, cols), F32)
+        for k in range(packers):
+            blocks_ref[k, 0:mine, :] = both[mine * k : mine * (k + 1)]
 
     outs = call(
         first_direction,
-        [(field, F32), (field, F32), ((8 * nco, cols), F32)] + [face_out] * nrounds,
-    )(*got_b, part, coarse_all_in, bases, table, schur_here)
-    direction, image, values = outs[:3]
-    got_d = trade(fill(outs[3:]))
-
-    def first_grams(dir_ref, image_ref, values_ref, mine_ref, gram_ref, blocks_ref):
-        first = gram_ref[...] + dot(mine_ref[0], values_ref[0:nco], 0, 0)
-        curvature = dot(dir_ref[...], image_ref[...], 0, 0)
-        write_blocks(blocks_ref, jnp.concatenate([curvature, first], axis=0))
-
-    (blocks,) = call(first_grams, [blocks_out])(direction, image, values, coarse_input, gram_part)
+        [(field, F32), (field, F32), ((8 * nco, cols), F32), ((devices, packed, cols), F32)]
+        + [face_out] * nrounds,
+    )(*got_b, part, coarse_all_in, bases, table, schur_here, coarse_input, gram_part)
+    direction, image, values, blocks = outs[:4]
+    got_d = trade(fill(outs[4:]))
     blocks = lax.all_to_all(blocks, AXES, 0, 0)
+    joint = 8 * -(-(mine + nco) // 8)
 
     def first_sums(*refs):
         got = take(spread(refs[:nrounds]))
         image_ref, blocks_ref, basis_ref = refs[nrounds : nrounds + 3]
-        full_ref, sum_ref, mine_ref = refs[nrounds + 3 :]
+        full_ref, sum_ref, mine_ref, diag_ref = refs[nrounds + 3 :]
         image_vec = add_faces(image_ref[...], got)
         full_ref[...] = image_vec
         coarse_image = dot(basis_ref[...], weighted(image_vec, face_weights()))
         mine_ref[...] = coarse_image
-        block = jnp.concatenate(
-            [jnp.sum(blocks_ref[...], axis=0), coarse_image, jnp.zeros((8 - nco, cols), F32)], axis=0
-        )
-        sum_ref[...] = jnp.broadcast_to(block[None], sum_ref.shape)
-
-    image_vec, sums, coarse_image = call(
+        total = jnp.sum(blocks_ref[...], axis=0)
+        diag_ref[...] = total[mine : mine + 1]
+        rows = [total[0:mine], coarse_image]
+        if mine + nco < joint:
+            rows.append(jnp.zeros((joint - mine - nco, cols), F32))
+        sum_ref[...] = jnp.broadcast_to(jnp.concatenate(rows, axis=0)[None], sum_ref.shape)
+
+    image_vec, sums, coarse_image, diagonal = call(
         first_sums,
-        [(field, F32), ((devices, per + 8, cols), F32), ((nco, cols), F32)],
+        [(field, F32), ((devices, joint, cols), F32), ((nco, cols), F32), ((1, cols), F32)],
     )(*got_d, image, blocks, basis)
     sums = lax.all_to_all(sums, AXES, 0, 0)
 
-    def second_local(sums_ref, res_ref, full_ref, inverse_ref, *outs):
+    def second_local(sums_ref, diag_ref, res_ref, full_ref, inverse_ref, *outs):
         outs, work_ref = outs[:-1], outs[-1]
         curv_ref, first_ref, step_ref, scaled_ref, product_ref, part_ref = outs[:6]
         sends = spread(outs[6:])
-        both = sums_ref[:, 0:per, :].reshape(devices * per, cols)
-        curvature, first = both[:cols], both[cols : 2 * cols]
+        both = jnp.concatenate([sums_ref[k, 0:mine, :] for k in range(packers)], axis=0)
+        turned = both.T
+        above, on = triangles()
+        curvature = jnp.where(above, both, jnp.where(on, diag_ref[...], turned))
+        first = jnp.where(above, turned, both)
         step = solve(curvature, first, work_ref, (), 5)
         weights = face_weights()
         residual = res_ref[...] - dot(full_ref[...], step)
@@ -433,24 +472,34 @@
         second_local,
         [(gram_shape, F32)] * 3 + [(field, F32)] * 3 + [face_out] * nrounds,
         work,
-    )(sums, residual, image_vec, inverse_here)
+    )(sums, diagonal, residual, image_vec, inverse_here)
     curvature, first, step, scaled, product, part = outs[:6]
     got_e = trade(fill(outs[6:]))
 
     def second_coarse(
         sums_ref, table_ref, values_ref, mine_ref, image_ref, step_ref, scaled_ref, product_ref,
-        next_ref, values_out
+        first_ref, curv_ref, next_ref, values_out, inv_ref, quad_ref, work_ref
     ):
-        rows = sums_ref[:, per : per + 8, :].reshape(devices * 8, cols)
+        rows = jnp.concatenate([sums_ref[k, mine : mine + nco, :] for k in range(devices)], axis=0)
         step = step_ref[...]
         values_now = values_ref[...] - dot(dot(table_ref[...], rows), step)
         values_out[...] = values_now
         own = mine_ref[0] - dot(image_ref[...], step)
-        next_ref[...] = dot(scaled_ref[...], product_ref[...], 0, 0) + dot(own, values_now[:nco], 0, 0)
-
-    next_part, values = call(
-        second_coarse, [(gram_shape, F32), ((8 * nco, cols), F32)], flops=2 * 12 * unknowns * cols**2
-    )(sums, table_wide, values, coarse_input, coarse_image, step, scaled, product)
+        next_ref[...] = gram_dot(scaled_ref[...], product_ref[...]) + dot(own, values_now[:nco], 0, 0)
+        _, on = triangles()
+        inverse = solve(first_ref[...], on.astype(F32), work_ref, (), 4)
+        inv_ref[...] = inverse
+        quad_ref[...] = gram_dot(inverse, deep_dot(curv_ref[...], inverse))
+
+    next_part, values, first_inverse, quad = call(
+        second_coarse,
+        [(gram_shape, F32), ((8 * nco, cols), F32), (gram_shape, F32), (gram_shape, F32)],
+        work,
+        flops=2 * 12 * unknowns * cols**2,
+    )(sums, table, values, coarse_input, coarse_image, step, scaled, product, first, curvature)
+
+    per = 8 * -(-2 * cols // (8 * devices))
+    blocks_out = ((devices, per, cols), F32)
 
     def second_direction(*refs):
         got = take(spread(refs[:nrounds]))
@@ -463,7 +512,7 @@
         low = (update - high.astype(F32)).astype(BF16)
         both = half_dot(schur_ref[...], jnp.concatenate([high, low], axis=1))
         product = both[:, :cols] + both[:, cols:]
-        square = dot(update, product, 0, 0)
+        square = gram_dot(update, product)
         write_blocks(blocks_ref, jnp.concatenate([next_ref[...], square], axis=0))
 
     update, blocks = call(second_direction, [(field, F32), blocks_out])(
@@ -471,30 +520,29 @@
     )
     blocks = lax.all_to_all(blocks, AXES, 0, 0)
 
-    def invert(first_ref, out_ref, work_ref):
-        size = first_ref.shape[0]
-        row_id = lax.broadcasted_iota(jnp.int32, (size, size), 0)
-        col_id = lax.broadcasted_iota(jnp.int32, (size, size), 1)
-        out_ref[...] = solve(first_ref[...], (row_id == col_id).astype(F32), work_ref, (), 5)
-
-    (first_inverse,) = call(invert, [(gram_shape, F32)], work, flops=2 * 60 * cols**3)(first)
-
-    def second_sums(blocks_ref, out_ref):
-        out_ref[...] = jnp.broadcast_to(jnp.sum(blocks_ref[...], axis=0)[None], out_ref.shape)
-
-    (sums,) = call(second_sums, [blocks_out])(blocks)
+    def second_sums(blocks_ref, out_ref, keep_ref):
+        total = jnp.sum(blocks_ref[...], axis=0)
+        out_ref[...] = jnp.broadcast_to(total[None], out_ref.shape)
+        keep_ref[...] = total
+
+    sums, _ = call(second_sums, [blocks_out, ((per, cols), F32)])(blocks)
     sums = lax.all_to_all(sums, AXES, 0, 0).reshape(devices * per, cols)
 
-    def finish(sums_ref, first_ref, curv_ref, step_ref, dir_ref, update_ref, out_ref, work_ref):
+    def finish(sums_ref, inv_ref, quad_ref, step_ref, dir_ref, update_ref, out_ref, work_ref):
         next_gram, square = sums_ref[0:cols], sums_ref[cols : 2 * cols]
-        ratio = dot(first_ref[...], next_gram)
-        curvature = square - dot(ratio, dot(curv_ref[...], ratio), 0, 0)
+        curvature = square - gram_dot(next_gram, deep_dot(quad_ref[...], next_gram))
+        curvature = 0.5 * (curvature + curvature.T)
+        ratio = deep_dot(inv_ref[...], next_gram)
         step = solve(curvature, next_gram, work_ref, (1.8, 1.8, 1.5), 7)
-        total = step_ref[...] + dot(ratio, step)
-        out_ref[...] = dot(dir_ref[...], total) + dot(update_ref[...], step)
+        total = step_ref[...] + deep_dot(ratio, step)
+        fields = jnp.concatenate([dir_ref[...], update_ref[...]], axis=1)
+        coefs = jnp.concatenate([total, step], axis=0)
+        a, b, _ = thirds(fields)
+        p, q, _ = thirds(coefs)
+        out_ref[...] = plain(a, p) + (plain(a, q) + plain(b, p))
 
     (solved,) = call(finish, [(field, F32)], work)(
-        sums, first_inverse, curvature, step, direction, update
+        sums, first_inverse, quad, step, direction, update
     )
     return solved[None, None]
 

time: 98 us -> 90.9 us (0.928)
  waiting for transfers between devices: 17.5 us -> 8.1 us
  starting transfers between devices: 26.9 us -> 30.2 us
  blocking collectives: 30.2 us -> 33.3 us
  Pallas kernels: 21.6 us -> 18.7 us
    ppermute x12, starting transfers between devices: 10.2 us -> 20.9 us  [exchange(): got.append(lax.ppermute(piece, axis, pairs) if pairs else None)]
    all_to_all x0 -> x1, blocking collectives: none -> 9.99 us  [local(): sums = lax.all_to_all(sums, AXES, 0, 0).reshape(devices * per, cols)]
    all_to_all x1 -> x0, waiting for transfers between devices: 6.13 us -> none  [local(): sums = lax.all_to_all(sums, AXES, 0, 0).reshape(devices * per, cols)]
    all_to_all x1, blocking collectives: 15.7 us -> 12.2 us  [local(): sums = lax.all_to_all(sums, AXES, 0, 0)]
    all_to_all x1, blocking collectives: 14.5 us -> 11.1 us  [local(): blocks = lax.all_to_all(blocks, AXES, 0, 0)]
    all_to_all x1, starting transfers between devices: 8.06 us -> 4.84 us  [local(): lax.all_to_all(coarse_input, AXES, 0, 0).reshape(coarse_all, cols)]
    all_to_all x1, waiting for transfers between devices: 3.17 us -> 0.01 us  [local(): blocks = lax.all_to_all(blocks, AXES, 0, 0)]
    pallas_call x14 -> x11, Pallas kernels: 21.6 us -> 18.7 us  [run(): return kernel_call(body, outs, scratch, flops, moved, sems, specs)(*args)]
  transfers between devices with their start and end apart: 15 -> 14, of which waited for: 6 -> 4; matrix products, arithmetic and copies ran while one was open for 0% -> 0% of each run, Pallas kernels for 7% -> 6%
where the time goes in v3:
time: 90.9 us; the launch traced here: 90.4 us
  blocking collectives  33.3 us (37%)
  starting transfers between devices  30.2 us (33%)
  Pallas kernels  18.7 us (21%)
  waiting for transfers between devices  8.1 us (9%)
    ppermute x12, starting transfers between devices, exchange(): got.append(lax.ppermute(piece, axis, pairs) if pairs else None)  20.9 us
    pallas_call x11, Pallas kernels, run(): return kernel_call(body, outs, scratch, flops, moved, sems, specs)(*args)  18.7 us
    all_to_all x1, blocking collectives, local(): sums = lax.all_to_all(sums, AXES, 0, 0)  12.2 us
    all_to_all x1, blocking collectives, local(): blocks = lax.all_to_all(blocks, AXES, 0, 0)  11.1 us
    all_to_all x1, blocking collectives, local(): sums = lax.all_to_all(sums, AXES, 0, 0).reshape(devices * per, cols)  9.99 us
    ppermute x12, waiting for transfers between devices, exchange(): got.append(lax.ppermute(piece, axis, pairs) if pairs else None)  8.09 us
    all_to_all x1, starting transfers between devices, local(): lax.all_to_all(coarse_input, AXES, 0, 0).reshape(coarse_all, cols)  4.84 us
    all_to_all x1, starting transfers between devices, local(): blocks = lax.all_to_all(blocks, AXES, 0, 0)  4.46 us
  transfers between devices with their start and end apart: 14, of which 4 were waited for; matrix products, arithmetic and copies ran while one was open for 0% of the time, Pallas kernels for 6%

profile of v3, /device:TPU:0, one launch (start us, length us, event | category | flops | bytes accessed | tf_op | source)
XLA Modules:
  0.0 90.4 jit_solution(3242888791615172593)
XLA Ops:
  0.0 1.0 %shard_map.64 = (f32[512,128]{1,0:T(8,128)S(1)}, f32[4,512]{1,0:T(4,128)S(1)}, f32[4,128]{1,0:T(4,128)S(1)}, s32[1,512]{1,0:T(1,128)S(1)}, f32[136,128]{1,0:T(8,...) custom-call(bf16[512,128]{1,0:T(8,128)(2,1)} %bitcast.11, f32[4,512]{1,0:T(4,128)} %bitcast.12, ...), custom_call_target="tpu_custom_call" | custom-call | tf_op jit(solution)/shard_map/pallas_call | solution.py:67
  1.0 0.7 collective-permute-start
  1.7 5.7 %collective-permute-start.1 = (f32[136,128]{1,0:T(8,128)S(1)}, f32[136,128]{1,0:T(8,128)S(1)}, u32[]{:S(2)}, u32[]{:S(2)}) collective-permute-start(f32[136,128]{1,0:T(8,128)S(1)} %get-tuple-element.53), channel_id=1, source_target_pairs={{0,2},{4,6},{8,10},{12,14},{16,18},{20,22},{24,26},{28,30},{2,0},{... | collective-permute-start | bytes 208904 | tf_op jit(solution)/shard_map/ppermute | solution.py:93
  7.4 0.0 collective-permute-start.2
  7.4 2.5 %shard_map.65 = (bf16[512,512]{1,0:T(8,128)(2,1)S(1)}, bf16[512,512]{1,0:T(8,128)(2,1)S(1)}) custom-call(bf16[512,512]{1,0:T(8,128)(2,1)} %bitcast.15, bf16[512,512]{1,0:T(8,128)(2,1)} %bitcast.16, s32[1,512]{1,0:T(1,128)S(1)} %get-tuple-element.56.map_ref), custom_call_target="tpu_custom_call" | custom-call | flops 1073741824 | bytes 2097152 | tf_op jit(solution)/shard_map/pallas_call | solution.py:67
  9.9 0.0 collective-permute-done.refs_0_
  9.9 0.8 collective-permute-done.1.refs_1_
  10.7 0.0 collective-permute-done.2.refs_2_
  10.7 1.0 %shard_map.66 = (f32[512,128]{1,0:T(8,128)S(1)}, f32[512,128]{1,0:T(8,128)S(1)}, f32[512,128]{1,0:T(8,128)S(1)}, f32[512,128]{1,0:T(8,128)S(1)}, f32[32,4,128]{2...) custom-call(f32[136,128]{1,0:T(8,128)S(1)} %collective-permute-done.refs_0_, ...), custom_call_target="tpu_custom_call" | custom-call | tf_op jit(solution)/shard_map/pallas_call | solution.py:67
  11.7 4.8 %all-to-all-start = ((f32[32,4,128]{2,1,0:T(4,128)}), f32[32,4,128]{2,1,0:T(4,128)S(1)}, u32[]{:S(2)}, u32[]{:S(2)}) async-start(f32[32,4,128]{2,1,0:T(4,128)} %get-tuple-element.63.refs_8_.mine_ref), calls=%async_computation | async-start | bytes 131072 | tf_op jit(solution)/shard_map/all_to_all | solution.py:336
  16.6 0.7 collective-permute-start.3
  17.3 4.5 %collective-permute-start.4 = (f32[128,128]{1,0:T(8,128)S(1)}, f32[128,128]{1,0:T(8,128)S(1)}, u32[]{:S(2)}, u32[]{:S(2)}) collective-permute-start(f32[128,128]{1,0:T(8,128)S(1)} %get-tuple-element.60), channel_id=1, source_target_pairs={{0,2},{4,6},{8,10},{12,14},{16,18},{20,22},{24,26},{28,30},{2,0},{... | collective-permute-start | bytes 196616 | tf_op jit(solution)/shard_map/ppermute | solution.py:93
  21.8 0.0 collective-permute-start.5
  21.8 0.3 shard_map.67
  22.2 0.0 collective-permute-done.3.refs_0_
  22.2 3.2 %collective-permute-done.4.refs_1_ = f32[128,128]{1,0:T(8,128)S(1)} collective-permute-done((f32[128,128]{1,0:T(8,128)S(1)}, f32[128,128]{1,0:T(8,128)S(1)}, u32[]{:S(2)}, u32[]{:S(2)}) %collective-permute-start.4) | collective-permute-done | bytes 65568 | tf_op jit(solution)/shard_map/ppermute | solution.py:93
  25.4 0.0 collective-permute-done.5.refs_2_
  25.4 0.0 all-to-all-done
  25.4 2.8 %shard_map.68 = (f32[512,128]{1,0:T(8,128)S(1)}, f32[512,128]{1,0:T(8,128)S(1)}, f32[32,128]{1,0:T(8,128)S(1)}, f32[32,8,128]{2,1,0:T(8,128)}, f32[128,128]{1,0:...) custom-call(f32[128,128]{1,0:T(8,128)S(1)} %collective-permute-done.3.refs_0_, ...), custom_call_target="tpu_custom_call" | custom-call | tf_op jit(solution)/shard_map/pallas_call | solution.py:67
  28.2 4.5 %all-to-all-start.1 = ((f32[32,8,128]{2,1,0:T(8,128)}), f32[32,8,128]{2,1,0:T(8,128)S(1)}, u32[]{:S(2)}, u32[]{:S(2)}) async-start(f32[32,8,128]{2,1,0:T(8,128)} %get-tuple-element.75), calls=%async_computation.1 | async-start | bytes 262144 | tf_op jit(solution)/shard_map/all_to_all | solution.py:424
  32.7 0.7 collective-permute-start.6
  33.3 4.5 %collective-permute-start.7 = (f32[128,128]{1,0:T(8,128)S(1)}, f32[128,128]{1,0:T(8,128)S(1)}, u32[]{:S(2)}, u32[]{:S(2)}) collective-permute-start(f32[128,128]{1,0:T(8,128)S(1)} %get-tuple-element.72), channel_id=1, source_target_pairs={{0,2},{4,6},{8,10},{12,14},{16,18},{20,22},{24,26},{28,30},{2,0},{... | collective-permute-start | bytes 196616 | tf_op jit(solution)/shard_map/ppermute | solution.py:93
  37.9 0.0 collective-permute-start.8
  37.9 0.0 collective-permute-done.6.refs_0_
  37.9 3.8 %collective-permute-done.7.refs_1_ = f32[128,128]{1,0:T(8,128)S(1)} collective-permute-done((f32[128,128]{1,0:T(8,128)S(1)}, f32[128,128]{1,0:T(8,128)S(1)}, u32[]{:S(2)}, u32[]{:S(2)}) %collective-permute-start.7) | collective-permute-done | bytes 65568 | tf_op jit(solution)/shard_map/ppermute | solution.py:93
  41.7 0.0 collective-permute-done.8.refs_2_
  41.7 0.0 all-to-all-done.1.refs_4_
  41.7 0.3 shard_map.69
  42.0 12.2 %all_to_all.25.sums_ref = f32[32,8,128]{2,1,0:T(8,128)S(1)} all-to-all(f32[32,8,128]{2,1,0:T(8,128)S(1)} %get-tuple-element.76), channel_id=1, replica_groups=mesh['gx'=16,'gy'=2] {'gx','gy'}, dimensions={0} | all-to-all | bytes 262144 | tf_op jit(solution)/shard_map/all_to_all | solution.py:446
  54.2 2.4 %shard_map.70 = (f32[128,128]{1,0:T(8,128)S(1)}, f32[128,128]{1,0:T(8,128)S(1)}, f32[128,128]{1,0:T(8,128)S(1)}, f32[512,128]{1,0:T(8,128)S(1)}, f32[512,128]{1,...) custom-call(f32[32,8,128]{2,1,0:T(8,128)S(1)} %all_to_all.25.sums_re, ...), custom_call_target="tpu_custom_call" | custom-call | tf_op jit(solution)/shard_map/pallas_call | solution.py:67
  56.6 0.7 collective-permute-start.9
  57.3 3.4 %collective-permute-start.10 = (f32[128,128]{1,0:T(8,128)S(1)}, f32[128,128]{1,0:T(8,128)S(1)}, u32[]{:S(2)}, u32[]{:S(2)}) collective-permute-start(f32[128,128]{1,0:T(8,128)S(1)} %get-tuple-element.81), channel_id=1, source_target_pairs={{0,2},{4,6},{8,10},{12,14},{16,18},{20,22},{24,26},{28,30},{2,0},{... | collective-permute-start | bytes 196616 | tf_op jit(solution)/shard_map/ppermute | solution.py:93
  60.7 0.0 collective-permute-start.11
  60.8 2.9 %shard_map.71 = (f32[128,128]{1,0:T(8,128)S(1)}, f32[32,128]{1,0:T(8,128)S(1)}, f32[128,128]{1,0:T(8,128)S(1)}, f32[128,128]{1,0:T(8,128)S(1)}) custom-call(f32[32,8,128]{2,1,0:T(8,128)S(1)} %all_to_all.25.sums_ref, f32[32,128]{1,0:T(8,128)S(1)} %get-tuple-element.68.refs_6_.table_ref, f32[32,128]{1,0:T(8,128)S(1)} %get-tuple-element.84.values_ref, ...), custom_call_target="tpu_custom_call" | custom-call | flops 201326592 | tf_op jit(solution)/shard_map/pallas_call | solution.py:67
  63.7 0.0 collective-permute-done.9.refs_0_
  63.7 0.3 collective-permute-done.10.refs_1_
  63.9 0.0 collective-permute-done.11.refs_2_
  63.9 1.1 %shard_map.72 = (f32[512,128]{1,0:T(8,128)S(1)}, f32[32,8,128]{2,1,0:T(8,128)S(1)}) custom-call(f32[128,128]{1,0:T(8,128)S(1)} %collective-permute-done.9.refs_0_, f32[128,128]{1,0:T(8,128)S(1)} %collective-permute-done.10.refs_1_, f32[128,128]{1,0:T(8,128)S(1)} %collective-permute-done.11.refs_2_, f32[512,128]{1,0:T(8,128)S(1)} %get-tuple-element.83.refs_3_, ...), custom_call_target="tpu_custom_call" | custom-call | tf_op jit(solution)/shard_map/pallas_call | solution.py:67
  65.0 11.1 %all_to_all.26.blocks_ref = f32[32,8,128]{2,1,0:T(8,128)S(1)} all-to-all(f32[32,8,128]{2,1,0:T(8,128)S(1)} %get-tuple-element.93), channel_id=1, replica_groups=mesh['gx'=16,'gy'=2] {'gx','gy'}, dimensions={0} | all-to-all | bytes 262144 | tf_op jit(solution)/shard_map/all_to_all | solution.py:521
  76.1 0.6 shard_map.73
  76.7 10.0 %all_to_all.27 = f32[32,8,128]{2,1,0:T(8,128)S(1)} all-to-all(f32[32,8,128]{2,1,0:T(8,128)S(1)} %get-tuple-element.94), channel_id=1, replica_groups=mesh['gx'=16,'gy'=2] {'gx','gy'}, dimensions={0} | all-to-all | bytes 262144 | tf_op jit(solution)/shard_map/all_to_all | solution.py:529
  86.7 3.7 %shard_map.74 = f32[512,128]{1,0:T(8,128)} custom-call(f32[256,128]{1,0:T(8,128)S(1)} %bitcast.9, f32[128,128]{1,0:T(8,128)S(1)} %get-tuple-element.95.inv_ref, f32[128,128]{1,0:T(8,128)S(1)} %get-tuple-element.96.quad_ref, f32[128,128]{1,0:T(8,128)S(1)} %get-tuple-element.86.step_ref, f32[512,128]{1,0:T(8,128)S(1)} %get-tuple-element.97.dir_ref, ...), custom_call_target="tpu_custom_call" | custom-call | tf_op jit(solution)/shard_map/pallas_call | solution.py:67
Async XLA Ops:
  1.0 8.9 %collective-permute-start = (f32[136,128]{1,0:T(8,128)S(1)}, f32[136,128]{1,0:T(8,128)S(1)}, u32[]{:S(2)}, u32[]{:S(2)}) collective-permute-start(f32[136,128]{1,0:T(8,128)S(1)} %get-tuple-element.52), channel_id=1, source_target_pairs={{2,4},{6,8},{10,12},{14,16},{18,20},{22,24},{26,28},{4,2},{8,6},{1... | collective-permute-start | bytes 208904 | tf_op jit(solution)/shard_map/ppermute | solution.py:93
  1.7 9.0 %collective-permute-start.1 = (f32[136,128]{1,0:T(8,128)S(1)}, f32[136,128]{1,0:T(8,128)S(1)}, u32[]{:S(2)}, u32[]{:S(2)}) collective-permute-start(f32[136,128]{1,0:T(8,128)S(1)} %get-tuple-element.53), channel_id=1, source_target_pairs={{0,2},{4,6},{8,10},{12,14},{16,18},{20,22},{24,26},{28,30},{2,0},{... | collective-permute-start | bytes 208904 | tf_op jit(solution)/shard_map/ppermute | solution.py:93
  7.4 3.3 %collective-permute-start.2 = (f32[136,128]{1,0:T(8,128)S(1)}, f32[136,128]{1,0:T(8,128)S(1)}, u32[]{:S(2)}, u32[]{:S(2)}) collective-permute-start(f32[136,128]{1,0:T(8,128)S(1)} %get-tuple-element.54), channel_id=1, source_target_pairs={{0,1},{1,0},{2,3},{3,2},{4,5},{5,4},{6,7},{7,6},{8,9},{9,8},{10,11... | collective-permute-start | bytes 208904 | tf_op jit(solution)/shard_map/ppermute | solution.py:93
  11.7 13.6 %all-to-all-start = ((f32[32,4,128]{2,1,0:T(4,128)}), f32[32,4,128]{2,1,0:T(4,128)S(1)}, u32[]{:S(2)}, u32[]{:S(2)}) async-start(f32[32,4,128]{2,1,0:T(4,128)} %get-tuple-element.63.refs_8_.mine_ref), calls=%async_computation | async-start | bytes 131072 | tf_op jit(solution)/shard_map/all_to_all | solution.py:336
  16.6 5.6 %collective-permute-start.3 = (f32[128,128]{1,0:T(8,128)S(1)}, f32[128,128]{1,0:T(8,128)S(1)}, u32[]{:S(2)}, u32[]{:S(2)}) collective-permute-start(f32[128,128]{1,0:T(8,128)S(1)} %get-tuple-element.59), channel_id=1, source_target_pairs={{2,4},{6,8},{10,12},{14,16},{18,20},{22,24},{26,28},{4,2},{8,6},{1... | collective-permute-start | bytes 196616 | tf_op jit(solution)/shard_map/ppermute | solution.py:93
  17.3 8.1 %collective-permute-start.4 = (f32[128,128]{1,0:T(8,128)S(1)}, f32[128,128]{1,0:T(8,128)S(1)}, u32[]{:S(2)}, u32[]{:S(2)}) collective-permute-start(f32[128,128]{1,0:T(8,128)S(1)} %get-tuple-element.60), channel_id=1, source_target_pairs={{0,2},{4,6},{8,10},{12,14},{16,18},{20,22},{24,26},{28,30},{2,0},{... | collective-permute-start | bytes 196616 | tf_op jit(solution)/shard_map/ppermute | solution.py:93
  21.8 3.6 %collective-permute-start.5 = (f32[128,128]{1,0:T(8,128)S(1)}, f32[128,128]{1,0:T(8,128)S(1)}, u32[]{:S(2)}, u32[]{:S(2)}) collective-permute-start(f32[128,128]{1,0:T(8,128)S(1)} %get-tuple-element.61), channel_id=1, source_target_pairs={{0,1},{1,0},{2,3},{3,2},{4,5},{5,4},{6,7},{7,6},{8,9},{9,8},{10,11... | collective-permute-start | bytes 196616 | tf_op jit(solution)/shard_map/ppermute | solution.py:93
  28.2 13.5 %all-to-all-start.1 = ((f32[32,8,128]{2,1,0:T(8,128)}), f32[32,8,128]{2,1,0:T(8,128)S(1)}, u32[]{:S(2)}, u32[]{:S(2)}) async-start(f32[32,8,128]{2,1,0:T(8,128)} %get-tuple-element.75), calls=%async_computation.1 | async-start | bytes 262144 | tf_op jit(solution)/shard_map/all_to_all | solution.py:424
  32.7 5.2 %collective-permute-start.6 = (f32[128,128]{1,0:T(8,128)S(1)}, f32[128,128]{1,0:T(8,128)S(1)}, u32[]{:S(2)}, u32[]{:S(2)}) collective-permute-start(f32[128,128]{1,0:T(8,128)S(1)} %get-tuple-element.71), channel_id=1, source_target_pairs={{2,4},{6,8},{10,12},{14,16},{18,20},{22,24},{26,28},{4,2},{8,6},{1... | collective-permute-start | bytes 196616 | tf_op jit(solution)/shard_map/ppermute | solution.py:93
  33.3 8.4 %collective-permute-start.7 = (f32[128,128]{1,0:T(8,128)S(1)}, f32[128,128]{1,0:T(8,128)S(1)}, u32[]{:S(2)}, u32[]{:S(2)}) collective-permute-start(f32[128,128]{1,0:T(8,128)S(1)} %get-tuple-element.72), channel_id=1, source_target_pairs={{0,2},{4,6},{8,10},{12,14},{16,18},{20,22},{24,26},{28,30},{2,0},{... | collective-permute-start | bytes 196616 | tf_op jit(solution)/shard_map/ppermute | solution.py:93
  37.9 3.8 %collective-permute-start.8 = (f32[128,128]{1,0:T(8,128)S(1)}, f32[128,128]{1,0:T(8,128)S(1)}, u32[]{:S(2)}, u32[]{:S(2)}) collective-permute-start(f32[128,128]{1,0:T(8,128)S(1)} %get-tuple-element.73), channel_id=1, source_target_pairs={{0,1},{1,0},{2,3},{3,2},{4,5},{5,4},{6,7},{7,6},{8,9},{9,8},{10,11... | collective-permute-start | bytes 196616 | tf_op jit(solution)/shard_map/ppermute | solution.py:93
  56.6 7.0 %collective-permute-start.9 = (f32[128,128]{1,0:T(8,128)S(1)}, f32[128,128]{1,0:T(8,128)S(1)}, u32[]{:S(2)}, u32[]{:S(2)}) collective-permute-start(f32[128,128]{1,0:T(8,128)S(1)} %get-tuple-element.80), channel_id=1, source_target_pairs={{2,4},{6,8},{10,12},{14,16},{18,20},{22,24},{26,28},{4,2},{8,6},{1... | collective-permute-start | bytes 196616 | tf_op jit(solution)/shard_map/ppermute | solution.py:93
  57.3 6.6 %collective-permute-start.10 = (f32[128,128]{1,0:T(8,128)S(1)}, f32[128,128]{1,0:T(8,128)S(1)}, u32[]{:S(2)}, u32[]{:S(2)}) collective-permute-start(f32[128,128]{1,0:T(8,128)S(1)} %get-tuple-element.81), channel_id=1, source_target_pairs={{0,2},{4,6},{8,10},{12,14},{16,18},{20,22},{24,26},{28,30},{2,0},{... | collective-permute-start | bytes 196616 | tf_op jit(solution)/shard_map/ppermute | solution.py:93
  60.7 3.2 %collective-permute-start.11 = (f32[128,128]{1,0:T(8,128)S(1)}, f32[128,128]{1,0:T(8,128)S(1)}, u32[]{:S(2)}, u32[]{:S(2)}) collective-permute-start(f32[128,128]{1,0:T(8,128)S(1)} %get-tuple-element.82), channel_id=1, source_target_pairs={{0,1},{1,0},{2,3},{3,2},{4,5},{5,4},{6,7},{7,6},{8,9},{9,8},{10,11... | collective-permute-start | bytes 196616 | tf_op jit(solution)/shard_map/ppermute | solution.py:93

commit v4 on v3

--- a/solution.py
+++ b/solution.py
@@ -43,13 +43,17 @@
 
 
 def gram_dot(left, right):
-    a, b, c = thirds(left)
-    p, q, r = thirds(right)
+    a, b, _ = thirds(left)
+    p, q, _ = thirds(right)
     cols = right.shape[1]
-    pair = jnp.concatenate([p, q], axis=1)
-    first, second = plain(a, pair, 0, 0), plain(b, pair, 0, 0)
-    small = second[:, cols:] + plain(a, r, 0, 0) + plain(c, p, 0, 0)
-    return first[:, :cols] + (first[:, cols:] + second[:, :cols] + small)
+    pair = plain(a, jnp.concatenate([p, q], axis=1), 0, 0)
+    return pair[:, :cols] + (pair[:, cols:] + plain(b, p, 0, 0))
+
+
+def flat_dot(left, right):
+    a, b, _ = thirds(left)
+    p, q, _ = thirds(right)
+    return plain(jnp.concatenate([a, a, b], axis=1), jnp.concatenate([p, q, p], axis=0))
 
 
 def half_dot(left, right):
@@ -58,21 +62,23 @@
     )
 
 
-def call(body, outs, scratch=(), flops=0, moved=0, far=0, copies=0):
+def call(body, outs, scratch=(), flops=0, moved=0, far=0, copies=0, far_out=False):
     sems = [pltpu.SemaphoreType.DMA((copies,))] if copies else []
 
     def run(*args):
         specs = [pl.BlockSpec(memory_space=pltpu.HBM if i < far else pltpu.VMEM) for i in range(len(args))]
         args = [pltpu.with_memory_space_constraint(a, pltpu.HBM) if i < far else a for i, a in enumerate(args)]
-        return kernel_call(body, outs, scratch, flops, moved, sems, specs)(*args)
+        results = [pl.BlockSpec(memory_space=pltpu.HBM if far_out else pltpu.VMEM) for _ in outs]
+        return kernel_call(body, outs, scratch, flops, moved, sems, specs, results)(*args)
 
     return run
 
 
-def kernel_call(body, outs, scratch, flops, moved, sems, specs):
+def kernel_call(body, outs, scratch, flops, moved, sems, specs, results):
     return pl.pallas_call(
         body,
         in_specs=specs,
+        out_specs=results,
         scratch_shapes=[pltpu.VMEM(shape, kind) for shape, kind in scratch] + sems,
         out_shape=[jax.ShapeDtypeStruct(shape, kind) for shape, kind in outs],
         compiler_params=pltpu.CompilerParams(vmem_limit_bytes=48 * 1024 * 1024),
@@ -177,11 +183,11 @@
     answer = right * (by_row * scale)
     power = eye - scale * unit
 
-    def step(answer, power):
-        return answer + deep_dot(power, answer), deep_dot(power, power)
+    def step(answer, power, product=deep_dot):
+        return answer + product(power, answer), product(power, power)
 
     for k in range(squarings):
-        answer, power = step(answer, power)
+        answer, power = step(answer, power, flat_dot if boosts and k > 1 else deep_dot)
         if k < len(boosts):
             power = boosts[k] * power + (1.0 - boosts[k]) * eye
             answer = boosts[k] * answer
@@ -283,6 +289,8 @@
     loads, basis, coarse_rows, slot_map = outs[:4]
     got_a = trade(fill(outs[4:]))
 
+    square = (unknowns, unknowns)
+
     def reorder(first_hbm, second_hbm, map_ref, first_out, second_out, first_raw, second_raw, sems):
         fetches = [
             pltpu.make_async_copy(src, dst, sems.at[k])
@@ -290,16 +298,13 @@
         ]
         for fetch in fetches:
             fetch.start()
-        slots = lax.broadcasted_iota(jnp.int32, (unknowns, unknowns), 0)
+        slots = lax.broadcasted_iota(jnp.int32, square, 0)
         pick = (slots == map_ref[...]).astype(F32).astype(BF16)
         for fetch, ref, out in zip(fetches, (first_raw, second_raw), (first_out, second_out)):
             fetch.wait()
             rows = half_dot(pick, ref[...]).astype(BF16)
-            out[...] = lax.dot_general(
-                rows, pick, (((1,), (1,)), ((), ())), preferred_element_type=F32
-            ).astype(BF16)
-
-    square = (unknowns, unknowns)
+            out[...] = plain(rows, pick, 1, 1).astype(BF16)
+
     inverse_here, schur_here = call(
         reorder,
         [(square, BF16)] * 2,
@@ -338,19 +343,19 @@
     def first_tables(*refs):
         got = take(spread(refs[:nrounds]))
         scaled_ref, product_ref, basis_ref, rows_ref = refs[nrounds : nrounds + 4]
-        gram_ref, bases_ref, table_ref = refs[nrounds + 4 :]
+        gram_ref, bases_ref, deep_ref, table_ref = refs[nrounds + 4 :]
         weights = face_weights()
         gram_ref[...] = gram_dot(scaled_ref[...], product_ref[...])
         basis_now = basis_ref[...]
         bases, tables = [], []
         for f in range(4):
-            mine = weights[f] * basis_now[:, face * f : face * (f + 1)]
+            mine_now = weights[f] * basis_now[:, face * f : face * (f + 1)]
             other = got[f]
             if other is None:
-                bases += [mine, jnp.zeros_like(mine)]
+                both = [mine_now, jnp.zeros_like(mine_now)]
                 tables += [rows_ref[...], jnp.zeros((nco, coarse_all), F32)]
             else:
-                bases += [mine, 0.5 * other[face : face + nco]]
+                both = [mine_now, 0.5 * other[face : face + nco]]
                 tables += [
                     rows_ref[...],
                     jnp.concatenate(
@@ -361,102 +366,144 @@
                         axis=1,
                     ),
                 ]
-        bases_ref[...] = jnp.concatenate(bases, axis=0)
+            none = jnp.zeros((2 * nco, face), F32)
+            block = jnp.concatenate(both, axis=0)
+            bases.append(jnp.concatenate([block if k == f else none for k in range(4)], axis=1))
+        by_row = jnp.concatenate(bases, axis=0).T
+        bases_ref[...] = by_row
+        a, b, c = thirds(by_row)
+        deep_ref[...] = jnp.concatenate([a, a, b, a, c, b], axis=1)
         table_ref[...] = jnp.concatenate(tables, axis=0)
 
-    gram_part, bases, table = call(
+    gram_part, bases, deep_bases, table = call(
         first_tables,
         [
             (gram_shape, F32),
-            ((8 * nco, face), F32),
+            ((unknowns, 8 * nco), F32),
+            ((unknowns, 48 * nco), BF16),
             ((8 * nco, coarse_all), F32),
         ],
     )(*got_a, scaled, product, basis, coarse_rows)
 
-    def coarse_part(bases_now, values):
-        return [
-            dot(bases_now[2 * nco * f : 2 * nco * (f + 1)], values[2 * nco * f : 2 * nco * (f + 1)], 0, 0)
-            for f in range(4)
-        ]
+    def coarse_part(deep, values):
+        p, q, r = thirds(values)
+        return plain(deep, jnp.concatenate([p, q, p, r, p, q], axis=0))
 
     mine = -(-cols // devices)
     packers = cols // mine
-    packed = 8 * -(-(mine + 1) // 8)
+    packed = mine + 1 + nco
 
     def triangles():
         row_id = lax.broadcasted_iota(jnp.int32, gram_shape, 0)
         col_id = lax.broadcasted_iota(jnp.int32, gram_shape, 1)
         return row_id < col_id, row_id == col_id
 
+    def first_coarse(all_ref, deep_ref, table_ref, mine_ref, gram_ref, values_ref, coarse_ref, first_ref):
+        values = deep_dot(table_ref[...], all_ref[...])
+        values_ref[...] = values
+        coarse_ref[...] = coarse_part(deep_ref[...], values)
+        first = gram_ref[...] + dot(mine_ref[0], values[:nco], 0, 0)
+        first_ref[...] = 0.5 * (first + first.T)
+
+    values, coarse, first_part = call(
+        first_coarse, [((8 * nco, cols), F32), (field, F32), (gram_shape, F32)]
+    )(coarse_all_in, deep_bases, table, coarse_input, gram_part)
+
     def first_direction(*refs):
         got = take(spread(refs[:nrounds]))
-        part_ref, all_ref, bases_ref, table_ref, schur_ref, mine_ref, gram_ref = refs[nrounds : nrounds + 7]
-        dir_ref, image_ref, values_ref, blocks_ref = refs[nrounds + 7 : nrounds + 11]
-        sends = spread(refs[nrounds + 11 :])
-        values = dot(table_ref[...], all_ref[...])
-        values_ref[...] = values
-        coarse = coarse_part(bases_ref[...], values)
-        update = add_faces(part_ref[...], got) + jnp.concatenate(coarse, axis=0)
+        part_ref, coarse_ref, bases_ref, schur_ref, first_ref = refs[nrounds : nrounds + 5]
+        dir_ref, image_ref, blocks_ref = refs[nrounds + 5 : nrounds + 8]
+        sends = spread(refs[nrounds + 8 :])
+        if packers < devices:
+            blocks_ref[...] = jnp.zeros(blocks_ref.shape, F32)
+        else:
+            blocks_ref[:, mine + 1 :] = jnp.zeros((devices, nco, 1, cols), F32)
+        update = add_faces(part_ref[...], got) + coarse_ref[...]
         dir_ref[...] = update
         image = half_dot(schur_ref[...], update.astype(BF16))
         image_ref[...] = image
         give(sends, split_faces(image))
-        first = gram_ref[...] + dot(mine_ref[0], values[:nco], 0, 0)
-        curvature = gram_dot(update, image)
+        stack = gram_dot(jnp.concatenate([update, bases_ref[...]], axis=1), image)
+        curvature, shares = stack[:cols], stack[cols:]
         above, on = triangles()
-        both = jnp.where(above, curvature + curvature.T, first + first.T) * 0.5
+        both = jnp.where(above, 0.5 * (curvature + curvature.T), first_ref[...])
         diagonal = jnp.sum(jnp.where(on, curvature, 0.0), axis=0, keepdims=True)
-        blocks_ref[:, mine : mine + 1, :] = jnp.broadcast_to(diagonal[None], (devices, 1, cols))
-        if packers < devices:
-            blocks_ref[:, 0:mine, :] = jnp.zeros((devices, mine, cols), F32)
-        if mine + 1 < packed:
-            blocks_ref[:, mine + 1 :, :] = jnp.zeros((devices, packed - mine - 1, cols), F32)
+        blocks_ref[:, mine : mine + 1] = jnp.broadcast_to(
+            diagonal.reshape(1, 1, 1, cols), (devices, 1, 1, cols)
+        )
         for k in range(packers):
-            blocks_ref[k, 0:mine, :] = both[mine * k : mine * (k + 1)]
+            for r in range(mine):
+                blocks_ref[k, r] = both[mine * k + r : mine * k + r + 1]
+        ix, iy = lax.axis_index("gx"), lax.axis_index("gy")
+        sx, sy = lax.axis_size("gx"), lax.axis_size("gy")
+        own = shares[0:nco]
+        for f in range(1, 4):
+            own = own + shares[2 * nco * f : 2 * nco * f + nco]
+        here = ix * sy + iy
+        targets = [
+            (here, own, None),
+            (here - sy, shares[nco : 2 * nco], ix > 0),
+            (here + sy, shares[3 * nco : 4 * nco], ix < sx - 1),
+            (here - 1, shares[5 * nco : 6 * nco], iy > 0),
+            (here + 1, shares[7 * nco : 8 * nco], iy < sy - 1),
+        ]
+
+        def put(target, rows):
+            for r in range(nco):
+                blocks_ref[target, mine + 1 + r] = rows[r : r + 1]
+
+        for target, rows, flag in targets:
+            if flag is None:
+                put(target, rows)
+            else:
+                pl.when(flag)(lambda target=target, rows=rows: put(target, rows))
 
     outs = call(
         first_direction,
-        [(field, F32), (field, F32), ((8 * nco, cols), F32), ((devices, packed, cols), F32)]
-        + [face_out] * nrounds,
-    )(*got_b, part, coarse_all_in, bases, table, schur_here, coarse_input, gram_part)
-    direction, image, values, blocks = outs[:4]
-    got_d = trade(fill(outs[4:]))
+        [(field, F32), (field, F32), ((devices, packed, 1, cols), F32)] + [face_out] * nrounds,
+    )(*got_b, part, coarse, bases, schur_here, first_part)
+    direction, image, blocks = outs[:3]
+    got_d = trade(fill(outs[3:]))
     blocks = lax.all_to_all(blocks, AXES, 0, 0)
     joint = 8 * -(-(mine + nco) // 8)
 
-    def first_sums(*refs):
-        got = take(spread(refs[:nrounds]))
-        image_ref, blocks_ref, basis_ref = refs[nrounds : nrounds + 3]
-        full_ref, sum_ref, mine_ref, diag_ref = refs[nrounds + 3 :]
-        image_vec = add_faces(image_ref[...], got)
-        full_ref[...] = image_vec
-        coarse_image = dot(basis_ref[...], weighted(image_vec, face_weights()))
-        mine_ref[...] = coarse_image
+    def first_sums(blocks_ref, sum_ref, mine_ref, diag_ref):
         total = jnp.sum(blocks_ref[...], axis=0)
-        diag_ref[...] = total[mine : mine + 1]
-        rows = [total[0:mine], coarse_image]
+        diag_ref[...] = total[mine]
+        coarse_image = [total[mine + 1 + r] for r in range(nco)]
+        mine_ref[...] = jnp.concatenate(coarse_image, axis=0)
+        rows = [total[r] for r in range(mine)] + coarse_image
         if mine + nco < joint:
             rows.append(jnp.zeros((joint - mine - nco, cols), F32))
         sum_ref[...] = jnp.broadcast_to(jnp.concatenate(rows, axis=0)[None], sum_ref.shape)
 
-    image_vec, sums, coarse_image, diagonal = call(
+    sums, coarse_image, diagonal = call(
         first_sums,
-        [(field, F32), ((devices, joint, cols), F32), ((nco, cols), F32), ((1, cols), F32)],
-    )(*got_d, image, blocks, basis)
+        [((devices, joint, cols), F32), ((nco, cols), F32), ((1, cols), F32)],
+    )(blocks)
     sums = lax.all_to_all(sums, AXES, 0, 0)
 
-    def second_local(sums_ref, diag_ref, res_ref, full_ref, inverse_ref, *outs):
-        outs, work_ref = outs[:-1], outs[-1]
-        curv_ref, first_ref, step_ref, scaled_ref, product_ref, part_ref = outs[:6]
-        sends = spread(outs[6:])
+    def first_step(sums_ref, diag_ref, curv_ref, first_ref, step_ref, work_ref):
         both = jnp.concatenate([sums_ref[k, 0:mine, :] for k in range(packers)], axis=0)
         turned = both.T
         above, on = triangles()
         curvature = jnp.where(above, both, jnp.where(on, diag_ref[...], turned))
         first = jnp.where(above, turned, both)
-        step = solve(curvature, first, work_ref, (), 5)
+        step_ref[...] = solve(curvature, first, work_ref, (), 5)
+        curv_ref[...] = curvature
+        first_ref[...] = first
+
+    curvature, first, step = call(first_step, [(gram_shape, F32)] * 3, work, flops=2 * 12 * cols**3)(
+        sums, diagonal
+    )
+
+    def second_local(*refs):
+        got = take(spread(refs[:nrounds]))
+        step_ref, res_ref, image_ref, inverse_ref = refs[nrounds : nrounds + 4]
+        scaled_ref, product_ref, part_ref = refs[nrounds + 4 : nrounds + 7]
+        sends = spread(refs[nrounds + 7 :])
         weights = face_weights()
-        residual = res_ref[...] - dot(full_ref[...], step)
+        residual = res_ref[...] - dot(add_faces(image_ref[...], got), step_ref[...])
         scaled = weighted(residual, weights)
         product = half_dot(inverse_ref[...], scaled.astype(BF16))
         part = weighted(product, weights)
@@ -464,17 +511,12 @@
         give(sends, split_faces(part))
         scaled_ref[...] = scaled
         product_ref[...] = product
-        curv_ref[...] = curvature
-        first_ref[...] = first
-        step_ref[...] = step
-
-    outs = call(
-        second_local,
-        [(gram_shape, F32)] * 3 + [(field, F32)] * 3 + [face_out] * nrounds,
-        work,
-    )(sums, diagonal, residual, image_vec, inverse_here)
-    curvature, first, step, scaled, product, part = outs[:6]
-    got_e = trade(fill(outs[6:]))
+
+    outs = call(second_local, [(field, F32)] * 3 + [face_out] * nrounds)(
+        *got_d, step, residual, image, inverse_here
+    )
+    scaled, product, part = outs[:3]
+    got_e = trade(fill(outs[3:]))
 
     def second_coarse(
         sums_ref, table_ref, values_ref, mine_ref, image_ref, step_ref, scaled_ref, product_ref,
@@ -489,7 +531,7 @@
         _, on = triangles()
         inverse = solve(first_ref[...], on.astype(F32), work_ref, (), 4)
         inv_ref[...] = inverse
-        quad_ref[...] = gram_dot(inverse, deep_dot(curv_ref[...], inverse))
+        quad_ref[...] = dot(inverse, deep_dot(curv_ref[...], inverse), 0, 0)
 
     next_part, values, first_inverse, quad = call(
         second_coarse,
@@ -503,10 +545,9 @@
 
     def second_direction(*refs):
         got = take(spread(refs[:nrounds]))
-        part_ref, next_ref, values_ref, bases_ref, schur_ref = refs[nrounds : nrounds + 5]
+        part_ref, next_ref, values_ref, deep_ref, schur_ref = refs[nrounds : nrounds + 5]
         update_ref, blocks_ref = refs[nrounds + 5 :]
-        coarse = coarse_part(bases_ref[...], values_ref[...])
-        update = add_faces(part_ref[...], got) + jnp.concatenate(coarse, axis=0)
+        update = add_faces(part_ref[...], got) + coarse_part(deep_ref[...], values_ref[...])
         update_ref[...] = update
         high = update.astype(BF16)
         low = (update - high.astype(F32)).astype(BF16)
@@ -516,32 +557,39 @@
         write_blocks(blocks_ref, jnp.concatenate([next_ref[...], square], axis=0))
 
     update, blocks = call(second_direction, [(field, F32), blocks_out])(
-        *got_e, part, next_part, values, bases, schur_here
+        *got_e, part, next_part, values, deep_bases, schur_here
     )
     blocks = lax.all_to_all(blocks, AXES, 0, 0)
 
-    def second_sums(blocks_ref, out_ref, keep_ref):
-        total = jnp.sum(blocks_ref[...], axis=0)
-        out_ref[...] = jnp.broadcast_to(total[None], out_ref.shape)
-        keep_ref[...] = total
-
-    sums, _ = call(second_sums, [blocks_out, ((per, cols), F32)])(blocks)
+    def second_sums(blocks_ref, out_ref):
+        out_ref[...] = jnp.broadcast_to(jnp.sum(blocks_ref[...], axis=0)[None], out_ref.shape)
+
+    (sums,) = call(second_sums, [blocks_out])(blocks)
     sums = lax.all_to_all(sums, AXES, 0, 0).reshape(devices * per, cols)
 
-    def finish(sums_ref, inv_ref, quad_ref, step_ref, dir_ref, update_ref, out_ref, work_ref):
+    def finish(
+        sums_ref, inv_ref, quad_ref, step_ref, dir_ref, update_ref, out_hbm, work_ref, rows_ref, sems
+    ):
         next_gram, square = sums_ref[0:cols], sums_ref[cols : 2 * cols]
-        curvature = square - gram_dot(next_gram, deep_dot(quad_ref[...], next_gram))
-        curvature = 0.5 * (curvature + curvature.T)
+        square = 0.5 * (square + square.T)
+        curvature = square - dot(next_gram, deep_dot(quad_ref[...], next_gram), 0, 0)
         ratio = deep_dot(inv_ref[...], next_gram)
         step = solve(curvature, next_gram, work_ref, (1.8, 1.8, 1.5), 7)
         total = step_ref[...] + deep_dot(ratio, step)
-        fields = jnp.concatenate([dir_ref[...], update_ref[...]], axis=1)
-        coefs = jnp.concatenate([total, step], axis=0)
-        a, b, _ = thirds(fields)
-        p, q, _ = thirds(coefs)
-        out_ref[...] = plain(a, p) + (plain(a, q) + plain(b, p))
-
-    (solved,) = call(finish, [(field, F32)], work)(
+        p, q, _ = thirds(jnp.concatenate([total, step], axis=0))
+        copies = []
+        for f in range(4):
+            here = pl.ds(face * f, face)
+            a, b, _ = thirds(jnp.concatenate([dir_ref[here], update_ref[here]], axis=1))
+            rows_ref[here] = plain(a, p) + (plain(a, q) + plain(b, p))
+            copies.append(
+                pltpu.make_async_copy(rows_ref.at[here], out_hbm.at[here], sems.at[f])
+            )
+            copies[-1].start()
+        for copy in copies:
+            copy.wait()
+
+    (solved,) = call(finish, [(field, F32)], work + [(field, F32)], copies=4, far_out=True)(
         sums, first_inverse, quad, step, direction, update
     )
     return solved[None, None]

time: 90.9 us -> 86.9 us (0.956)
  waiting for transfers between devices: 8.1 us -> 6.07 us
  starting transfers between devices: 30.2 us -> 28.2 us
  Pallas kernels: 18.7 us -> 17.2 us
  blocking collectives: 33.3 us -> 34.8 us
    all_to_all x1 -> x2, blocking collectives: 11.1 us -> 24.8 us  [local(): blocks = lax.all_to_all(blocks, AXES, 0, 0)]
    all_to_all x1 -> x0, blocking collectives: 12.2 us -> none  [local(): sums = lax.all_to_all(sums, AXES, 0, 0)]
    ppermute x12, waiting for transfers between devices: 8.09 us -> 1.15 us  [exchange(): got.append(lax.ppermute(piece, axis, pairs) if pairs else None)]
    all_to_all x1, waiting for transfers between devices: 0.01 us -> 3.13 us  [local(): sums = lax.all_to_all(sums, AXES, 0, 0)]
    all_to_all x1, starting transfers between devices: 4.46 us -> 2.58 us  [local(): sums = lax.all_to_all(sums, AXES, 0, 0)]
    all_to_all x1, waiting for transfers between devices: 0.01 us -> 1.79 us  [local(): lax.all_to_all(coarse_input, AXES, 0, 0).reshape(coarse_all, cols)]
    pallas_call x11 -> x13, Pallas kernels: 18.7 us -> 17.2 us  [run(): kernel_call(body, outs, scratch, flops, moved, sems, specs, results)(*args)]
  transfers between devices with their start and end apart: 14 -> 14, of which waited for: 4 -> 4; matrix products, arithmetic and copies ran while one was open for 0% -> 0% of each run, Pallas kernels for 6% -> 10%
where the time goes in v4:
time: 86.9 us; the launch traced here: 86.4 us
  blocking collectives  34.8 us (40%)
  starting transfers between devices  28.2 us (32%)
  Pallas kernels  17.2 us (20%)
  waiting for transfers between devices  6.07 us (7%)
    all_to_all x2, blocking collectives, local(): blocks = lax.all_to_all(blocks, AXES, 0, 0)  24.8 us
    ppermute x12, starting transfers between devices, exchange(): got.append(lax.ppermute(piece, axis, pairs) if pairs else None)  20.8 us
    pallas_call x13, Pallas kernels, run(): kernel_call(body, outs, scratch, flops, moved, sems, specs, results)(*args)  17.2 us
    all_to_all x1, blocking collectives, local(): sums = lax.all_to_all(sums, AXES, 0, 0).reshape(devices * per, cols)  10 us
    all_to_all x1, starting transfers between devices, local(): lax.all_to_all(coarse_input, AXES, 0, 0).reshape(coarse_all, cols)  4.84 us
    all_to_all x1, waiting for transfers between devices, local(): sums = lax.all_to_all(sums, AXES, 0, 0)  3.13 us
    all_to_all x1, starting transfers between devices, local(): sums = lax.all_to_all(sums, AXES, 0, 0)  2.58 us
    all_to_all x1, waiting for transfers between devices, local(): lax.all_to_all(coarse_input, AXES, 0, 0).reshape(coarse_all, cols)  1.79 us
  transfers between devices with their start and end apart: 14, of which 4 were waited for; matrix products, arithmetic and copies ran while one was open for 0% of the time, Pallas kernels for 10%

profile of v4, /device:TPU:0, one launch (start us, length us, event | category | flops | bytes accessed | tf_op | source)
XLA Modules:
  0.0 86.4 jit_solution(9398665951464432501)
XLA Ops:
  0.0 1.0 %shard_map.64 = (f32[512,128]{1,0:T(8,128)S(1)}, f32[4,512]{1,0:T(4,128)S(1)}, f32[4,128]{1,0:T(4,128)S(1)}, s32[1,512]{1,0:T(1,128)S(1)}, f32[136,128]{1,0:T(8,...) custom-call(bf16[512,128]{1,0:T(8,128)(2,1)} %bitcast.11, f32[4,512]{1,0:T(4,128)} %bitcast.12, ...), custom_call_target="tpu_custom_call" | custom-call | tf_op jit(solution)/shard_map/pallas_call | solution.py:72
  1.0 0.7 collective-permute-start
  1.7 5.7 %collective-permute-start.1 = (f32[136,128]{1,0:T(8,128)S(1)}, f32[136,128]{1,0:T(8,128)S(1)}, u32[]{:S(2)}, u32[]{:S(2)}) collective-permute-start(f32[136,128]{1,0:T(8,128)S(1)} %get-tuple-element.54), channel_id=1, source_target_pairs={{0,2},{4,6},{8,10},{12,14},{16,18},{20,22},{24,26},{28,30},{2,0},{... | collective-permute-start | bytes 208904 | tf_op jit(solution)/shard_map/ppermute | solution.py:99
  7.4 0.0 collective-permute-start.2
  7.4 2.5 %shard_map.65 = (bf16[512,512]{1,0:T(8,128)(2,1)S(1)}, bf16[512,512]{1,0:T(8,128)(2,1)S(1)}) custom-call(bf16[512,512]{1,0:T(8,128)(2,1)} %bitcast.15, bf16[512,512]{1,0:T(8,128)(2,1)} %bitcast.16, s32[1,512]{1,0:T(1,128)S(1)} %get-tuple-element.57.map_ref), custom_call_target="tpu_custom_call" | custom-call | flops 1073741824 | bytes 2097152 | tf_op jit(solution)/shard_map/pallas_call | solution.py:72
  9.9 0.0 collective-permute-done.refs_0_
  9.9 0.8 collective-permute-done.1.refs_1_
  10.7 0.0 collective-permute-done.2.refs_2_
  10.7 1.1 %shard_map.66 = (f32[512,128]{1,0:T(8,128)S(1)}, f32[512,128]{1,0:T(8,128)S(1)}, f32[512,128]{1,0:T(8,128)S(1)}, f32[512,128]{1,0:T(8,128)S(1)}, f32[32,4,128]{2...) custom-call(f32[136,128]{1,0:T(8,128)S(1)} %collective-permute-done.refs_0_, ...), custom_call_target="tpu_custom_call" | custom-call | tf_op jit(solution)/shard_map/pallas_call | solution.py:72
  11.8 4.8 %all-to-all-start = ((f32[32,4,128]{2,1,0:T(4,128)}), f32[32,4,128]{2,1,0:T(4,128)S(1)}, u32[]{:S(2)}, u32[]{:S(2)}) async-start(f32[32,4,128]{2,1,0:T(4,128)} %get-tuple-element.64.mine_ref), calls=%async_computation | async-start | bytes 131072 | tf_op jit(solution)/shard_map/all_to_all | solution.py:341
  16.6 0.7 collective-permute-start.3
  17.3 4.5 %collective-permute-start.4 = (f32[128,128]{1,0:T(8,128)S(1)}, f32[128,128]{1,0:T(8,128)S(1)}, u32[]{:S(2)}, u32[]{:S(2)}) collective-permute-start(f32[128,128]{1,0:T(8,128)S(1)} %get-tuple-element.61), channel_id=1, source_target_pairs={{0,2},{4,6},{8,10},{12,14},{16,18},{20,22},{24,26},{28,30},{2,0},{... | collective-permute-start | bytes 196616 | tf_op jit(solution)/shard_map/ppermute | solution.py:99
  21.8 0.0 collective-permute-start.5
  21.8 0.4 shard_map.67
  22.2 1.8 %all-to-all-done = f32[32,4,128]{2,1,0:T(4,128)S(1)} async-done(((f32[32,4,128]{2,1,0:T(4,128)}), f32[32,4,128]{2,1,0:T(4,128)S(1)}, u32[]{:S(2)}, u32[]{:S(2)}) %all-to-all-start) | async-done | bytes 65568 | tf_op jit(solution)/shard_map/all_to_all | solution.py:341
  24.0 1.3 %shard_map.68 = (f32[32,128]{1,0:T(8,128)S(1)}, f32[512,128]{1,0:T(8,128)S(1)}, f32[128,128]{1,0:T(8,128)S(1)}) custom-call(f32[128,128]{1,0:T(8,128)S(1)} %bitcast.10, bf16[512,192]{1,0:T(8,128)(2,1)S(1)} %get-tuple-element.68.deep_ref.refs_6_, f32[32,128]{1,0:T(8,128)S(1)} %get-tuple-element.69.table_ref, f32[32,4,128]{2,1,0:T(4,128)} %get-tuple-element.64.mine_ref, ...), custom_call_target="tpu_custom_call" | custom-call | tf_op jit(solution)/shard_map/pallas_call | solution.py:72
  25.3 0.0 collective-permute-done.3.refs_0_
  25.3 0.0 collective-permute-done.4.refs_1_
  25.4 0.0 collective-permute-done.5.refs_2_
  25.4 0.7 shard_map.69
  26.1 12.7 %all_to_all.25.blocks_ref = f32[32,9,1,128]{3,2,1,0:T(1,128)S(1)} all-to-all(f32[32,9,1,128]{3,2,1,0:T(1,128)S(1)} %get-tuple-element.78), channel_id=1, replica_groups=mesh['gx'=16,'gy'=2] {'gx','gy'}, dimensions={0} | all-to-all | bytes 294912 | tf_op jit(solution)/shard_map/all_to_all | solution.py:467
  38.8 0.8 shard_map.70
  39.6 2.6 %all-to-all-start.2 = ((f32[32,8,128]{2,1,0:T(8,128)}), f32[32,8,128]{2,1,0:T(8,128)S(1)}, u32[]{:S(2)}, u32[]{:S(2)}) async-start(f32[32,8,128]{2,1,0:T(8,128)} %get-tuple-element.79), calls=%async_computation.2 | async-start | bytes 262144 | tf_op jit(solution)/shard_map/all_to_all | solution.py:484
  42.2 0.7 collective-permute-start.6
  42.8 4.4 %collective-permute-start.7 = (f32[128,128]{1,0:T(8,128)S(1)}, f32[128,128]{1,0:T(8,128)S(1)}, u32[]{:S(2)}, u32[]{:S(2)}) collective-permute-start(f32[128,128]{1,0:T(8,128)S(1)} %get-tuple-element.76), channel_id=1, source_target_pairs={{0,2},{4,6},{8,10},{12,14},{16,18},{20,22},{24,26},{28,30},{2,0},{... | collective-permute-start | bytes 196616 | tf_op jit(solution)/shard_map/ppermute | solution.py:99
  47.3 0.0 collective-permute-start.8
  47.3 3.1 %all-to-all-done.2.sums_ref = f32[32,8,128]{2,1,0:T(8,128)S(1)} async-done(((f32[32,8,128]{2,1,0:T(8,128)}), f32[32,8,128]{2,1,0:T(8,128)S(1)}, u32[]{:S(2)}, u32[]{:S(2)}) %all-to-all-start.2) | async-done | bytes 131104 | tf_op jit(solution)/shard_map/all_to_all | solution.py:484
  50.4 1.6 %shard_map.71 = (f32[128,128]{1,0:T(8,128)S(1)}, f32[128,128]{1,0:T(8,128)S(1)}, f32[128,128]{1,0:T(8,128)S(1)}) custom-call(f32[32,8,128]{2,1,0:T(8,128)S(1)} %all-to-all-done.2.sums_ref, f32[1,128]{1,0:T(1,128)S(1)} %get-tuple-element.80.diag_ref), custom_call_target="tpu_custom_call" | custom-call | flops 50331648 | tf_op jit(solution)/shard_map/pallas_call | solution.py:72
  52.0 0.0 collective-permute-done.6.refs_0_
  52.0 0.0 collective-permute-done.7.refs_1_
  52.0 0.0 collective-permute-done.8.refs_2_
  52.0 0.8 shard_map.72
  52.9 0.7 collective-permute-start.9
  53.5 3.4 %collective-permute-start.10 = (f32[128,128]{1,0:T(8,128)S(1)}, f32[128,128]{1,0:T(8,128)S(1)}, u32[]{:S(2)}, u32[]{:S(2)}) collective-permute-start(f32[128,128]{1,0:T(8,128)S(1)} %get-tuple-element.85), channel_id=1, source_target_pairs={{0,2},{4,6},{8,10},{12,14},{16,18},{20,22},{24,26},{28,30},{2,0},{... | collective-permute-start | bytes 196616 | tf_op jit(solution)/shard_map/ppermute | solution.py:99
  57.0 0.0 collective-permute-start.11
  57.0 2.8 %shard_map.73 = (f32[128,128]{1,0:T(8,128)S(1)}, f32[32,128]{1,0:T(8,128)S(1)}, f32[128,128]{1,0:T(8,128)S(1)}, f32[128,128]{1,0:T(8,128)S(1)}) custom-call(f32[32,8,128]{2,1,0:T(8,128)S(1)} %all-to-all-done.2.sums_ref, f32[32,128]{1,0:T(8,128)S(1)} %get-tuple-element.69.table_ref, f32[32,128]{1,0:T(8,128)S(1)} %get-tuple-element.88.values_ref, ...), custom_call_target="tpu_custom_call" | custom-call | flops 201326592 | tf_op jit(solution)/shard_map/pallas_call | solution.py:72
  59.8 0.0 collective-permute-done.9.refs_0_
  59.8 0.3 collective-permute-done.10.refs_1_
  60.1 0.0 collective-permute-done.11.refs_2_
  60.1 0.8 shard_map.74
  60.9 12.1 %all_to_all.26.blocks_ref = f32[32,8,128]{2,1,0:T(8,128)S(1)} all-to-all(f32[32,8,128]{2,1,0:T(8,128)S(1)} %get-tuple-element.96), channel_id=1, replica_groups=mesh['gx'=16,'gy'=2] {'gx','gy'}, dimensions={0} | all-to-all | bytes 262144 | tf_op jit(solution)/shard_map/all_to_all | solution.py:562
  73.1 10.0 %all_to_all.27 = f32[32,8,128]{2,1,0:T(8,128)S(1)} all-to-all(f32[32,8,128]{2,1,0:T(8,128)S(1)} %shard_map.75), channel_id=1, replica_groups=mesh['gx'=16,'gy'=2] {'gx','gy'}, dimensions={0} | all-to-all | bytes 262144 | tf_op jit(solution)/shard_map/all_to_all | solution.py:568
  83.1 3.3 %shard_map.76 = f32[512,128]{1,0:T(8,128)} custom-call(f32[256,128]{1,0:T(8,128)S(1)} %bitcast.9, f32[128,128]{1,0:T(8,128)S(1)} %get-tuple-element.97.inv_ref, f32[128,128]{1,0:T(8,128)S(1)} %get-tuple-element.98.quad_ref, f32[128,128]{1,0:T(8,128)S(1)} %get-tuple-element.81.refs_3_.step_ref, f32[512,128]{1,0:T(8,128)S(1)} %get-tuple-element.99.dir_ref, ...), custom_call_target="tpu_custom_call" | custom-call | tf_op jit(solution)/shard_map/pallas_call | solution.py:72
  (1 shorter events, 0.0 us)
Async XLA Ops:
  1.0 8.9 %collective-permute-start = (f32[136,128]{1,0:T(8,128)S(1)}, f32[136,128]{1,0:T(8,128)S(1)}, u32[]{:S(2)}, u32[]{:S(2)}) collective-permute-start(f32[136,128]{1,0:T(8,128)S(1)} %get-tuple-element.53), channel_id=1, source_target_pairs={{2,4},{6,8},{10,12},{14,16},{18,20},{22,24},{26,28},{4,2},{8,6},{1... | collective-permute-start | bytes 208904 | tf_op jit(solution)/shard_map/ppermute | solution.py:99
  1.7 9.0 %collective-permute-start.1 = (f32[136,128]{1,0:T(8,128)S(1)}, f32[136,128]{1,0:T(8,128)S(1)}, u32[]{:S(2)}, u32[]{:S(2)}) collective-permute-start(f32[136,128]{1,0:T(8,128)S(1)} %get-tuple-element.54), channel_id=1, source_target_pairs={{0,2},{4,6},{8,10},{12,14},{16,18},{20,22},{24,26},{28,30},{2,0},{... | collective-permute-start | bytes 208904 | tf_op jit(solution)/shard_map/ppermute | solution.py:99
  7.4 3.3 %collective-permute-start.2 = (f32[136,128]{1,0:T(8,128)S(1)}, f32[136,128]{1,0:T(8,128)S(1)}, u32[]{:S(2)}, u32[]{:S(2)}) collective-permute-start(f32[136,128]{1,0:T(8,128)S(1)} %get-tuple-element.55), channel_id=1, source_target_pairs={{0,1},{1,0},{2,3},{3,2},{4,5},{5,4},{6,7},{7,6},{8,9},{9,8},{10,11... | collective-permute-start | bytes 208904 | tf_op jit(solution)/shard_map/ppermute | solution.py:99
  11.8 12.3 %all-to-all-start = ((f32[32,4,128]{2,1,0:T(4,128)}), f32[32,4,128]{2,1,0:T(4,128)S(1)}, u32[]{:S(2)}, u32[]{:S(2)}) async-start(f32[32,4,128]{2,1,0:T(4,128)} %get-tuple-element.64.mine_ref), calls=%async_computation | async-start | bytes 131072 | tf_op jit(solution)/shard_map/all_to_all | solution.py:341
  16.6 8.7 %collective-permute-start.3 = (f32[128,128]{1,0:T(8,128)S(1)}, f32[128,128]{1,0:T(8,128)S(1)}, u32[]{:S(2)}, u32[]{:S(2)}) collective-permute-start(f32[128,128]{1,0:T(8,128)S(1)} %get-tuple-element.60), channel_id=1, source_target_pairs={{2,4},{6,8},{10,12},{14,16},{18,20},{22,24},{26,28},{4,2},{8,6},{1... | collective-permute-start | bytes 196616 | tf_op jit(solution)/shard_map/ppermute | solution.py:99
  17.3 8.1 %collective-permute-start.4 = (f32[128,128]{1,0:T(8,128)S(1)}, f32[128,128]{1,0:T(8,128)S(1)}, u32[]{:S(2)}, u32[]{:S(2)}) collective-permute-start(f32[128,128]{1,0:T(8,128)S(1)} %get-tuple-element.61), channel_id=1, source_target_pairs={{0,2},{4,6},{8,10},{12,14},{16,18},{20,22},{24,26},{28,30},{2,0},{... | collective-permute-start | bytes 196616 | tf_op jit(solution)/shard_map/ppermute | solution.py:99
  21.8 3.6 %collective-permute-start.5 = (f32[128,128]{1,0:T(8,128)S(1)}, f32[128,128]{1,0:T(8,128)S(1)}, u32[]{:S(2)}, u32[]{:S(2)}) collective-permute-start(f32[128,128]{1,0:T(8,128)S(1)} %get-tuple-element.62), channel_id=1, source_target_pairs={{0,1},{1,0},{2,3},{3,2},{4,5},{5,4},{6,7},{7,6},{8,9},{9,8},{10,11... | collective-permute-start | bytes 196616 | tf_op jit(solution)/shard_map/ppermute | solution.py:99
  39.6 10.8 %all-to-all-start.2 = ((f32[32,8,128]{2,1,0:T(8,128)}), f32[32,8,128]{2,1,0:T(8,128)S(1)}, u32[]{:S(2)}, u32[]{:S(2)}) async-start(f32[32,8,128]{2,1,0:T(8,128)} %get-tuple-element.79), calls=%async_computation.2 | async-start | bytes 262144 | tf_op jit(solution)/shard_map/all_to_all | solution.py:484
  42.2 9.8 %collective-permute-start.6 = (f32[128,128]{1,0:T(8,128)S(1)}, f32[128,128]{1,0:T(8,128)S(1)}, u32[]{:S(2)}, u32[]{:S(2)}) collective-permute-start(f32[128,128]{1,0:T(8,128)S(1)} %get-tuple-element.75), channel_id=1, source_target_pairs={{2,4},{6,8},{10,12},{14,16},{18,20},{22,24},{26,28},{4,2},{8,6},{1... | collective-permute-start | bytes 196616 | tf_op jit(solution)/shard_map/ppermute | solution.py:99
  42.8 9.2 %collective-permute-start.7 = (f32[128,128]{1,0:T(8,128)S(1)}, f32[128,128]{1,0:T(8,128)S(1)}, u32[]{:S(2)}, u32[]{:S(2)}) collective-permute-start(f32[128,128]{1,0:T(8,128)S(1)} %get-tuple-element.76), channel_id=1, source_target_pairs={{0,2},{4,6},{8,10},{12,14},{16,18},{20,22},{24,26},{28,30},{2,0},{... | collective-permute-start | bytes 196616 | tf_op jit(solution)/shard_map/ppermute | solution.py:99
  47.3 4.8 %collective-permute-start.8 = (f32[128,128]{1,0:T(8,128)S(1)}, f32[128,128]{1,0:T(8,128)S(1)}, u32[]{:S(2)}, u32[]{:S(2)}) collective-permute-start(f32[128,128]{1,0:T(8,128)S(1)} %get-tuple-element.77), channel_id=1, source_target_pairs={{0,1},{1,0},{2,3},{3,2},{4,5},{5,4},{6,7},{7,6},{8,9},{9,8},{10,11... | collective-permute-start | bytes 196616 | tf_op jit(solution)/shard_map/ppermute | solution.py:99
  52.9 7.0 %collective-permute-start.9 = (f32[128,128]{1,0:T(8,128)S(1)}, f32[128,128]{1,0:T(8,128)S(1)}, u32[]{:S(2)}, u32[]{:S(2)}) collective-permute-start(f32[128,128]{1,0:T(8,128)S(1)} %get-tuple-element.84), channel_id=1, source_target_pairs={{2,4},{6,8},{10,12},{14,16},{18,20},{22,24},{26,28},{4,2},{8,6},{1... | collective-permute-start | bytes 196616 | tf_op jit(solution)/shard_map/ppermute | solution.py:99
  53.5 6.6 %collective-permute-start.10 = (f32[128,128]{1,0:T(8,128)S(1)}, f32[128,128]{1,0:T(8,128)S(1)}, u32[]{:S(2)}, u32[]{:S(2)}) collective-permute-start(f32[128,128]{1,0:T(8,128)S(1)} %get-tuple-element.85), channel_id=1, source_target_pairs={{0,2},{4,6},{8,10},{12,14},{16,18},{20,22},{24,26},{28,30},{2,0},{... | collective-permute-start | bytes 196616 | tf_op jit(solution)/shard_map/ppermute | solution.py:99
  57.0 3.2 %collective-permute-start.11 = (f32[128,128]{1,0:T(8,128)S(1)}, f32[128,128]{1,0:T(8,128)S(1)}, u32[]{:S(2)}, u32[]{:S(2)}) collective-permute-start(f32[128,128]{1,0:T(8,128)S(1)} %get-tuple-element.86), channel_id=1, source_target_pairs={{0,1},{1,0},{2,3},{3,2},{4,5},{5,4},{6,7},{7,6},{8,9},{9,8},{10,11... | collective-permute-start | bytes 196616 | tf_op jit(solution)/shard_map/ppermute | solution.py:99

commit v5 on v4

--- a/solution.py
+++ b/solution.py
@@ -62,13 +62,16 @@
     )
 
 
-def call(body, outs, scratch=(), flops=0, moved=0, far=0, copies=0, far_out=False):
+def call(body, outs, scratch=(), flops=0, moved=0, far=0, copies=0, far_outs=()):
     sems = [pltpu.SemaphoreType.DMA((copies,))] if copies else []
 
     def run(*args):
         specs = [pl.BlockSpec(memory_space=pltpu.HBM if i < far else pltpu.VMEM) for i in range(len(args))]
         args = [pltpu.with_memory_space_constraint(a, pltpu.HBM) if i < far else a for i, a in enumerate(args)]
-        results = [pl.BlockSpec(memory_space=pltpu.HBM if far_out else pltpu.VMEM) for _ in outs]
+        results = [
+            pl.BlockSpec(memory_space=pltpu.HBM if k in far_outs else pltpu.VMEM)
+            for k in range(len(outs))
+        ]
         return kernel_call(body, outs, scratch, flops, moved, sems, specs, results)(*args)
 
     return run
@@ -169,7 +172,7 @@
     out_ref[0:used] = rows.reshape(used, per, rows.shape[1])
 
 
-def solve(matrix, right, work_ref, boosts, squarings):
+def solve(matrix, right, work_ref, boosts, squarings, exact):
     size = matrix.shape[0]
     row_id = lax.broadcasted_iota(jnp.int32, (size, size), 0)
     col_id = lax.broadcasted_iota(jnp.int32, (size, size), 1)
@@ -187,15 +190,12 @@
         return answer + product(power, answer), product(power, power)
 
     for k in range(squarings):
-        answer, power = step(answer, power, flat_dot if boosts and k > 1 else deep_dot)
+        answer, power = step(answer, power, deep_dot if k < exact else flat_dot)
         if k < len(boosts):
             power = boosts[k] * power + (1.0 - boosts[k]) * eye
             answer = boosts[k] * answer
-    work_ref[:, 0:size] = answer + deep_dot(power, answer)
-    largest = jnp.max(jnp.abs(power))
-
-    @pl.when(jnp.logical_not(largest < 3e-4))
-    def _():
+
+    def resume():
         work_ref[:, 0:size] = answer
         work_ref[:, size:] = power
 
@@ -208,10 +208,12 @@
         lax.while_loop(
             lambda carry: jnp.logical_and(carry[0] < 40, carry[1] > 1e-7),
             again,
-            (jnp.int32(0), largest),
+            (jnp.int32(0), jnp.float32(1.0)),
         )
-
-    return work_ref[:, 0:size] * by_row
+        return work_ref[:, 0:size] * by_row
+
+    good = jnp.sum(power * power) < 1e-4
+    return (answer + deep_dot(power, answer)) * by_row, good, resume
 
 
 def local(loads, schur, local_inverse, coarse_basis, coarse_inverse, face_map):
@@ -318,26 +320,35 @@
     def first_local(*refs):
         got = take(spread(refs[:nrounds]))
         loads_ref, inverse_ref, basis_ref = refs[nrounds : nrounds + 3]
-        res_ref, scaled_ref, product_ref, part_ref, ci_ref = refs[nrounds + 3 : nrounds + 8]
-        sends = spread(refs[nrounds + 8 :])
+        res_ref, scaled_ref, product_ref, part_ref, mine_ref, ci_hbm = refs[nrounds + 3 : nrounds + 9]
+        sends, ci_ref, sems = spread(refs[nrounds + 9 : -2]), refs[-2], refs[-1]
         weights = face_weights()
         residual = add_faces(loads_ref[...], [g if g is None else g[:face] for g in got])
         scaled = weighted(residual, weights)
+        coarse_input = dot(basis_ref[...], scaled)
+        mine_ref[...] = coarse_input
+        ci_ref[...] = jnp.broadcast_to(coarse_input[None], ci_ref.shape)
+        copy = pltpu.make_async_copy(ci_ref, ci_hbm, sems.at[0])
+        copy.start()
         product = half_dot(inverse_ref[...], scaled.astype(BF16))
         part = weighted(product, weights)
         give(sends, split_faces(part))
-        coarse_input = dot(basis_ref[...], scaled)
-        ci_ref[...] = jnp.broadcast_to(coarse_input[None], ci_ref.shape)
         res_ref[...] = residual
         scaled_ref[...] = scaled
         product_ref[...] = product
         part_ref[...] = part
-
+        copy.wait()
+
+    spread_rows = ((devices, nco, cols), F32)
     outs = call(
-        first_local, [(field, F32)] * 4 + [((devices, nco, cols), F32)] + [face_out] * nrounds
+        first_local,
+        [(field, F32)] * 4 + [((nco, cols), F32), spread_rows] + [face_out] * nrounds,
+        [spread_rows],
+        copies=1,
+        far_outs=(5,),
     )(*got_a, loads, inverse_here, basis)
-    residual, scaled, product, part, coarse_input = outs[:5]
-    got_b = trade(fill(outs[5:]))
+    residual, scaled, product, part, coarse_mine, coarse_input = outs[:6]
+    got_b = trade(fill(outs[6:]))
     coarse_all_in = lax.all_to_all(coarse_input, AXES, 0, 0).reshape(coarse_all, cols)
 
     def first_tables(*refs):
@@ -391,33 +402,34 @@
 
     mine = -(-cols // devices)
     packers = cols // mine
-    packed = mine + 1 + nco
-
-    def triangles():
+    tall = max(mine, nco)
+    block_shape = (devices, 3, tall, cols)
+
+    def identity():
         row_id = lax.broadcasted_iota(jnp.int32, gram_shape, 0)
         col_id = lax.broadcasted_iota(jnp.int32, gram_shape, 1)
-        return row_id < col_id, row_id == col_id
+        return (row_id == col_id).astype(F32)
 
     def first_coarse(all_ref, deep_ref, table_ref, mine_ref, gram_ref, values_ref, coarse_ref, first_ref):
         values = deep_dot(table_ref[...], all_ref[...])
         values_ref[...] = values
         coarse_ref[...] = coarse_part(deep_ref[...], values)
-        first = gram_ref[...] + dot(mine_ref[0], values[:nco], 0, 0)
-        first_ref[...] = 0.5 * (first + first.T)
+        rows, results = mine_ref[...], values[:nco]
+        first_ref[...] = gram_ref[...] + dot(rows, results, 0, 0)
 
     values, coarse, first_part = call(
         first_coarse, [((8 * nco, cols), F32), (field, F32), (gram_shape, F32)]
-    )(coarse_all_in, deep_bases, table, coarse_input, gram_part)
+    )(coarse_all_in, deep_bases, table, coarse_mine, gram_part)
 
     def first_direction(*refs):
         got = take(spread(refs[:nrounds]))
         part_ref, coarse_ref, bases_ref, schur_ref, first_ref = refs[nrounds : nrounds + 5]
         dir_ref, image_ref, blocks_ref = refs[nrounds + 5 : nrounds + 8]
         sends = spread(refs[nrounds + 8 :])
-        if packers < devices:
+        if packers < devices or mine < tall:
             blocks_ref[...] = jnp.zeros(blocks_ref.shape, F32)
         else:
-            blocks_ref[:, mine + 1 :] = jnp.zeros((devices, nco, 1, cols), F32)
+            blocks_ref[:, 2] = jnp.zeros((devices, tall, cols), F32)
         update = add_faces(part_ref[...], got) + coarse_ref[...]
         dir_ref[...] = update
         image = half_dot(schur_ref[...], update.astype(BF16))
@@ -425,15 +437,9 @@
         give(sends, split_faces(image))
         stack = gram_dot(jnp.concatenate([update, bases_ref[...]], axis=1), image)
         curvature, shares = stack[:cols], stack[cols:]
-        above, on = triangles()
-        both = jnp.where(above, 0.5 * (curvature + curvature.T), first_ref[...])
-        diagonal = jnp.sum(jnp.where(on, curvature, 0.0), axis=0, keepdims=True)
-        blocks_ref[:, mine : mine + 1] = jnp.broadcast_to(
-            diagonal.reshape(1, 1, 1, cols), (devices, 1, 1, cols)
-        )
-        for k in range(packers):
-            for r in range(mine):
-                blocks_ref[k, r] = both[mine * k + r : mine * k + r + 1]
+        for at, gram in ((0, curvature), (1, first_ref[...])):
+            for k in range(packers):
+                blocks_ref[k, at, 0:mine] = gram[mine * k : mine * (k + 1)]
         ix, iy = lax.axis_index("gx"), lax.axis_index("gy")
         sx, sy = lax.axis_size("gx"), lax.axis_size("gy")
         own = shares[0:nco]
@@ -449,8 +455,7 @@
         ]
 
         def put(target, rows):
-            for r in range(nco):
-                blocks_ref[target, mine + 1 + r] = rows[r : r + 1]
+            blocks_ref[target, 2, 0:nco] = rows
 
         for target, rows, flag in targets:
             if flag is None:
@@ -460,41 +465,57 @@
 
     outs = call(
         first_direction,
-        [(field, F32), (field, F32), ((devices, packed, 1, cols), F32)] + [face_out] * nrounds,
+        [(field, F32), (field, F32), (block_shape, F32)] + [face_out] * nrounds,
     )(*got_b, part, coarse, bases, schur_here, first_part)
     direction, image, blocks = outs[:3]
     got_d = trade(fill(outs[3:]))
     blocks = lax.all_to_all(blocks, AXES, 0, 0)
-    joint = 8 * -(-(mine + nco) // 8)
-
-    def first_sums(blocks_ref, sum_ref, mine_ref, diag_ref):
+
+    groups = 4 if devices % 4 == 0 else 1
+
+    def first_sums(blocks_ref, sum_hbm, mine_ref, sum_ref, sems):
         total = jnp.sum(blocks_ref[...], axis=0)
-        diag_ref[...] = total[mine]
-        coarse_image = [total[mine + 1 + r] for r in range(nco)]
-        mine_ref[...] = jnp.concatenate(coarse_image, axis=0)
-        rows = [total[r] for r in range(mine)] + coarse_image
-        if mine + nco < joint:
-            rows.append(jnp.zeros((joint - mine - nco, cols), F32))
-        sum_ref[...] = jnp.broadcast_to(jnp.concatenate(rows, axis=0)[None], sum_ref.shape)
-
-    sums, coarse_image, diagonal = call(
+        mine_ref[...] = total[2, 0:nco]
+        sum_ref[...] = jnp.broadcast_to(total[None], sum_ref.shape)
+        copies = [
+            pltpu.make_async_copy(
+                sum_ref, sum_hbm.at[pl.ds(devices // groups * k, devices // groups)], sems.at[k]
+            )
+            for k in range(groups)
+        ]
+        for copy in copies:
+            copy.start()
+        for copy in copies:
+            copy.wait()
+
+    sums, coarse_image = call(
         first_sums,
-        [((devices, joint, cols), F32), ((nco, cols), F32), ((1, cols), F32)],
+        [(block_shape, F32), ((nco, cols), F32)],
+        [((devices // groups, 3, tall, cols), F32)],
+        copies=groups,
+        far_outs=(0,),
     )(blocks)
     sums = lax.all_to_all(sums, AXES, 0, 0)
 
-    def first_step(sums_ref, diag_ref, curv_ref, first_ref, step_ref, work_ref):
-        both = jnp.concatenate([sums_ref[k, 0:mine, :] for k in range(packers)], axis=0)
-        turned = both.T
-        above, on = triangles()
-        curvature = jnp.where(above, both, jnp.where(on, diag_ref[...], turned))
-        first = jnp.where(above, turned, both)
-        step_ref[...] = solve(curvature, first, work_ref, (), 5)
+    def gathered(ref, at, rows, blocks):
+        return jnp.concatenate([ref[k, at, 0:rows] for k in range(blocks)], axis=0)
+
+    def first_step(sums_ref, raw_ref, curv_ref, first_ref, step_ref, work_ref):
+        raw = gathered(sums_ref, 0, mine, packers)
+        curvature = 0.5 * (raw + raw.T)
+        first = gathered(sums_ref, 1, mine, packers)
+        raw_ref[...] = raw
         curv_ref[...] = curvature
         first_ref[...] = first
-
-    curvature, first, step = call(first_step, [(gram_shape, F32)] * 3, work, flops=2 * 12 * cols**3)(
-        sums, diagonal
+        step, good, resume = solve(curvature, first, work_ref, (1.33,), 4, 2)
+        step_ref[...] = step
+
+        @pl.when(jnp.logical_not(good))
+        def _():
+            step_ref[...] = resume()
+
+    raw_curvature, curvature, first, step = call(first_step, [(gram_shape, F32)] * 4, work, flops=2 * 12 * cols**3)(
+        sums
     )
 
     def second_local(*refs):
@@ -520,25 +541,34 @@
 
     def second_coarse(
         sums_ref, table_ref, values_ref, mine_ref, image_ref, step_ref, scaled_ref, product_ref,
-        first_ref, curv_ref, next_ref, values_out, inv_ref, quad_ref, work_ref
+        first_ref, curv_ref, raw_ref, next_ref, values_out, inv_ref, quad_ref, mend_ref, work_ref
     ):
-        rows = jnp.concatenate([sums_ref[k, mine : mine + nco, :] for k in range(devices)], axis=0)
+        rows = gathered(sums_ref, 2, nco, devices)
         step = step_ref[...]
         values_now = values_ref[...] - dot(dot(table_ref[...], rows), step)
         values_out[...] = values_now
-        own = mine_ref[0] - dot(image_ref[...], step)
+        own = mine_ref[...] - dot(image_ref[...], step)
         next_ref[...] = gram_dot(scaled_ref[...], product_ref[...]) + dot(own, values_now[:nco], 0, 0)
-        _, on = triangles()
-        inverse = solve(first_ref[...], on.astype(F32), work_ref, (), 4)
-        inv_ref[...] = inverse
-        quad_ref[...] = dot(inverse, deep_dot(curv_ref[...], inverse), 0, 0)
-
-    next_part, values, first_inverse, quad = call(
+        first, curvature = first_ref[...], curv_ref[...]
+        mend_ref[...] = 2.0 * (first.T - deep_dot(raw_ref[...], step))
+        inverse, good, resume = solve(0.5 * (first + first.T), identity(), work_ref, (), 4, 1)
+
+        def keep(inverse):
+            inv_ref[...] = inverse
+            quad_ref[...] = deep_dot(deep_dot(inverse, curvature), inverse)
+
+        keep(inverse)
+
+        @pl.when(jnp.logical_not(good))
+        def _():
+            keep(resume())
+
+    next_part, values, first_inverse, quad, mend = call(
         second_coarse,
-        [(gram_shape, F32), ((8 * nco, cols), F32), (gram_shape, F32), (gram_shape, F32)],
+        [(gram_shape, F32), ((8 * nco, cols), F32)] + [(gram_shape, F32)] * 3,
         work,
         flops=2 * 12 * unknowns * cols**2,
-    )(sums, table, values, coarse_input, coarse_image, step, scaled, product, first, curvature)
+    )(sums, table, values, coarse_mine, coarse_image, step, scaled, product, first, curvature, raw_curvature)
 
     per = 8 * -(-2 * cols // (8 * devices))
     blocks_out = ((devices, per, cols), F32)
@@ -568,29 +598,29 @@
     sums = lax.all_to_all(sums, AXES, 0, 0).reshape(devices * per, cols)
 
     def finish(
-        sums_ref, inv_ref, quad_ref, step_ref, dir_ref, update_ref, out_hbm, work_ref, rows_ref, sems
+        sums_ref, inv_ref, quad_ref, mend_ref, step_ref, dir_ref, update_ref, out_ref, work_ref
     ):
         next_gram, square = sums_ref[0:cols], sums_ref[cols : 2 * cols]
-        square = 0.5 * (square + square.T)
-        curvature = square - dot(next_gram, deep_dot(quad_ref[...], next_gram), 0, 0)
         ratio = deep_dot(inv_ref[...], next_gram)
-        step = solve(curvature, next_gram, work_ref, (1.8, 1.8, 1.5), 7)
-        total = step_ref[...] + deep_dot(ratio, step)
-        p, q, _ = thirds(jnp.concatenate([total, step], axis=0))
-        copies = []
-        for f in range(4):
-            here = pl.ds(face * f, face)
-            a, b, _ = thirds(jnp.concatenate([dir_ref[here], update_ref[here]], axis=1))
-            rows_ref[here] = plain(a, p) + (plain(a, q) + plain(b, p))
-            copies.append(
-                pltpu.make_async_copy(rows_ref.at[here], out_hbm.at[here], sems.at[f])
-            )
-            copies[-1].start()
-        for copy in copies:
-            copy.wait()
-
-    (solved,) = call(finish, [(field, F32)], work + [(field, F32)], copies=4, far_out=True)(
-        sums, first_inverse, quad, step, direction, update
+        reduced = square - dot(next_gram, deep_dot(quad_ref[...], next_gram - mend_ref[...]), 0, 0)
+        curvature = 0.5 * (reduced + reduced.T)
+        step, good, resume = solve(curvature, next_gram, work_ref, (1.8, 1.8, 1.5, 1.14), 6, 2)
+
+        def write(step):
+            total = step_ref[...] + deep_dot(ratio, step)
+            p, q, _ = thirds(jnp.concatenate([total, step], axis=0))
+            a, b, _ = thirds(jnp.concatenate([dir_ref[...], update_ref[...]], axis=1))
+            pair = plain(a, jnp.concatenate([p, q], axis=1))
+            out_ref[...] = pair[:, :cols] + (pair[:, cols:] + plain(b, p))
+
+        write(step)
+
+        @pl.when(jnp.logical_not(good))
+        def _():
+            write(resume())
+
+    (solved,) = call(finish, [(field, F32)], work)(
+        sums, first_inverse, quad, mend, step, direction, update
     )
     return solved[None, None]
 

time: 86.9 us -> 88.9 us (1.023)
  waiting for transfers between devices: 6.07 us -> 8.33 us
    ppermute x12, waiting for transfers between devices: 1.15 us -> 2.86 us  [exchange(): got.append(lax.ppermute(piece, axis, pairs) if pairs else None)]
  transfers between devices with their start and end apart: 14 -> 14, of which waited for: 4 -> 5; matrix products, arithmetic and copies ran while one was open for 0% -> 0% of each run, Pallas kernels for 10% -> 8%
where the time goes in v5:
time: 88.9 us; the launch traced here: 88.8 us
  blocking collectives  34.7 us (39%)
  starting transfers between devices  28.7 us (32%)
  Pallas kernels  16.8 us (19%)
  waiting for transfers between devices  8.33 us (9%)
    all_to_all x2, blocking collectives, local(): blocks = lax.all_to_all(blocks, AXES, 0, 0)  24.7 us
    ppermute x12, starting transfers between devices, exchange(): got.append(lax.ppermute(piece, axis, pairs) if pairs else None)  21.2 us
    pallas_call x13, Pallas kernels, run(): kernel_call(body, outs, scratch, flops, moved, sems, specs, results)(*args)  16.8 us
    all_to_all x1, blocking collectives, local(): sums = lax.all_to_all(sums, AXES, 0, 0).reshape(devices * per, cols)  10 us
    all_to_all x1, starting transfers between devices, local(): lax.all_to_all(coarse_input, AXES, 0, 0).reshape(coarse_all, cols)  4.84 us
    all_to_all x1, waiting for transfers between devices, local(): sums = lax.all_to_all(sums, AXES, 0, 0)  3.67 us
    ppermute x12, waiting for transfers between devices, exchange(): got.append(lax.ppermute(piece, axis, pairs) if pairs else None)  2.86 us
    all_to_all x1, starting transfers between devices, local(): sums = lax.all_to_all(sums, AXES, 0, 0)  2.72 us
  transfers between devices with their start and end apart: 14, of which 5 were waited for; matrix products, arithmetic and copies ran while one was open for 0% of the time, Pallas kernels for 8%

profile of v5, /device:TPU:0, one launch (start us, length us, event | category | flops | bytes accessed | tf_op | source)
XLA Modules:
  0.0 88.8 jit_solution(420135682746894776)
XLA Ops:
  0.0 1.0 %shard_map.64 = (f32[512,128]{1,0:T(8,128)S(1)}, f32[4,512]{1,0:T(4,128)S(1)}, f32[4,128]{1,0:T(4,128)S(1)}, s32[1,512]{1,0:T(1,128)S(1)}, f32[136,128]{1,0:T(8,...) custom-call(bf16[512,128]{1,0:T(8,128)(2,1)} %bitcast.11, f32[4,512]{1,0:T(4,128)} %bitcast.12, ...), custom_call_target="tpu_custom_call" | custom-call | tf_op jit(solution)/shard_map/pallas_call | solution.py:75
  1.0 0.7 collective-permute-start
  1.7 5.7 %collective-permute-start.1 = (f32[136,128]{1,0:T(8,128)S(1)}, f32[136,128]{1,0:T(8,128)S(1)}, u32[]{:S(2)}, u32[]{:S(2)}) collective-permute-start(f32[136,128]{1,0:T(8,128)S(1)} %get-tuple-element.56), channel_id=1, source_target_pairs={{0,2},{4,6},{8,10},{12,14},{16,18},{20,22},{24,26},{28,30},{2,0},{... | collective-permute-start | bytes 208904 | tf_op jit(solution)/shard_map/ppermute | solution.py:102
  7.4 0.0 collective-permute-start.2
  7.4 2.5 %shard_map.65 = (bf16[512,512]{1,0:T(8,128)(2,1)S(1)}, bf16[512,512]{1,0:T(8,128)(2,1)S(1)}) custom-call(bf16[512,512]{1,0:T(8,128)(2,1)} %bitcast.15, bf16[512,512]{1,0:T(8,128)(2,1)} %bitcast.16, s32[1,512]{1,0:T(1,128)S(1)} %get-tuple-element.59.map_ref), custom_call_target="tpu_custom_call" | custom-call | flops 1073741824 | bytes 2097152 | tf_op jit(solution)/shard_map/pallas_call | solution.py:75
  9.9 0.0 collective-permute-done.refs_0_
  9.9 0.8 collective-permute-done.1.refs_1_
  10.7 0.0 collective-permute-done.2.refs_2_
  10.7 0.9 %shard_map.66 = (f32[512,128]{1,0:T(8,128)S(1)}, f32[512,128]{1,0:T(8,128)S(1)}, f32[512,128]{1,0:T(8,128)S(1)}, f32[512,128]{1,0:T(8,128)S(1)}, f32[4,128]{1,0:...) custom-call(f32[136,128]{1,0:T(8,128)S(1)} %collective-permute-done., ...), custom_call_target="tpu_custom_call" | custom-call | tf_op jit(solution)/shard_map/pallas_call | solution.py:75
  11.6 4.8 %all-to-all-start = ((f32[32,4,128]{2,1,0:T(4,128)}), f32[32,4,128]{2,1,0:T(4,128)S(1)}, u32[]{:S(2)}, u32[]{:S(2)}) async-start(f32[32,4,128]{2,1,0:T(4,128)} %get-tuple-element.66), calls=%async_computation | async-start | bytes 131072 | tf_op jit(solution)/shard_map/all_to_all | solution.py:352
  16.5 0.7 collective-permute-start.3
  17.2 4.5 %collective-permute-start.4 = (f32[128,128]{1,0:T(8,128)S(1)}, f32[128,128]{1,0:T(8,128)S(1)}, u32[]{:S(2)}, u32[]{:S(2)}) collective-permute-start(f32[128,128]{1,0:T(8,128)S(1)} %get-tuple-element.63), channel_id=1, source_target_pairs={{0,2},{4,6},{8,10},{12,14},{16,18},{20,22},{24,26},{28,30},{2,0},{... | collective-permute-start | bytes 196616 | tf_op jit(solution)/shard_map/ppermute | solution.py:102
  21.7 0.0 collective-permute-start.5
  21.7 0.4 shard_map.67
  22.1 1.8 %all-to-all-done = f32[32,4,128]{2,1,0:T(4,128)S(1)} async-done(((f32[32,4,128]{2,1,0:T(4,128)}), f32[32,4,128]{2,1,0:T(4,128)S(1)}, u32[]{:S(2)}, u32[]{:S(2)}) %all-to-all-start) | async-done | bytes 65568 | tf_op jit(solution)/shard_map/all_to_all | solution.py:352
  23.9 0.4 shard_map.68
  24.3 0.0 collective-permute-done.3.refs_0_
  24.4 0.9 %collective-permute-done.4.refs_1_ = f32[128,128]{1,0:T(8,128)S(1)} collective-permute-done((f32[128,128]{1,0:T(8,128)S(1)}, f32[128,128]{1,0:T(8,128)S(1)}, u32[]{:S(2)}, u32[]{:S(2)}) %collective-permute-start.4) | collective-permute-done | bytes 65568 | tf_op jit(solution)/shard_map/ppermute | solution.py:102
  25.3 0.0 collective-permute-done.5.refs_2_
  25.3 0.7 shard_map.69
  25.9 13.2 %all_to_all.25.blocks_ref = f32[32,3,4,128]{3,2,1,0:T(4,128)S(1)} all-to-all(f32[32,3,4,128]{3,2,1,0:T(4,128)S(1)} %get-tuple-element.81), channel_id=1, replica_groups=mesh['gx'=16,'gy'=2] {'gx','gy'}, dimensions={0} | all-to-all | bytes 393216 | tf_op jit(solution)/shard_map/all_to_all | solution.py:472
  39.1 0.8 shard_map.70
  39.9 2.7 %all-to-all-start.2 = ((f32[32,3,4,128]{3,2,1,0:T(4,128)}), f32[32,3,4,128]{3,2,1,0:T(4,128)S(1)}, u32[]{:S(2)}, u32[]{:S(2)}) async-start(f32[32,3,4,128]{3,2,1,0:T(4,128)} %get-tuple-element.82), calls=%async_computation.2 | async-start | bytes 393216 | tf_op jit(solution)/shard_map/all_to_all | solution.py:498
  42.6 0.7 collective-permute-start.6
  43.3 4.5 %collective-permute-start.7 = (f32[128,128]{1,0:T(8,128)S(1)}, f32[128,128]{1,0:T(8,128)S(1)}, u32[]{:S(2)}, u32[]{:S(2)}) collective-permute-start(f32[128,128]{1,0:T(8,128)S(1)} %get-tuple-element.79), channel_id=1, source_target_pairs={{0,2},{4,6},{8,10},{12,14},{16,18},{20,22},{24,26},{28,30},{2,0},{... | collective-permute-start | bytes 196616 | tf_op jit(solution)/shard_map/ppermute | solution.py:102
  47.8 0.0 collective-permute-start.8
  47.8 3.7 %all-to-all-done.2.sums_ref = f32[32,3,4,128]{3,2,1,0:T(4,128)S(1)} async-done(((f32[32,3,4,128]{3,2,1,0:T(4,128)}), f32[32,3,4,128]{3,2,1,0:T(4,128)S(1)}, u32[]{:S(2)}, u32[]{:S(2)}) %all-to-all-start.2) | async-done | bytes 196640 | tf_op jit(solution)/shard_map/all_to_all | solution.py:498
  51.5 2.1 %shard_map.71 = (f32[128,128]{1,0:T(8,128)S(1)}, f32[128,128]{1,0:T(8,128)S(1)}, f32[128,128]{1,0:T(8,128)S(1)}, f32[128,128]{1,0:T(8,128)S(1)}) custom-call(f32[32,3,4,128]{3,2,1,0:T(4,128)S(1)} %all-to-all-done.2.sums_ref), custom_call_target="tpu_custom_call" | custom-call | flops 50331648 | tf_op jit(solution)/shard_map/pallas_call | solution.py:75
  53.5 0.0 collective-permute-done.6.refs_0_
  53.6 0.0 collective-permute-done.7.refs_1_
  53.6 0.0 collective-permute-done.8.refs_2_
  53.6 0.8 shard_map.72
  54.4 0.7 collective-permute-start.9
  55.1 3.7 %collective-permute-start.10 = (f32[128,128]{1,0:T(8,128)S(1)}, f32[128,128]{1,0:T(8,128)S(1)}, u32[]{:S(2)}, u32[]{:S(2)}) collective-permute-start(f32[128,128]{1,0:T(8,128)S(1)} %get-tuple-element.87), channel_id=1, source_target_pairs={{0,2},{4,6},{8,10},{12,14},{16,18},{20,22},{24,26},{28,30},{2,0},{... | collective-permute-start | bytes 196616 | tf_op jit(solution)/shard_map/ppermute | solution.py:102
  58.8 0.0 collective-permute-start.11
  58.8 1.8 %shard_map.73 = (f32[128,128]{1,0:T(8,128)S(1)}, f32[32,128]{1,0:T(8,128)S(1)}, f32[128,128]{1,0:T(8,128)S(1)}, f32[128,128]{1,0:T(8,128)S(1)}, f32[128,128]{1,0:T(8,128)S(1)}) custom-call(f32[32,3,4,128]{3,2,1,0:T(4,128)S(1)} %all-to-all-done.2.sums_ref, f32[32,128]{1,0:T(8,128)S(1)} %get-tuple-element.71.table_ref, ...), custom_call_target="tpu_custom_call" | custom-call | flops 201326592 | tf_op jit(solution)/shard_map/pallas_call | solution.py:75
  60.6 0.0 collective-permute-done.9.refs_0_
  60.6 1.1 %collective-permute-done.10.refs_1_ = f32[128,128]{1,0:T(8,128)S(1)} collective-permute-done((f32[128,128]{1,0:T(8,128)S(1)}, f32[128,128]{1,0:T(8,128)S(1)}, u32[]{:S(2)}, u32[]{:S(2)}) %collective-permute-start.10) | collective-permute-done | bytes 65568 | tf_op jit(solution)/shard_map/ppermute | solution.py:102
  61.8 0.0 collective-permute-done.11.refs_2_
  61.8 0.8 shard_map.74
  62.6 11.5 %all_to_all.26.blocks_ref = f32[32,8,128]{2,1,0:T(8,128)S(1)} all-to-all(f32[32,8,128]{2,1,0:T(8,128)S(1)} %get-tuple-element.99), channel_id=1, replica_groups=mesh['gx'=16,'gy'=2] {'gx','gy'}, dimensions={0} | all-to-all | bytes 262144 | tf_op jit(solution)/shard_map/all_to_all | solution.py:592
  74.2 10.0 %all_to_all.27 = f32[32,8,128]{2,1,0:T(8,128)S(1)} all-to-all(f32[32,8,128]{2,1,0:T(8,128)S(1)} %shard_map.75), channel_id=1, replica_groups=mesh['gx'=16,'gy'=2] {'gx','gy'}, dimensions={0} | all-to-all | bytes 262144 | tf_op jit(solution)/shard_map/all_to_all | solution.py:598
  84.2 4.6 %shard_map.76 = f32[512,128]{1,0:T(8,128)} custom-call(f32[256,128]{1,0:T(8,128)S(1)} %bitcast.9, f32[128,128]{1,0:T(8,128)S(1)} %get-tuple-element.100.inv_ref, f32[128,128]{1,0:T(8,128)S(1)} %get-tuple-element.101.quad_ref, f32[128,128]{1,0:T(8,128)S(1)} %get-tuple-element.102.mend_ref, f32[128,128]{1,0:T(8,128)S(1)} %get-tuple-element.83.refs_3_.step_ref, ...), custom_call_target="tpu_custom_call" | custom-call | tf_op jit(solution)/shard_map/pallas_call | solution.py:75
  (1 shorter events, 0.0 us)
Async XLA Ops:
  1.0 8.9 %collective-permute-start = (f32[136,128]{1,0:T(8,128)S(1)}, f32[136,128]{1,0:T(8,128)S(1)}, u32[]{:S(2)}, u32[]{:S(2)}) collective-permute-start(f32[136,128]{1,0:T(8,128)S(1)} %get-tuple-element.55), channel_id=1, source_target_pairs={{2,4},{6,8},{10,12},{14,16},{18,20},{22,24},{26,28},{4,2},{8,6},{1... | collective-permute-start | bytes 208904 | tf_op jit(solution)/shard_map/ppermute | solution.py:102
  1.7 9.0 %collective-permute-start.1 = (f32[136,128]{1,0:T(8,128)S(1)}, f32[136,128]{1,0:T(8,128)S(1)}, u32[]{:S(2)}, u32[]{:S(2)}) collective-permute-start(f32[136,128]{1,0:T(8,128)S(1)} %get-tuple-element.56), channel_id=1, source_target_pairs={{0,2},{4,6},{8,10},{12,14},{16,18},{20,22},{24,26},{28,30},{2,0},{... | collective-permute-start | bytes 208904 | tf_op jit(solution)/shard_map/ppermute | solution.py:102
  7.4 3.3 %collective-permute-start.2 = (f32[136,128]{1,0:T(8,128)S(1)}, f32[136,128]{1,0:T(8,128)S(1)}, u32[]{:S(2)}, u32[]{:S(2)}) collective-permute-start(f32[136,128]{1,0:T(8,128)S(1)} %get-tuple-element.57), channel_id=1, source_target_pairs={{0,1},{1,0},{2,3},{3,2},{4,5},{5,4},{6,7},{7,6},{8,9},{9,8},{10,11... | collective-permute-start | bytes 208904 | tf_op jit(solution)/shard_map/ppermute | solution.py:102
  11.6 12.3 %all-to-all-start = ((f32[32,4,128]{2,1,0:T(4,128)}), f32[32,4,128]{2,1,0:T(4,128)S(1)}, u32[]{:S(2)}, u32[]{:S(2)}) async-start(f32[32,4,128]{2,1,0:T(4,128)} %get-tuple-element.66), calls=%async_computation | async-start | bytes 131072 | tf_op jit(solution)/shard_map/all_to_all | solution.py:352
  16.5 7.9 %collective-permute-start.3 = (f32[128,128]{1,0:T(8,128)S(1)}, f32[128,128]{1,0:T(8,128)S(1)}, u32[]{:S(2)}, u32[]{:S(2)}) collective-permute-start(f32[128,128]{1,0:T(8,128)S(1)} %get-tuple-element.62), channel_id=1, source_target_pairs={{2,4},{6,8},{10,12},{14,16},{18,20},{22,24},{26,28},{4,2},{8,6},{1... | collective-permute-start | bytes 196616 | tf_op jit(solution)/shard_map/ppermute | solution.py:102
  17.2 8.1 %collective-permute-start.4 = (f32[128,128]{1,0:T(8,128)S(1)}, f32[128,128]{1,0:T(8,128)S(1)}, u32[]{:S(2)}, u32[]{:S(2)}) collective-permute-start(f32[128,128]{1,0:T(8,128)S(1)} %get-tuple-element.63), channel_id=1, source_target_pairs={{0,2},{4,6},{8,10},{12,14},{16,18},{20,22},{24,26},{28,30},{2,0},{... | collective-permute-start | bytes 196616 | tf_op jit(solution)/shard_map/ppermute | solution.py:102
  21.7 3.6 %collective-permute-start.5 = (f32[128,128]{1,0:T(8,128)S(1)}, f32[128,128]{1,0:T(8,128)S(1)}, u32[]{:S(2)}, u32[]{:S(2)}) collective-permute-start(f32[128,128]{1,0:T(8,128)S(1)} %get-tuple-element.64), channel_id=1, source_target_pairs={{0,1},{1,0},{2,3},{3,2},{4,5},{5,4},{6,7},{7,6},{8,9},{9,8},{10,11... | collective-permute-start | bytes 196616 | tf_op jit(solution)/shard_map/ppermute | solution.py:102
  39.9 11.6 %all-to-all-start.2 = ((f32[32,3,4,128]{3,2,1,0:T(4,128)}), f32[32,3,4,128]{3,2,1,0:T(4,128)S(1)}, u32[]{:S(2)}, u32[]{:S(2)}) async-start(f32[32,3,4,128]{3,2,1,0:T(4,128)} %get-tuple-element.82), calls=%async_computation.2 | async-start | bytes 393216 | tf_op jit(solution)/shard_map/all_to_all | solution.py:498
  42.6 11.0 %collective-permute-start.6 = (f32[128,128]{1,0:T(8,128)S(1)}, f32[128,128]{1,0:T(8,128)S(1)}, u32[]{:S(2)}, u32[]{:S(2)}) collective-permute-start(f32[128,128]{1,0:T(8,128)S(1)} %get-tuple-element.78), channel_id=1, source_target_pairs={{2,4},{6,8},{10,12},{14,16},{18,20},{22,24},{26,28},{4,2},{8,6},{1... | collective-permute-start | bytes 196616 | tf_op jit(solution)/shard_map/ppermute | solution.py:102
  43.3 10.3 %collective-permute-start.7 = (f32[128,128]{1,0:T(8,128)S(1)}, f32[128,128]{1,0:T(8,128)S(1)}, u32[]{:S(2)}, u32[]{:S(2)}) collective-permute-start(f32[128,128]{1,0:T(8,128)S(1)} %get-tuple-element.79), channel_id=1, source_target_pairs={{0,2},{4,6},{8,10},{12,14},{16,18},{20,22},{24,26},{28,30},{2,0},{... | collective-permute-start | bytes 196616 | tf_op jit(solution)/shard_map/ppermute | solution.py:102
  47.8 5.8 %collective-permute-start.8 = (f32[128,128]{1,0:T(8,128)S(1)}, f32[128,128]{1,0:T(8,128)S(1)}, u32[]{:S(2)}, u32[]{:S(2)}) collective-permute-start(f32[128,128]{1,0:T(8,128)S(1)} %get-tuple-element.80), channel_id=1, source_target_pairs={{0,1},{1,0},{2,3},{3,2},{4,5},{5,4},{6,7},{7,6},{8,9},{9,8},{10,11... | collective-permute-start | bytes 196616 | tf_op jit(solution)/shard_map/ppermute | solution.py:102
  54.4 6.2 %collective-permute-start.9 = (f32[128,128]{1,0:T(8,128)S(1)}, f32[128,128]{1,0:T(8,128)S(1)}, u32[]{:S(2)}, u32[]{:S(2)}) collective-permute-start(f32[128,128]{1,0:T(8,128)S(1)} %get-tuple-element.86), channel_id=1, source_target_pairs={{2,4},{6,8},{10,12},{14,16},{18,20},{22,24},{26,28},{4,2},{8,6},{1... | collective-permute-start | bytes 196616 | tf_op jit(solution)/shard_map/ppermute | solution.py:102
  55.1 6.7 %collective-permute-start.10 = (f32[128,128]{1,0:T(8,128)S(1)}, f32[128,128]{1,0:T(8,128)S(1)}, u32[]{:S(2)}, u32[]{:S(2)}) collective-permute-start(f32[128,128]{1,0:T(8,128)S(1)} %get-tuple-element.87), channel_id=1, source_target_pairs={{0,2},{4,6},{8,10},{12,14},{16,18},{20,22},{24,26},{28,30},{2,0},{... | collective-permute-start | bytes 196616 | tf_op jit(solution)/shard_map/ppermute | solution.py:102
  58.8 3.0 %collective-permute-start.11 = (f32[128,128]{1,0:T(8,128)S(1)}, f32[128,128]{1,0:T(8,128)S(1)}, u32[]{:S(2)}, u32[]{:S(2)}) collective-permute-start(f32[128,128]{1,0:T(8,128)S(1)} %get-tuple-element.88), channel_id=1, source_target_pairs={{0,1},{1,0},{2,3},{3,2},{4,5},{5,4},{6,7},{7,6},{8,9},{9,8},{10,11... | collective-permute-start | bytes 196616 | tf_op jit(solution)/shard_map/ppermute | solution.py:102

commit v6 on v5

--- a/solution.py
+++ b/solution.py
@@ -183,7 +183,8 @@
     unit = matrix * by_row * by_col
     bound = jnp.max(jnp.sum(jnp.abs(unit), axis=0, keepdims=True), axis=1, keepdims=True)
     scale = 1.9 / bound
-    answer = right * (by_row * scale)
+    right = right * by_row
+    answer = right * scale
     power = eye - scale * unit
 
     def step(answer, power, product=deep_dot):
@@ -196,21 +197,27 @@
             answer = boosts[k] * answer
 
     def resume():
-        work_ref[:, 0:size] = answer
-        work_ref[:, size:] = power
+        work_ref[:, 2 * size :] = jnp.zeros((size, size), F32)
 
         def again(carry):
-            answer, power = step(work_ref[:, 0:size], work_ref[:, size:])
+            answer, power = step(work_ref[:, 0:size], work_ref[:, size : 2 * size])
             work_ref[:, 0:size] = answer
-            work_ref[:, size:] = power
+            work_ref[:, size : 2 * size] = power
             return carry[0] + 1, jnp.max(jnp.abs(power))
 
-        lax.while_loop(
-            lambda carry: jnp.logical_and(carry[0] < 40, carry[1] > 1e-7),
-            again,
-            (jnp.int32(0), jnp.float32(1.0)),
-        )
-        return work_ref[:, 0:size] * by_row
+        def refine(_, carry):
+            work_ref[:, 0:size] = (right - deep_dot(unit, work_ref[:, 2 * size :])) * scale
+            work_ref[:, size : 2 * size] = eye - scale * unit
+            lax.while_loop(
+                lambda carry: jnp.logical_and(carry[0] < 40, carry[1] > 1e-7),
+                again,
+                (jnp.int32(0), jnp.float32(1.0)),
+            )
+            work_ref[:, 2 * size :] = work_ref[:, 2 * size :] + work_ref[:, 0:size]
+            return carry
+
+        lax.fori_loop(0, 3, refine, jnp.int32(0))
+        return work_ref[:, 2 * size :] * by_row
 
     good = jnp.sum(power * power) < 1e-4
     return (answer + deep_dot(power, answer)) * by_row, good, resume
@@ -227,7 +234,7 @@
     used = rounds_used()
     field = (unknowns, cols)
     gram_shape = (cols, cols)
-    work = [((cols, 2 * cols), F32)]
+    work = [((cols, 3 * cols), F32)]
     face_out = ((face, cols), F32)
 
     def give(refs, faces):
@@ -507,7 +514,7 @@
         raw_ref[...] = raw
         curv_ref[...] = curvature
         first_ref[...] = first
-        step, good, resume = solve(curvature, first, work_ref, (1.33,), 4, 2)
+        step, good, resume = solve(curvature, first, work_ref, (1.33,), 4, 4)
         step_ref[...] = step
 
         @pl.when(jnp.logical_not(good))

time: 88.9 us -> 101 us (1.14)
  Pallas kernels: 16.8 us -> 28.7 us
    pallas_call x13, Pallas kernels: 16.8 us -> 28.7 us  [run(): kernel_call(body, outs, scratch, flops, moved, sems, specs, results)(*args)]
  transfers between devices with their start and end apart: 14 -> 14, of which waited for: 5 -> 5; matrix products, arithmetic and copies ran while one was open for 0% -> 0% of each run, Pallas kernels for 8% -> 6%
where the time goes in v6:
time: 101 us
  blocking collectives  34.9 us (35%)
  Pallas kernels  28.7 us (28%)
  starting transfers between devices  28.7 us (28%)
  waiting for transfers between devices  8.33 us (8%)
    pallas_call x13, Pallas kernels, run(): kernel_call(body, outs, scratch, flops, moved, sems, specs, results)(*args)  28.7 us
    all_to_all x2, blocking collectives, local(): blocks = lax.all_to_all(blocks, AXES, 0, 0)  24.9 us
    ppermute x12, starting transfers between devices, exchange(): got.append(lax.ppermute(piece, axis, pairs) if pairs else None)  21.2 us
    all_to_all x1, blocking collectives, local(): sums = lax.all_to_all(sums, AXES, 0, 0).reshape(devices * per, cols)  10 us
    all_to_all x1, starting transfers between devices, local(): lax.all_to_all(coarse_input, AXES, 0, 0).reshape(coarse_all, cols)  4.84 us
    all_to_all x1, waiting for transfers between devices, local(): sums = lax.all_to_all(sums, AXES, 0, 0)  3.67 us
    ppermute x12, waiting for transfers between devices, exchange(): got.append(lax.ppermute(piece, axis, pairs) if pairs else None)  2.86 us
    all_to_all x1, starting transfers between devices, local(): sums = lax.all_to_all(sums, AXES, 0, 0)  2.72 us
  transfers between devices with their start and end apart: 14, of which 5 were waited for; matrix products, arithmetic and copies ran while one was open for 0% of the time, Pallas kernels for 6%

profile of v6, /device:TPU:0, one launch (start us, length us, event | category | flops | bytes accessed | tf_op | source)
XLA Modules:
  0.0 100.8 jit_solution(1410867949571029005)
XLA Ops:
  0.0 1.0 shard_map.64
  1.0 0.7 collective-permute-start
  1.7 5.7 %collective-permute-start.1 = (f32[136,128]{1,0:T(8,128)S(1)}, f32[136,128]{1,0:T(8,128)S(1)}, u32[]{:S(2)}, u32[]{:S(2)}) collective-permute-start(f32[136,128]{1,0:T(8,128)S(1)} %get-tuple-element.56), channel_id=1, source_target_pairs={{0,2},{4,6},{8,10},{12,14},{16,18},{20,22},{24,26},{28,30},{2,0},{... | collective-permute-start | bytes 208904 | tf_op jit(solution)/shard_map/ppermute | solution.py:102
  7.4 0.0 collective-permute-start.2
  7.4 2.5 %shard_map.65 = (bf16[512,512]{1,0:T(8,128)(2,1)S(1)}, bf16[512,512]{1,0:T(8,128)(2,1)S(1)}) custom-call(bf16[512,512]{1,0:T(8,128)(2,1)} %bitcast.15, bf16[512,512]{1,0:T(8,128)(2,1)} %bitcast.16, s32[1,512]{1,0:T(1,128)S(1)} %get-tuple-element.59.map_ref), custom_call_target="tpu_custom_call" | custom-call | flops 1073741824 | bytes 2097152 | tf_op jit(solution)/shard_map/pallas_call | solution.py:75
  9.9 0.0 collective-permute-done.refs_0_
  9.9 0.8 collective-permute-done.1.refs_1_
  10.7 0.0 collective-permute-done.2.refs_2_
  10.7 0.9 shard_map.66
  11.6 4.8 %all-to-all-start = ((f32[32,4,128]{2,1,0:T(4,128)}), f32[32,4,128]{2,1,0:T(4,128)S(1)}, u32[]{:S(2)}, u32[]{:S(2)}) async-start(f32[32,4,128]{2,1,0:T(4,128)} %get-tuple-element.66), calls=%async_computation | async-start | bytes 131072 | tf_op jit(solution)/shard_map/all_to_all | solution.py:359
  16.5 0.7 collective-permute-start.3
  17.2 4.5 %collective-permute-start.4 = (f32[128,128]{1,0:T(8,128)S(1)}, f32[128,128]{1,0:T(8,128)S(1)}, u32[]{:S(2)}, u32[]{:S(2)}) collective-permute-start(f32[128,128]{1,0:T(8,128)S(1)} %get-tuple-element.63), channel_id=1, source_target_pairs={{0,2},{4,6},{8,10},{12,14},{16,18},{20,22},{24,26},{28,30},{2,0},{... | collective-permute-start | bytes 196616 | tf_op jit(solution)/shard_map/ppermute | solution.py:102
  21.7 0.0 collective-permute-start.5
  21.7 0.4 shard_map.67
  22.1 1.8 %all-to-all-done = f32[32,4,128]{2,1,0:T(4,128)S(1)} async-done(((f32[32,4,128]{2,1,0:T(4,128)}), f32[32,4,128]{2,1,0:T(4,128)S(1)}, u32[]{:S(2)}, u32[]{:S(2)}) %all-to-all-start) | async-done | bytes 65568 | tf_op jit(solution)/shard_map/all_to_all | solution.py:359
  23.9 0.4 shard_map.68
  24.3 0.0 collective-permute-done.3.refs_0_
  24.4 0.9 collective-permute-done.4.refs_1_
  25.3 0.0 collective-permute-done.5.refs_2_
  25.3 0.7 shard_map.69
  25.9 13.2 %all_to_all.25.blocks_ref = f32[32,3,4,128]{3,2,1,0:T(4,128)S(1)} all-to-all(f32[32,3,4,128]{3,2,1,0:T(4,128)S(1)} %get-tuple-element.81), channel_id=1, replica_groups=mesh['gx'=16,'gy'=2] {'gx','gy'}, dimensions={0} | all-to-all | bytes 393216 | tf_op jit(solution)/shard_map/all_to_all | solution.py:479
  39.1 0.8 shard_map.70
  39.9 2.7 %all-to-all-start.2 = ((f32[32,3,4,128]{3,2,1,0:T(4,128)}), f32[32,3,4,128]{3,2,1,0:T(4,128)S(1)}, u32[]{:S(2)}, u32[]{:S(2)}) async-start(f32[32,3,4,128]{3,2,1,0:T(4,128)} %get-tuple-element.82), calls=%async_computation.2 | async-start | bytes 393216 | tf_op jit(solution)/shard_map/all_to_all | solution.py:505
  42.6 0.7 collective-permute-start.6
  43.3 4.5 %collective-permute-start.7 = (f32[128,128]{1,0:T(8,128)S(1)}, f32[128,128]{1,0:T(8,128)S(1)}, u32[]{:S(2)}, u32[]{:S(2)}) collective-permute-start(f32[128,128]{1,0:T(8,128)S(1)} %get-tuple-element.79), channel_id=1, source_target_pairs={{0,2},{4,6},{8,10},{12,14},{16,18},{20,22},{24,26},{28,30},{2,0},{... | collective-permute-start | bytes 196616 | tf_op jit(solution)/shard_map/ppermute | solution.py:102
  47.8 0.0 collective-permute-start.8
  47.8 3.7 %all-to-all-done.2.sums_ref = f32[32,3,4,128]{3,2,1,0:T(4,128)S(1)} async-done(((f32[32,3,4,128]{3,2,1,0:T(4,128)}), f32[32,3,4,128]{3,2,1,0:T(4,128)S(1)}, u32[]{:S(2)}, u32[]{:S(2)}) %all-to-all-start.2) | async-done | bytes 196640 | tf_op jit(solution)/shard_map/all_to_all | solution.py:505
  51.5 1.4 %shard_map.71 = (f32[128,128]{1,0:T(8,128)S(1)}, f32[128,128]{1,0:T(8,128)S(1)}, f32[128,128]{1,0:T(8,128)S(1)}, f32[128,128]{1,0:T(8,128)S(1)}) custom-call(f32[32,3,4,128]{3,2,1,0:T(4,128)S(1)} %all-to-all-done.2.sums_ref), custom_call_target="tpu_custom_call" | custom-call | flops 50331648 | tf_op jit(solution)/shard_map/pallas_call | solution.py:75
  52.8 0.0 collective-permute-done.6.refs_0_
  52.9 0.0 collective-permute-done.7.refs_1_
  52.9 0.0 collective-permute-done.8.refs_2_
  52.9 0.8 shard_map.72
  53.7 0.7 collective-permute-start.9
  54.4 3.7 %collective-permute-start.10 = (f32[128,128]{1,0:T(8,128)S(1)}, f32[128,128]{1,0:T(8,128)S(1)}, u32[]{:S(2)}, u32[]{:S(2)}) collective-permute-start(f32[128,128]{1,0:T(8,128)S(1)} %get-tuple-element.87), channel_id=1, source_target_pairs={{0,2},{4,6},{8,10},{12,14},{16,18},{20,22},{24,26},{28,30},{2,0},{... | collective-permute-start | bytes 196616 | tf_op jit(solution)/shard_map/ppermute | solution.py:102
  58.1 0.0 collective-permute-start.11
  58.1 1.8 %shard_map.73 = (f32[128,128]{1,0:T(8,128)S(1)}, f32[32,128]{1,0:T(8,128)S(1)}, f32[128,128]{1,0:T(8,128)S(1)}, f32[128,128]{1,0:T(8,128)S(1)}, f32[128,128]{1,0:T(8,128)S(1)}) custom-call(f32[32,3,4,128]{3,2,1,0:T(4,128)S(1)} %all-to-all-done.2.sums_ref, f32[32,128]{1,0:T(8,128)S(1)} %get-tuple-element.71.table_ref, ...), custom_call_target="tpu_custom_call" | custom-call | flops 201326592 | tf_op jit(solution)/shard_map/pallas_call | solution.py:75
  59.9 0.0 collective-permute-done.9.refs_0_
  59.9 1.1 %collective-permute-done.10.refs_1_ = f32[128,128]{1,0:T(8,128)S(1)} collective-permute-done((f32[128,128]{1,0:T(8,128)S(1)}, f32[128,128]{1,0:T(8,128)S(1)}, u32[]{:S(2)}, u32[]{:S(2)}) %collective-permute-start.10) | collective-permute-done | bytes 65568 | tf_op jit(solution)/shard_map/ppermute | solution.py:102
  61.1 0.0 collective-permute-done.11.refs_2_
  61.1 0.8 shard_map.74
  61.9 11.7 %all_to_all.26.blocks_ref = f32[32,8,128]{2,1,0:T(8,128)S(1)} all-to-all(f32[32,8,128]{2,1,0:T(8,128)S(1)} %get-tuple-element.99), channel_id=1, replica_groups=mesh['gx'=16,'gy'=2] {'gx','gy'}, dimensions={0} | all-to-all | bytes 262144 | tf_op jit(solution)/shard_map/all_to_all | solution.py:599
  73.7 10.0 %all_to_all.27 = f32[32,8,128]{2,1,0:T(8,128)S(1)} all-to-all(f32[32,8,128]{2,1,0:T(8,128)S(1)} %shard_map.75), channel_id=1, replica_groups=mesh['gx'=16,'gy'=2] {'gx','gy'}, dimensions={0} | all-to-all | bytes 262144 | tf_op jit(solution)/shard_map/all_to_all | solution.py:605
  83.7 17.1 %shard_map.76 = f32[512,128]{1,0:T(8,128)} custom-call(f32[256,128]{1,0:T(8,128)S(1)} %bitcast.9, f32[128,128]{1,0:T(8,128)S(1)} %get-tuple-element.100.inv_ref, f32[128,128]{1,0:T(8,128)S(1)} %get-tuple-element.101.quad_ref, f32[128,128]{1,0:T(8,128)S(1)} %get-tuple-element.102.mend_ref, f32[128,128]{1,0:T(8,128)S(1)} %get-tuple-element.83.refs_3_.step_ref, ...), custom_call_target="tpu_custom_call" | custom-call | tf_op jit(solution)/shard_map/pallas_call | solution.py:75
  (1 shorter events, 0.0 us)
Async XLA Ops:
  1.0 8.9 %collective-permute-start = (f32[136,128]{1,0:T(8,128)S(1)}, f32[136,128]{1,0:T(8,128)S(1)}, u32[]{:S(2)}, u32[]{:S(2)}) collective-permute-start(f32[136,128]{1,0:T(8,128)S(1)} %get-tuple-element.55), channel_id=1, source_target_pairs={{2,4},{6,8},{10,12},{14,16},{18,20},{22,24},{26,28},{4,2},{8,6},{1... | collective-permute-start | bytes 208904 | tf_op jit(solution)/shard_map/ppermute | solution.py:102
  1.7 9.0 %collective-permute-start.1 = (f32[136,128]{1,0:T(8,128)S(1)}, f32[136,128]{1,0:T(8,128)S(1)}, u32[]{:S(2)}, u32[]{:S(2)}) collective-permute-start(f32[136,128]{1,0:T(8,128)S(1)} %get-tuple-element.56), channel_id=1, source_target_pairs={{0,2},{4,6},{8,10},{12,14},{16,18},{20,22},{24,26},{28,30},{2,0},{... | collective-permute-start | bytes 208904 | tf_op jit(solution)/shard_map/ppermute | solution.py:102
  7.4 3.3 %collective-permute-start.2 = (f32[136,128]{1,0:T(8,128)S(1)}, f32[136,128]{1,0:T(8,128)S(1)}, u32[]{:S(2)}, u32[]{:S(2)}) collective-permute-start(f32[136,128]{1,0:T(8,128)S(1)} %get-tuple-element.57), channel_id=1, source_target_pairs={{0,1},{1,0},{2,3},{3,2},{4,5},{5,4},{6,7},{7,6},{8,9},{9,8},{10,11... | collective-permute-start | bytes 208904 | tf_op jit(solution)/shard_map/ppermute | solution.py:102
  11.6 12.3 %all-to-all-start = ((f32[32,4,128]{2,1,0:T(4,128)}), f32[32,4,128]{2,1,0:T(4,128)S(1)}, u32[]{:S(2)}, u32[]{:S(2)}) async-start(f32[32,4,128]{2,1,0:T(4,128)} %get-tuple-element.66), calls=%async_computation | async-start | bytes 131072 | tf_op jit(solution)/shard_map/all_to_all | solution.py:359
  16.5 7.9 %collective-permute-start.3 = (f32[128,128]{1,0:T(8,128)S(1)}, f32[128,128]{1,0:T(8,128)S(1)}, u32[]{:S(2)}, u32[]{:S(2)}) collective-permute-start(f32[128,128]{1,0:T(8,128)S(1)} %get-tuple-element.62), channel_id=1, source_target_pairs={{2,4},{6,8},{10,12},{14,16},{18,20},{22,24},{26,28},{4,2},{8,6},{1... | collective-permute-start | bytes 196616 | tf_op jit(solution)/shard_map/ppermute | solution.py:102
  17.2 8.1 %collective-permute-start.4 = (f32[128,128]{1,0:T(8,128)S(1)}, f32[128,128]{1,0:T(8,128)S(1)}, u32[]{:S(2)}, u32[]{:S(2)}) collective-permute-start(f32[128,128]{1,0:T(8,128)S(1)} %get-tuple-element.63), channel_id=1, source_target_pairs={{0,2},{4,6},{8,10},{12,14},{16,18},{20,22},{24,26},{28,30},{2,0},{... | collective-permute-start | bytes 196616 | tf_op jit(solution)/shard_map/ppermute | solution.py:102
  21.7 3.6 %collective-permute-start.5 = (f32[128,128]{1,0:T(8,128)S(1)}, f32[128,128]{1,0:T(8,128)S(1)}, u32[]{:S(2)}, u32[]{:S(2)}) collective-permute-start(f32[128,128]{1,0:T(8,128)S(1)} %get-tuple-element.64), channel_id=1, source_target_pairs={{0,1},{1,0},{2,3},{3,2},{4,5},{5,4},{6,7},{7,6},{8,9},{9,8},{10,11... | collective-permute-start | bytes 196616 | tf_op jit(solution)/shard_map/ppermute | solution.py:102
  39.9 11.6 %all-to-all-start.2 = ((f32[32,3,4,128]{3,2,1,0:T(4,128)}), f32[32,3,4,128]{3,2,1,0:T(4,128)S(1)}, u32[]{:S(2)}, u32[]{:S(2)}) async-start(f32[32,3,4,128]{3,2,1,0:T(4,128)} %get-tuple-element.82), calls=%async_computation.2 | async-start | bytes 393216 | tf_op jit(solution)/shard_map/all_to_all | solution.py:505
  42.6 10.3 %collective-permute-start.6 = (f32[128,128]{1,0:T(8,128)S(1)}, f32[128,128]{1,0:T(8,128)S(1)}, u32[]{:S(2)}, u32[]{:S(2)}) collective-permute-start(f32[128,128]{1,0:T(8,128)S(1)} %get-tuple-element.78), channel_id=1, source_target_pairs={{2,4},{6,8},{10,12},{14,16},{18,20},{22,24},{26,28},{4,2},{8,6},{1... | collective-permute-start | bytes 196616 | tf_op jit(solution)/shard_map/ppermute | solution.py:102
  43.3 9.6 %collective-permute-start.7 = (f32[128,128]{1,0:T(8,128)S(1)}, f32[128,128]{1,0:T(8,128)S(1)}, u32[]{:S(2)}, u32[]{:S(2)}) collective-permute-start(f32[128,128]{1,0:T(8,128)S(1)} %get-tuple-element.79), channel_id=1, source_target_pairs={{0,2},{4,6},{8,10},{12,14},{16,18},{20,22},{24,26},{28,30},{2,0},{... | collective-permute-start | bytes 196616 | tf_op jit(solution)/shard_map/ppermute | solution.py:102
  47.8 5.1 %collective-permute-start.8 = (f32[128,128]{1,0:T(8,128)S(1)}, f32[128,128]{1,0:T(8,128)S(1)}, u32[]{:S(2)}, u32[]{:S(2)}) collective-permute-start(f32[128,128]{1,0:T(8,128)S(1)} %get-tuple-element.80), channel_id=1, source_target_pairs={{0,1},{1,0},{2,3},{3,2},{4,5},{5,4},{6,7},{7,6},{8,9},{9,8},{10,11... | collective-permute-start | bytes 196616 | tf_op jit(solution)/shard_map/ppermute | solution.py:102
  53.7 6.2 %collective-permute-start.9 = (f32[128,128]{1,0:T(8,128)S(1)}, f32[128,128]{1,0:T(8,128)S(1)}, u32[]{:S(2)}, u32[]{:S(2)}) collective-permute-start(f32[128,128]{1,0:T(8,128)S(1)} %get-tuple-element.86), channel_id=1, source_target_pairs={{2,4},{6,8},{10,12},{14,16},{18,20},{22,24},{26,28},{4,2},{8,6},{1... | collective-permute-start | bytes 196616 | tf_op jit(solution)/shard_map/ppermute | solution.py:102
  54.4 6.7 %collective-permute-start.10 = (f32[128,128]{1,0:T(8,128)S(1)}, f32[128,128]{1,0:T(8,128)S(1)}, u32[]{:S(2)}, u32[]{:S(2)}) collective-permute-start(f32[128,128]{1,0:T(8,128)S(1)} %get-tuple-element.87), channel_id=1, source_target_pairs={{0,2},{4,6},{8,10},{12,14},{16,18},{20,22},{24,26},{28,30},{2,0},{... | collective-permute-start | bytes 196616 | tf_op jit(solution)/shard_map/ppermute | solution.py:102
  58.1 3.0 %collective-permute-start.11 = (f32[128,128]{1,0:T(8,128)S(1)}, f32[128,128]{1,0:T(8,128)S(1)}, u32[]{:S(2)}, u32[]{:S(2)}) collective-permute-start(f32[128,128]{1,0:T(8,128)S(1)} %get-tuple-element.88), channel_id=1, source_target_pairs={{0,1},{1,0},{2,3},{3,2},{4,5},{5,4},{6,7},{7,6},{8,9},{9,8},{10,11... | collective-permute-start | bytes 196616 | tf_op jit(solution)/shard_map/ppermute | solution.py:102
